TPU v7x, 32 devices: a whole 2x2x4 slice. The times are simulated.
32 devices in a mesh: dp: 16 (over z, y, core), seq: 2 (over x).
Axes of the slice: x: 2, y: 2, z: 4, core: 2. Of those that a mesh axis runs over, the one named last changes fastest.
Arguments:
- tokens_short: bfloat16 [16, 128, 768], P('dp', 'seq'), may hold values from -6 to 6
- tokens_middle: bfloat16 [16, 256, 768], P('dp', 'seq'), may hold values from -6 to 6
- tokens_long: bfloat16 [64, 512, 768], P('dp', 'seq'), may hold values from -6 to 6
- length_short: int32 [16], P('dp'), may hold values from 16 to 128, as said below
- length_middle: int32 [16], P('dp'), may hold values from 32 to 256, as said below
- length_long: int32 [64], P('dp'), may hold values from 64 to 512, as said below
- query_weight: bfloat16 [768, 768], replicated, may hold values from -0.21875 to 0.21875
- query_bias: float32 [768], replicated, may hold values from -3 to 3
- key_weight: bfloat16 [768, 768], replicated, may hold values from -0.21875 to 0.21875
- value_weight: bfloat16 [768, 768], replicated, may hold values from -0.21875 to 0.21875
- value_bias: float32 [768], replicated, may hold values from -3 to 3
- output_weight: bfloat16 [768, 768], replicated, may hold values from -0.875 to 0.875
- output_bias: float32 [768], replicated, may hold values from -3 to 3
- attention_gain: float32 [768], replicated, may hold values from 0.1 to 1.9
- attention_shift: float32 [768], replicated, may hold values from -3 to 3
- up_weight: bfloat16 [768, 3072], replicated, may hold values from -0.21875 to 0.21875
- up_bias: float32 [3072], replicated, may hold values from -3 to 3
- down_weight: bfloat16 [3072, 768], replicated, may hold values from -0.109375 to 0.109375
- down_bias: float32 [768], replicated, may hold values from -3 to 3
- output_gain: float32 [768], replicated, may hold values from 0.1 to 1.9
- output_shift: float32 [768], replicated, may hold values from -3 to 3
- upstream_short: bfloat16 [16, 128, 768], P('dp', 'seq'), may hold values from -6 to 6
- upstream_middle: bfloat16 [16, 256, 768], P('dp', 'seq'), may hold values from -6 to 6
- upstream_long: bfloat16 [64, 512, 768], P('dp', 'seq'), may hold values from -6 to 6
Outputs:
- result_short: bfloat16 [16, 128, 768], P('dp', 'seq')
- result_middle: bfloat16 [16, 256, 768], P('dp', 'seq')
- result_long: bfloat16 [64, 512, 768], P('dp', 'seq')
- input_grad_short: bfloat16 [16, 128, 768], P('dp', 'seq')
- input_grad_middle: bfloat16 [16, 256, 768], P('dp', 'seq')
- input_grad_long: bfloat16 [64, 512, 768], P('dp', 'seq')
- query_weight_grad: float32 [768, 768], P(('dp', 'seq'))
- query_bias_grad: float32 [768], P(('dp', 'seq'))
- key_weight_grad: float32 [768, 768], P(('dp', 'seq'))
- value_weight_grad: float32 [768, 768], P(('dp', 'seq'))
- value_bias_grad: float32 [768], P(('dp', 'seq'))
- output_weight_grad: float32 [768, 768], P(('dp', 'seq'))
- output_bias_grad: float32 [768], P(('dp', 'seq'))
- attention_gain_grad: float32 [768], P(('dp', 'seq'))
- attention_shift_grad: float32 [768], P(('dp', 'seq'))
- up_weight_grad: float32 [768, 3072], P(('dp', 'seq'))
- up_bias_grad: float32 [3072], P(('dp', 'seq'))
- down_weight_grad: float32 [3072, 768], P(('dp', 'seq'))
- down_bias_grad: float32 [768], P(('dp', 'seq'))
- output_gain_grad: float32 [768], P(('dp', 'seq'))
- output_shift_grad: float32 [768], P(('dp', 'seq'))
Inputs may be any that keep to these rules, and one draw needn't show every extreme that they name: `length_short`: in each aligned block of 8 rows, one row drawn from the seed has length 128; the others are at least one eighth of it. `length_middle`: in each aligned block of 8 rows, one row drawn from the seed has length 256; the others are at least one eighth of it. `length_long`: in each aligned block of 32 rows, one row drawn from the seed has length 512; the others are at least one eighth of it.
All inputs are finite; a program needn't handle non-finite values.
Results may differ from a plain program's by a relative error of at most 0.014.
Values may be sent and summed in bfloat16 or wider, within the bound.
No kernel may reach another device: no remote copies, remote signals or barrier semaphores. Data moves between devices by JAX's collectives and lax.ppermute only.
A program may use at most 256 MiB of HBM per device.

v0:
```python
import functools

import jax
import jax.numpy as jnp
from jax import lax
from jax.experimental import pallas as pl
from jax.experimental.pallas import tpu as pltpu
from jax.sharding import PartitionSpec as P

D = 768
FF = 3072
HEADS = 12
PAIRS = HEADS // 2
EPS = 1e-12
NEG = -1e30
SHORT_HALF = 64
BLOCKS = 32
VMEM_LIMIT = 60 * 2**20

bf16 = jnp.bfloat16
f32 = jnp.float32
SDS = jax.ShapeDtypeStruct
ANY = pl.BlockSpec(memory_space=pl.ANY)
HINT = pl.CostEstimate(flops=1024, bytes_accessed=1024, transcendentals=0)


def dot(a, b):
    return lax.dot_general(a, b, (((1,), (0,)), ((), ())), preferred_element_type=f32)


def dot_nt(a, b):
    return lax.dot_general(a, b, (((1,), (1,)), ((), ())), preferred_element_type=f32)


def dot_tn(a, b):
    return lax.dot_general(a, b, (((0,), (0,)), ((), ())), preferred_element_type=f32)


def wide(vector):
    return vector[...].reshape(1, -1)


def mean(v):
    return jnp.mean(v, axis=-1, keepdims=True)


def column_sum(v):
    return jnp.sum(v.astype(f32), axis=0, keepdims=True)


A1, A2, A3, A4, A5 = 0.254829592, -0.284496736, 1.421413741, -1.453152027, 1.061405429
P_SCALED = 0.3275911 * 0.7071067811865476
INV_SQRT_2PI = 0.3989422804014327


def gelu_and_slope(v):
    t = 1.0 / (1.0 + P_SCALED * jnp.abs(v))
    e = jnp.exp(v * v * -0.5)
    tail = t * (A1 + t * (A2 + t * (A3 + t * (A4 + t * A5)))) * (0.5 * e)
    cdf = jnp.where(v < 0, tail, 1.0 - tail)
    return v * cdf, cdf + v * (e * INV_SQRT_2PI)


def mask_column(place, row, length):
    seq, short, middle, long = place
    half = length // 2
    mine = long.shape[0] // 2
    s = seq[0]
    if row < mine:
        count, valid, own, other = long[mine * s + row], half, half * s, half * (1 - s)
    else:
        is_first = s == 0
        count = jnp.where(is_first, middle[0], short[0])
        valid = jnp.where(is_first, half, SHORT_HALF)
        own, other = jnp.where(is_first, 0, SHORT_HALF), jnp.where(is_first, half, 0)
    i = lax.broadcasted_iota(jnp.int32, (length, 1), 0)
    inner = jnp.where(i < half, i, i - half)
    live = (inner + jnp.where(i < half, own, other) < count) & (inner < valid)
    return jnp.where(live, 0.0, NEG).astype(f32)


def low_lanes():
    return lax.broadcasted_iota(jnp.int32, (1, 128), 1) < 64


def stack_heads(pair, low):
    zero = jnp.zeros_like(pair)
    return jnp.concatenate([jnp.where(low, pair, zero), jnp.where(low, zero, pair)], axis=0)


def split_rows(pair_t):
    row = lax.broadcasted_iota(jnp.int32, (128, 1), 0) < 64
    zero = jnp.zeros_like(pair_t)
    return jnp.where(row, pair_t, zero), jnp.where(row, zero, pair_t)


def scaled(q):
    return (q.astype(f32) * 0.125).astype(bf16)


def emit_24(scr, lane, d, out, r, base):
    for g in range(3):
        rows = pl.ds(pl.multiple_of(24 * d + 8 * g, 8), 8)
        both = jnp.concatenate(
            [scr[rows, lane : lane + 384], scr[rows, lane + 384 : lane + 768]], axis=0
        )
        out[r, :, base + 384 * g : base + 384 * (g + 1)] = both.astype(bf16)


def block_number(half, r):
    return ((r >> 1) << 2) | (half << 1) | (r & 1)


def forward_kernel(s0, s1, s2, s3, xl, xr, wq, wk, wv, bq, bv, *rest, length, row, chained):
    x_o, q_o, k_o, v_o, c_o, lse_o, xt_o = rest[7:] if chained else rest
    x = jnp.concatenate([xl[...], xr[...]], axis=0)
    x_o[...] = x
    xt_o[...] = x.T
    q_o[...] = (dot(x, wq[...]) + wide(bq)).astype(bf16)
    k_o[...] = dot(x, wk[...]).astype(bf16)
    v_o[...] = (dot(x, wv[...]) + wide(bv)).astype(bf16)
    bias = mask_column((s0, s1, s2, s3), row, length)
    low = low_lanes()
    row_low = lax.broadcasted_iota(jnp.int32, (128, 1), 0) < 64
    for p in range(PAIRS):
        sl = slice(128 * p, 128 * p + 128)
        scores = dot_nt(stack_heads(k_o[:, sl], low), scaled(q_o[:, sl]))
        parts = []
        inverse = []
        for h in range(2):
            s = scores[h * length : (h + 1) * length, :] + bias
            top = jnp.max(s, axis=0, keepdims=True)
            raised = jnp.exp(s - top)
            total = jnp.sum(raised, axis=0, keepdims=True)
            lse_o[2 * p + h : 2 * p + h + 1, 0:length] = top + jnp.log(total)
            parts.append(raised.astype(bf16))
            inverse.append(1.0 / total)
        upper, lower = split_rows(v_o[:, sl].T)
        context = dot(upper, parts[0]) + dot(lower, parts[1])
        context = context * jnp.where(row_low, inverse[0], inverse[1])
        c_o[:, sl] = context.T.astype(bf16)


def attention_forward(place, own, other, weights, row, length, block, chain, rows):
    half = pl.BlockSpec((length // 2, D), lambda i: (0, 0))
    full = lambda a: pl.BlockSpec(a.shape, lambda i: (0,) * a.ndim)
    tok = pl.BlockSpec((length, D), lambda i: (block, 0))
    lse = pl.BlockSpec((16, 512), lambda i: (row, 0))
    turned = pl.BlockSpec((D, length), lambda i: (0, block))
    chained = chain is not None
    extra = list(chain) if chained else []
    return pl.pallas_call(
        functools.partial(forward_kernel, length=length, row=row, chained=chained),
        grid=(1,),
        in_specs=[pl.BlockSpec(memory_space=pltpu.SMEM)] * 4
        + [half, half]
        + [full(w) for w in weights]
        + [ANY] * len(extra),
        out_specs=[tok] * 5 + [lse, turned],
        out_shape=[SDS((rows, D), bf16)] * 5 + [SDS((48, 512), f32), SDS((D, rows), bf16)],
        input_output_aliases={11 + i: i for i in range(7)} if chained else {},
        compiler_params=pltpu.CompilerParams(vmem_limit_bytes=VMEM_LIMIT),
        cost_estimate=HINT,
        name=f"attend_{row}",
    )(*place, own, other, *weights, *extra)


def drop_first(kernel):
    return lambda _, *refs, **options: kernel(*refs, **options)


def dense_kernel(*refs, chunks, own):
    ctx, x = refs[0], refs[1]
    step = pl.program_id(0)
    last = step == pl.num_programs(0) - 1
    if own:
        up_refs, refs = refs[2:3], refs[3:]
        up = up_refs[0][0]
    else:
        up_refs, refs = refs[2:5], refs[5:]
        up = jnp.concatenate([jnp.where(last, up_refs[2][...], up_refs[0][...]), up_refs[1][...]], axis=0)
    wo, wup, wdn, bup, bo, g1, s1, bdn, g2, s2 = refs[:10]
    bup, bo, g1, s1, bdn, g2, s2 = (wide(v) for v in (bup, bo, g1, s1, bdn, g2, s2))
    if own:
        res_own, act, dinn, nlow_o, dbr, datt, dr1_o, dctx, vec, slope_s = refs[10:]
    else:
        vec_in = refs[10]
        res_other, res_mid, act, dinn, nlow_o, dbr, datt, dr1_o, dctx, vec, slope_s = refs[18:]

    @pl.when(step == 0)
    def _():
        vec[...] = jnp.zeros_like(vec) if own else vec_in[...]

    r1 = x[...].astype(f32) + dot(ctx[...], wo[...]) + bo
    c1 = r1 - mean(r1)
    rs1 = lax.rsqrt(mean(c1 * c1) + EPS)
    n1 = c1 * rs1
    normed = n1 * g1 + s1
    nlow = normed.astype(bf16)
    nlow_o[...] = nlow
    acc = normed + bdn
    width = FF // chunks
    for j in range(chunks):
        sl = slice(j * width, (j + 1) * width)
        value, slope = gelu_and_slope(dot(nlow, wup[:, sl]) + bup[:, sl])
        value = value.astype(bf16)
        act[:, sl] = value
        slope_s[:, sl] = slope
        acc = acc + dot(value, wdn[sl, :])
    c2 = acc - mean(acc)
    rs2 = lax.rsqrt(mean(c2 * c2) + EPS)
    n2 = c2 * rs2
    result = (n2 * g2 + s2).astype(bf16)
    if own:
        res_own[...] = result
    else:
        size = result.shape[0]

        @pl.when(jnp.logical_not(last))
        def _():
            res_other[pl.ds(pl.multiple_of(step * size, size), size), :] = result

        @pl.when(last)
        def _():
            res_mid[...] = result[: size // 2]
            res_other[res_other.shape[0] - size // 2 :, :] = result[size // 2 :]

    upstream = up.astype(f32)
    u = upstream * g2
    dr2 = (u - mean(u) - n2 * mean(u * n2)) * rs2
    branch = dr2.astype(bf16)
    dbr[...] = branch
    vec[0:1, :] += column_sum(upstream * n2)
    vec[1:2, :] += column_sum(upstream)
    vec[2:3, :] += column_sum(branch)
    acc = dr2
    for j in range(chunks):
        sl = slice(j * width, (j + 1) * width)
        d_inner = (dot_nt(branch, wdn[sl, :]) * slope_s[:, sl]).astype(bf16)
        dinn[:, sl] = d_inner
        vec[8 + j : 9 + j, :] += column_sum(d_inner)
        acc = acc + dot_nt(d_inner, wup[:, sl])
    vec[3:4, :] += column_sum(acc * n1)
    vec[4:5, :] += column_sum(acc)
    u1 = acc * g1
    d1 = (u1 - mean(u1) - n1 * mean(u1 * n1)) * rs1
    d_attn = d1.astype(bf16)
    datt[...] = d_attn
    dr1_o[...] = d1
    vec[5:6, :] += column_sum(d_attn)
    dctx[...] = dot_nt(d_attn, wo[...]).astype(bf16)


def dense_steps(seq, ctx, x, ups, mats, vecs, tokens, rows, before):
    tile = 256
    half = tile // 2
    mine = tokens // tile // 2
    own = before is None
    full = lambda a: pl.BlockSpec(a.shape, lambda i, s: (0,) * a.ndim, pipeline_mode=pl.Buffered(1))
    whole = lambda n: pl.BlockSpec((n, D), lambda i, s: (0, 0))
    if own:
        place = lambda i: 2 * i
        steps = mine
        up_specs = [pl.BlockSpec((1, tile, D), lambda i, s: (s[0] * mine + i, 0, 0))]
        res_specs = [pl.BlockSpec((tile, D), lambda i, s: (i, 0))]
        res_shapes = [SDS((mine * tile, D), bf16)]
        extra, extra_specs, aliases = [], [], {}
    else:
        place = lambda i: jnp.minimum(2 * i + 1, 2 * mine)
        steps = mine + 1
        up_specs = [
            pl.BlockSpec((half, D), lambda i, s: (jnp.minimum(2 * i, 2 * mine - 2), 0)),
            pl.BlockSpec((half, D), lambda i, s: (jnp.minimum(2 * i + 1, 2 * mine), 0)),
            whole(half),
        ]
        res_specs = [whole(tokens // 2), whole(half)]
        res_shapes = [SDS((tokens // 2, D), bf16), SDS((half, D), bf16)]
        *arrays, vec = before
        extra = [vec] + arrays
        extra_specs = [whole(16)] + [ANY] * len(arrays)
        first = 1 + 2 + len(ups) + len(mats) + len(vecs) + 1
        aliases = {first + i: 2 + i for i in range(len(arrays))}
    tok = pl.BlockSpec((tile, D), lambda i, s: (place(i), 0))
    ffs = pl.BlockSpec((tile, FF), lambda i, s: (place(i), 0))
    return pl.pallas_call(
        functools.partial(drop_first(dense_kernel), chunks=4, own=own),
        grid_spec=pltpu.PrefetchScalarGridSpec(
            num_scalar_prefetch=1,
            grid=(steps,),
            in_specs=[tok, tok] + up_specs + [full(a) for a in mats + vecs] + extra_specs,
            out_specs=res_specs + [ffs, ffs] + [tok] * 5 + [whole(16)],
            scratch_shapes=[pltpu.VMEM((tile, FF), f32)],
        ),
        out_shape=res_shapes
        + [SDS((tokens, FF), bf16)] * 2
        + [SDS((tokens, D), bf16)] * 3
        + [SDS((rows, D), f32), SDS((rows, D), bf16), SDS((16, D), f32)],
        input_output_aliases=aliases,
        compiler_params=pltpu.CompilerParams(vmem_limit_bytes=VMEM_LIMIT),
        cost_estimate=HINT,
        name="dense_own" if own else "dense_rest",
    )(seq, ctx, x, *ups, *mats, *vecs, *extra)


def up_grad_kernel(me, nlow, left, right, send, keep, turned, scr):

    @pl.when(pl.program_id(0) == 0)
    def _():
        turned[...] = nlow[...].T

    scr[:, 0:384] = dot(turned[...], left[...])
    scr[:, 384:768] = dot(turned[...], right[...])
    for half, out in ((0, keep), (1, send)):
        for r in range(16):
            emit_24(scr, 0, block_number(half, r) ^ me[0], out, r, 0)


def up_grad(me, nlow, dinn, tokens):
    out = pl.BlockSpec((16, 16, 1152), lambda j, m: (0, 0, j))
    return pl.pallas_call(
        up_grad_kernel,
        grid_spec=pltpu.PrefetchScalarGridSpec(
            num_scalar_prefetch=1,
            grid=(4,),
            in_specs=[
                pl.BlockSpec((tokens, D), lambda j, m: (0, 0)),
                pl.BlockSpec((tokens, 384), lambda j, m: (0, j)),
                pl.BlockSpec((tokens, 384), lambda j, m: (0, j + 4)),
            ],
            out_specs=[out, out],
            scratch_shapes=[pltpu.VMEM((D, tokens), bf16), pltpu.VMEM((D, D), f32)],
        ),
        out_shape=[SDS((16, 16, 4608), bf16)] * 2,
        compiler_params=pltpu.CompilerParams(vmem_limit_bytes=VMEM_LIMIT),
        cost_estimate=HINT,
        name="up_grad",
    )(me, nlow, dinn, dinn)


DOWN_WIDTH = 4608 + 1152 + 128


def down_grad_kernel(me, act, dbr, ctx, datt, vec, send, keep, scr, wo_s):
    j = pl.program_id(0)

    @pl.when(j == 0)
    def _():
        wo_s[...] = dot_tn(ctx[...], datt[...])

    scr[...] = dot_tn(act[...], dbr[...])
    z = j ^ (me[0] >> 3)
    for half, out in ((0, keep), (1, send)):
        for r in range(4):
            near = block_number(half, r) ^ (me[0] & 7)
            d = z * 8 + near
            for g in range(6):
                rows = pl.ds(pl.multiple_of(96 * near + 16 * g, 16), 16)
                out[r, :, D * g : D * (g + 1)] = scr[rows, :].astype(bf16)
            emit_24(wo_s, 0, d, out, r, 4608)
            small = pltpu.roll(vec[0:8, :], lax.rem(D - 24 * d, D), 1)[:, 0:128]
            wide = pltpu.roll(vec[8:16, :], lax.rem(D - 96 * near, D), 1)[:, 0:128]
            out[r, :, 5760:5888] = jnp.concatenate([small, wide], axis=0).astype(bf16)


def down_grad(me, act, dbr, ctx, datt, vec, tokens):
    out = pl.BlockSpec((4, 16, DOWN_WIDTH), lambda j, m: (j, 0, 0))
    tok = pl.BlockSpec((tokens, D), lambda j, m: (0, 0))
    return pl.pallas_call(
        down_grad_kernel,
        grid_spec=pltpu.PrefetchScalarGridSpec(
            num_scalar_prefetch=1,
            grid=(4,),
            in_specs=[
                pl.BlockSpec((tokens, D), lambda j, m: (0, j ^ (m[0] >> 3))),
                tok,
                tok,
                tok,
                pl.BlockSpec((16, D), lambda j, m: (0, 0)),
            ],
            out_specs=[out, out],
            scratch_shapes=[pltpu.VMEM((D, D), f32), pltpu.VMEM((D, D), f32)],
        ),
        out_shape=[SDS((16, 16, DOWN_WIDTH), bf16)] * 2,
        compiler_params=pltpu.CompilerParams(vmem_limit_bytes=VMEM_LIMIT),
        cost_estimate=HINT,
        name="down_grad",
    )(me, act, dbr, ctx, datt, vec)


def backward_pairs(pairs, place, row, length, q_r, k_r, v_r, g_r, lse, first, dq_o, dk_o, dv_o):
    n = slice(0, length)
    bias = mask_column(place, row, length)
    low = low_lanes()
    for p in range(pairs):
        sl = slice(128 * p, 128 * p + 128)
        q2 = scaled(q_r[n, sl])
        k2 = k_r[n, sl]
        g2 = g_r[n, sl]
        scores = dot_nt(stack_heads(k2, low), q2)
        d_probs = dot_nt(stack_heads(v_r[n, sl], low), g2)
        probs_low = []
        d_scores = []
        for h in range(2):
            part = slice(h * length, (h + 1) * length)
            head = 2 * (first + p) + h
            probs = jnp.exp(scores[part, :] + bias - lse[head : head + 1, n])
            d_part = d_probs[part, :]
            centre = jnp.sum(probs * d_part, axis=0, keepdims=True)
            probs_low.append(probs.astype(bf16))
            d_scores.append((probs * (d_part - centre)).astype(bf16))
        dv_o[n, sl] = jnp.where(low, dot(probs_low[0], g2), dot(probs_low[1], g2)).astype(bf16)
        dk_o[n, sl] = jnp.where(low, dot(d_scores[0], q2), dot(d_scores[1], q2)).astype(bf16)
        upper, lower = split_rows(k2.T)
        turned = dot(upper, d_scores[0]) + dot(lower, d_scores[1])
        dq_o[n, sl] = (turned * 0.125).T.astype(bf16)


def first_row_kernel(s0, s1, s2, s3, q_r, k_r, v_r, g_r, lse, dr1, wq, wk, wv, dq, dk, dv, ig_own, ig_other, *, length):
    backward_pairs(PAIRS, (s0, s1, s2, s3), 0, length, q_r, k_r, v_r, g_r, lse, 0, dq, dk, dv)
    ig = dr1[...] + dot_nt(dq[...], wq[...]) + dot_nt(dk[...], wk[...]) + dot_nt(dv[...], wv[...])
    ig = ig.astype(bf16)
    ig_own[...] = ig[: length // 2]
    ig_other[...] = ig[length // 2 :]


def first_row_backward(place, q, k, v, dctx, lse, dr1, weights, length):
    tok = pl.BlockSpec((length, D), lambda i: (0, 0))
    half = pl.BlockSpec((length // 2, D), lambda i: (0, 0))
    full = pl.BlockSpec((D, D), lambda i: (0, 0))
    return pl.pallas_call(
        functools.partial(first_row_kernel, length=length),
        grid=(1,),
        in_specs=[pl.BlockSpec(memory_space=pltpu.SMEM)] * 4
        + [tok] * 4
        + [pl.BlockSpec((16, 512), lambda i: (0, 0)), tok]
        + [full] * 3,
        out_specs=[tok] * 3 + [half] * 2,
        out_shape=[SDS((length, D), bf16)] * 3 + [SDS((length // 2, D), bf16)] * 2,
        compiler_params=pltpu.CompilerParams(vmem_limit_bytes=VMEM_LIMIT),
        cost_estimate=HINT,
        name="back_first",
    )(*place, q, k, v, dctx, lse, dr1, *weights)


def group_kernel(me, s0, s1, s2, s3, q_r, k_r, v_r, g_r, lse, dq0, dk0, dv0, xt, *rest, lengths, pairs, first, final):
    if final:
        bg_before, rest = rest[0], rest[1:]
    dq, dk, dv, send, keep, bg, every, dw = rest
    width = 128 * pairs
    long, mid = lengths
    step = pl.program_id(0)

    @pl.when(step == 0)
    def _():
        backward_pairs(pairs, (s0, s1, s2, s3), 1, long, q_r, k_r, v_r, g_r, lse, first, dq, dk, dv)
        for a, (old, new) in enumerate(((dq0, dq), (dk0, dk), (dv0, dv))):
            lanes = slice(a * width, (a + 1) * width)
            every[0:long, lanes] = old[...]
            every[long : 2 * long, lanes] = new[...]

    @pl.when(step == 1)
    def _():
        backward_pairs(pairs, (s0, s1, s2, s3), 2, mid, q_r, k_r, v_r, g_r, lse, first, dq, dk, dv)
        for a, new in enumerate((dq, dk, dv)):
            every[2 * long : 2 * long + mid, a * width : (a + 1) * width] = new[0:mid, :]
        count = 2 * long + mid
        for c in range(3 * width // D):
            dw[:, D * c : D * (c + 1)] = dot(xt[:, 0:count], every[:, D * c : D * (c + 1)])
        bg[...] = jnp.zeros_like(bg)
        bg[0:1, :] = column_sum(every[:, 0:width])
        bg[1:2, :] = column_sum(every[:, 2 * width : 3 * width])
        if final:
            sums = jnp.concatenate([bg_before[...], bg[...]], axis=1)
        for half, out in ((0, keep), (1, send)):
            for r in range(16):
                d = block_number(half, r) ^ me[0]
                for c in range(3 * width // D):
                    emit_24(dw, D * c, d, out, r, 1152 * c)
                if final:
                    small = pltpu.roll(sums, lax.rem(D - 24 * d, D), 1)[:, 0:128]
                    small = jnp.concatenate([small, small], axis=0)
                    out[r, :, 1152 * (3 * width // D) :] = small.astype(bf16)


def group_backward(me, place, q, k, v, dctx, lse, before, xt, lengths, pairs, first, bg_before):
    final = bg_before is not None
    width = 128 * pairs
    column = first // pairs
    long, mid = lengths
    count = 2 * long + mid
    tok = pl.BlockSpec((long, width), lambda i, *_: (1 + i, column))
    old = pl.BlockSpec((long, width), lambda i, *_: (0, column))
    new = pl.BlockSpec((long, width), lambda i, *_: (i, 0))
    size = 3 * width * 24 // 16 + (128 if final else 0)
    out = pl.BlockSpec((16, 16, size), lambda i, *_: (0, 0, 0))
    extra = [bg_before] if final else []
    specs = [pl.BlockSpec(a.shape, lambda i, *_: (0, 0)) for a in extra]
    return pl.pallas_call(
        functools.partial(group_kernel, lengths=lengths, pairs=pairs, first=first, final=final),
        grid_spec=pltpu.PrefetchScalarGridSpec(
            num_scalar_prefetch=5,
            grid=(2,),
            in_specs=[tok] * 4
            + [pl.BlockSpec((16, 512), lambda i, *_: (1 + i, 0))]
            + [old] * 3
            + [pl.BlockSpec(xt.shape, lambda i, *_: (0, 0))]
            + specs,
            out_specs=[new] * 3 + [out, out, pl.BlockSpec((8, width), lambda i, *_: (0, 0))],
            scratch_shapes=[pltpu.VMEM((count, 3 * width), bf16), pltpu.VMEM((D, 3 * width), f32)],
        ),
        out_shape=[SDS((2 * long, width), bf16)] * 3
        + [SDS((16, 16, size), bf16)] * 2
        + [SDS((8, width), f32)],
        compiler_params=pltpu.CompilerParams(vmem_limit_bytes=VMEM_LIMIT),
        cost_estimate=HINT,
        name=f"back_group_{first}",
    )(me, *place, q, k, v, dctx, lse, *before, xt, *extra)


def input_grad_kernel(dr1, *rest, lengths, lanes):
    groups = len(lanes)
    blocks, (wq, wk, wv), (own, other) = rest[: 3 * groups], rest[3 * groups : 3 * groups + 3], rest[-2:]
    long, mid = lengths
    n = slice(0, long + mid)
    total = dr1[...]
    for a, w in enumerate((wq, wk, wv)):
        for g, (low, high) in enumerate(lanes):
            total = total + dot_nt(blocks[3 * g + a][n, :], w[:, low:high])
    total = total.astype(bf16)
    own[0 : long // 2, :] = total[0 : long // 2]
    other[0 : long // 2, :] = total[long // 2 : long]
    own[long // 2 :, :] = total[long : long + mid // 2]
    other[long // 2 :, :] = total[long + mid // 2 :]


def input_grad(dr1, groups, lanes, weights, lengths):
    long, mid = lengths
    flat = [a for g in groups for a in g]
    whole = lambda a: pl.BlockSpec(a.shape, lambda i: (0, 0))
    side = pl.BlockSpec(((long + mid) // 2, D), lambda i: (0, 0))
    return pl.pallas_call(
        functools.partial(input_grad_kernel, lengths=lengths, lanes=lanes),
        grid=(1,),
        in_specs=[pl.BlockSpec((pl.Element(long + mid), pl.Element(D)), lambda i: (long, 0))]
        + [whole(a) for a in flat + list(weights)],
        out_specs=[side, side],
        out_shape=[SDS(((long + mid) // 2, D), bf16)] * 2,
        compiler_params=pltpu.CompilerParams(vmem_limit_bytes=VMEM_LIMIT),
        cost_estimate=HINT,
        name="input_grad",
    )(dr1, *flat, *weights)


def swap_seq(v):
    return lax.ppermute(v, "seq", [(0, 1), (1, 0)])


def swap_dp(v, bit):
    n = lax.axis_size("dp")
    return lax.ppermute(v, "dp", [(i, i ^ bit) for i in range(n)])


STEPS = {"x": (3, swap_seq), "y": (2, lambda v: swap_dp(v, 2)), "z": (1, lambda v: swap_dp(v, 4)), "w": (0, lambda v: swap_dp(v, 8))}


def later(value, *others):
    return lax.optimization_barrier((value, *others))[0]


class Halving:
    def __init__(self, groups, order):
        self.groups = groups
        self.order = order

    def total(self, groups):
        sums = [functools.reduce(lambda a, b: a + b, [p.astype(f32) for p in g]) for g in groups]
        return jnp.concatenate(sums, axis=5)

    def send(self):
        axis, self.swap = STEPS[self.order[0]]
        self.order = self.order[1:]
        half = lambda i: [[lax.index_in_dim(p, i, axis, keepdims=True) for p in g] for g in self.groups]
        self.outgoing = self.total(half(1)).astype(bf16)
        self.groups = half(0)
        return self

    def receive(self, after=None):
        received = self.swap(self.outgoing)
        if after is not None:
            received = later(received, after)
        low = 0
        for g in self.groups:
            width = g[0].shape[5]
            g.append(lax.slice_in_dim(received, low, low + width, axis=5))
            low += width
        return self

    def result(self):
        return self.total(self.groups).reshape(16, -1)


def join(*sums):
    return Halving([g for h in sums for g in h.groups], sums[0].order)


def across_cores(pair, after, widths, orders):
    send, keep = pair
    received = swap_dp(send, 1)
    if after is not None:
        received = later(received, after)
    both = [v.reshape(2, 2, 2, 2, 16, -1) for v in (keep, received)]
    parts = []
    low = 0
    for width, order in zip(widths, orders):
        parts.append(Halving([[lax.slice_in_dim(v, low, low + width, axis=5) for v in both]], order).send())
        low += width
    return parts


def rows_24(block):
    return block.reshape(2, 8, 3, 384).transpose(2, 1, 0, 3).reshape(24, D)


def unpack_up(block):
    return block.reshape(2, 8, 4, 3, 384).transpose(3, 1, 0, 2, 4).reshape(24, FF)


def unpack_down(block):
    return block[:, :4608].reshape(16, 6, D).transpose(1, 0, 2).reshape(96, D), rows_24(block[:, 4608:5760])


def unpack_qkv(blocks):
    wide, narrow = blocks
    left = jnp.concatenate([rows_24(wide[:, :1152]), rows_24(wide[:, 1152:])], axis=1)
    right = rows_24(narrow[:, :1152])
    return [
        jnp.concatenate([left[:, 512 * a : 512 * (a + 1)], right[:, 256 * a : 256 * (a + 1)]], axis=1) for a in range(3)
    ]


def finish_sums(up, down, qkv, me):
    w_up = unpack_up(up)
    w_down, w_out = unpack_down(down)
    w_query, w_key, w_value = unpack_qkv(qkv)
    vec = down[:8, 5760:5784]
    b_up = lax.dynamic_slice(down, (8 + (me >> 3), 5760), (1, 96))[0]
    bq, bv = qkv[1][0, 1152:1176], qkv[1][1, 1152:1176]
    return w_query, bq, w_key, w_value, bv, w_out, vec, w_up, b_up, w_down


def reduce_plain(up_pair, down_pair, qkv_pairs, vec, bg):
    def ordered(pair):
        send, keep = pair
        both = jnp.stack([keep.reshape(8, 2, 16, -1), send.reshape(8, 2, 16, -1)], axis=1)
        return both.reshape(BLOCKS, 16, -1).astype(f32)

    scatter = lambda v: lax.psum_scatter(v, ("dp", "seq"), scatter_dimension=0, tiled=True)
    w_up = jax.vmap(unpack_up)(ordered(up_pair)).reshape(D, FF)
    w_down, w_out = (a.reshape(-1, D) for a in jax.vmap(unpack_down)(ordered(down_pair)))
    qkv = [a.reshape(D, D) for a in jax.vmap(unpack_qkv)([ordered(p) for p in qkv_pairs])]
    small = [scatter(vec[i]) for i in range(6)]
    return (
        scatter(qkv[0]), scatter(bg[0]), scatter(qkv[1]), scatter(qkv[2]), scatter(bg[1]), scatter(w_out),
        small, scatter(w_up), scatter(vec[8:12].reshape(FF)), scatter(w_down),
    )


def per_device(
    tokens_short, tokens_middle, tokens_long, length_short, length_middle, length_long,
    query_weight, query_bias, key_weight, value_weight, value_bias, output_weight, output_bias,
    attention_gain, attention_shift, up_weight, up_bias, down_weight, down_bias, output_gain, output_shift,
    upstream_short, upstream_middle, upstream_long,
):
    seq = lax.axis_index("seq")
    first = seq == 0
    device = (lax.axis_index("dp") * 2 + seq).astype(jnp.int32)
    fast = lax.axis_size("dp") * lax.axis_size("seq") == BLOCKS
    me = device if fast else jnp.int32(0)
    me_ref = me.reshape(1)
    count, half, _ = tokens_long.shape
    mine = count // 2
    mid = tokens_middle.shape[1]
    short = tokens_short.shape[1]
    lengths = (2 * half,) * mine + (2 * mid,)
    tokens = sum(lengths)
    rows = 2 * half * (mine + 1)

    def own_rows(v):
        return lax.dynamic_slice_in_dim(v, mine * seq, mine, 0)

    def other_rows(v):
        return lax.dynamic_slice_in_dim(v, mine * (1 - seq), mine, 0)

    def middle_rows(middle, low):
        low = jnp.pad(low[0], ((0, mid - short), (0, 0)))
        return jnp.where(first, middle[0], low), jnp.where(first, low, middle[0])

    x_mid, x_mid_out = middle_rows(tokens_middle, tokens_short)
    x_mid_in = swap_seq(x_mid_out)
    x_own, x_out = own_rows(tokens_long), other_rows(tokens_long)
    x_in = [swap_seq(x_out[i]) for i in range(mine)]
    u_mid, u_mid_out = middle_rows(upstream_middle, upstream_short)
    u_out = jnp.concatenate([other_rows(upstream_long).reshape(mine * half, D), u_mid_out], axis=0)

    place = (seq.astype(jnp.int32).reshape(1), length_short, length_middle, length_long)
    qkv = [query_weight, key_weight, value_weight]
    projections = qkv + [query_bias, value_bias]
    chain = attention_forward(place, x_mid, x_mid_in, projections, mine, 2 * mid, mine * half // mid, None, rows)
    for i in range(mine):
        chain = attention_forward(place, x_own[i], x_in[i], projections, i, 2 * half, i, chain, rows)
    x, q, k, v, ctx, lse, xt = chain
    u_in = swap_seq(later(u_out, lse))

    mats = [output_weight, up_weight, down_weight]
    dense = functools.partial(
        dense_steps, place[0], ctx, x, tokens=tokens, rows=rows, mats=mats,
        vecs=[up_bias, output_bias, attention_gain, attention_shift, down_bias, output_gain, output_shift],
    )
    res_long, *before = dense(ups=[upstream_long], before=None)
    res_other, res_mid, act, dinn, nlow, dbr, datt, dr1, dctx, vec = dense(ups=[u_in, u_in, u_mid], before=before)

    def give_back(own, got):
        body = mine * half
        here, there = (a[:body].reshape(mine, half, D) for a in (own, got))
        long = jnp.concatenate([jnp.where(first, here, there), jnp.where(first, there, here)], axis=0)
        low, middle = jnp.where(first, got[body:], own[body:]), jnp.where(first, own[body:], got[body:])
        return low[None, :short], middle[None], long

    body = half
    first_got = swap_seq(res_other[:body])
    up_pair = up_grad(me_ref, nlow, dinn, tokens)
    first_got = later(first_got, up_pair[0])
    rest_got = swap_seq(later(res_other[body:], first_got))
    down_pair = down_grad(later(me_ref, up_pair[0]), act, dbr, ctx, datt, vec, tokens)

    def ready(value, *sums):
        return later(value, *[h.outgoing for h in sums])

    after_sums = ready if fast else lambda value, *sums: value
    at = lambda before, *sums: (after_sums(later(place[0], before), *sums), *place[1:])
    up = down = wide_sum = []
    if fast:
        up = across_cores(up_pair, down_pair[0], [2304, 2304], ["zxyw", "yxzw"])
    *before, ig_own, ig_other = first_row_backward(
        at(down_pair[0], *up), q, k, v, dctx, lse, dr1, qkv, 2 * half
    )
    if fast:
        up = [h.receive(ig_own).send() for h in up]
        down = across_cores(down_pair, ig_own, [3072, 2816], ["zyxw", "yzxw"])
    rest_got = later(rest_got, ig_own)
    later_rows = (2 * half, 2 * mid)
    *wide, send, keep, bg = group_backward(
        me_ref, at(ig_own, *up, *down), q, k, v, dctx, lse, before, xt, later_rows, 4, 0, None
    )
    wide_pair = (send, keep)
    if fast:
        up = [h.receive(bg).send() for h in up]
        down = [h.receive(bg).send() for h in down]
    ig_got = [swap_seq(later(ig_other, bg))]
    *narrow, send, keep, bg_last = group_backward(
        me_ref, at(bg, *up, *down), q, k, v, dctx, lse, before, xt, later_rows, 2, 4, bg
    )
    narrow_pair = (send, keep)
    ig_got[0] = later(ig_got[0], bg_last)
    if fast:
        up = [join(*[h.receive(bg_last) for h in up]).send()]
        down = [join(*[h.receive(bg_last) for h in down]).send()]
        wide_sum = across_cores(wide_pair, bg_last, [1152, 1152], ["yzxw", "zyxw"])
    own, other = input_grad(
        after_sums(later(dr1, ig_got[0]), *up, *down, *wide_sum), [wide, narrow], [(0, 512), (512, 768)], qkv, later_rows
    )
    ig_got.append(swap_seq(other))
    results = give_back(later(jnp.concatenate([res_long, res_mid], axis=0), own), jnp.concatenate([first_got, rest_got], axis=0))
    if fast:
        up_block = up[0].receive(own).result()
        down = down[0].receive(own).send()
        wide_sum = [h.receive(own).send() for h in wide_sum]
        (narrow_sum,) = across_cores(narrow_pair, own, [1280], ["yzxw"])
        wide_sum = join(*[h.receive() for h in wide_sum]).send()
        narrow_sum.receive().send()
        down_block = down.receive().result()
        narrow_sum.receive().send()
        last = join(wide_sum.receive(), narrow_sum.receive()).send().receive().result()
        done = finish_sums(up_block, down_block, [last[:, :2304], last[:, 2304:]], me)
    else:
        done = reduce_plain(up_pair, down_pair, [wide_pair, narrow_pair], vec, jnp.concatenate([bg, bg_last], axis=1))
    input_grads = give_back(jnp.concatenate([ig_own, own], axis=0), jnp.concatenate(ig_got, axis=0))
    w_query, bq, w_key, w_value, bv, w_out, small, w_up, b_up, w_down = done
    return (
        *results, *input_grads,
        w_query, bq, w_key, w_value, bv, w_out, small[5], small[3], small[4],
        w_up, b_up, w_down, small[2], small[0], small[1],
    )


def solution(mesh):
    tokens = P("dp", "seq", None)
    wide = P(("dp", "seq"), None)
    flat = P(("dp", "seq"))
    in_specs = (tokens,) * 3 + (P("dp"),) * 3 + (P(),) * 15 + (tokens,) * 3
    out_specs = (tokens,) * 6 + (
        wide, flat, wide, wide, flat, wide, flat, flat, flat, wide, flat, wide, flat, flat, flat,
    )
    return jax.shard_map(per_device, mesh=mesh, in_specs=in_specs, out_specs=out_specs, check_vma=False)
```

profile of v0, /device:TPU:0, one launch (start us, length us, event | category | flops | bytes accessed | tf_op | source)
XLA Modules:
  0.0 304.4 jit_solution(4580684192620020812)
XLA Ops:
  0.7 2.5 dynamic-slice_bitcast_fusion
  3.2 2.9 collective-permute-start.1
  6.9 2.0 collective-permute-start
  11.1 9.2 %collective-permute-done.2.xr = bf16[128,768]{1,0:T(8,128)(2,1)S(1)} collective-permute-done((bf16[128,768]{1,0:T(8,128)(2,1)S(1)}, bf16[128,768]{1,0:T(8,128)(2,1)S(1)}, u32[]{:S(2)}, u32[]{:S(2)}) %collective-permute-start.2) | collective-permute-done | bytes 196640 | tf_op jit(solution)/shard_map/ppermute | solution.py:555
  21.0 6.3 %attend_2.1 = (bf16[1536,768]{1,0:T(8,128)(2,1)}, bf16[1536,768]{1,0:T(8,128)(2,1)}, bf16[1536,768]{1,0:T(8,128)(2,1)}, bf16[1536,768]{1,0:T(8,128)(2,1)}, bf16[...) custom-call(s32[1]{0:T(128)} %bitcast.s0._, s32[1]{0:T(128)S(6)} %copy.104.s1, s32[1]{0:T(128)S(6)} %copy.105.s2, ...), custom_call_target="tpu_custom_call" | custom-call | flops 1024 | bytes 1024 | tf_op jit(solution)/shard_map/attend_2/pallas_call | solution.py:152
  27.3 9.9 %attend_0.1 = (bf16[1536,768]{1,0:T(8,128)(2,1)}, bf16[1536,768]{1,0:T(8,128)(2,1)}, bf16[1536,768]{1,0:T(8,128)(2,1)}, bf16[1536,768]{1,0:T(8,128)(2,1)}, bf16[...) custom-call(s32[1]{0:T(128)} %bitcast.s0._, ...), custom_call_target="tpu_custom_call", output_to_operand_aliasing={{0}: (11, {}), {1}: (12, {}), {2}: (13, {}), {3}: (14, {}),... | custom-call | flops 1024 | bytes 1024 | tf_op jit(solution)/shard_map/attend_0/pallas_call | solution.py:152
  38.0 10.1 %attend_1.1 = (bf16[1536,768]{1,0:T(8,128)(2,1)}, bf16[1536,768]{1,0:T(8,128)(2,1)}, bf16[1536,768]{1,0:T(8,128)(2,1)}, bf16[1536,768]{1,0:T(8,128)(2,1)}, bf16[...) custom-call(s32[1]{0:T(128)} %bitcast.s0._, ...), custom_call_target="tpu_custom_call", output_to_operand_aliasing={{0}: (11, {}), {1}: (12, {}), {2}: (13, {}), {3}: (14, {}),... | custom-call | flops 1024 | bytes 1024 | tf_op jit(solution)/shard_map/attend_1/pallas_call | solution.py:152
  48.1 2.1 collective-permute-start.3
  50.2 24.5 %dense_own.1 = (bf16[512,768]{1,0:T(8,128)(2,1)}, bf16[1280,3072]{1,0:T(8,128)(2,1)}, bf16[1280,3072]{1,0:T(8,128)(2,1)}, bf16[1280,768]{1,0:T(8,128)(2,1)}, bf1...) custom-call(s32[1]{0:T(128)} %bitcast.s0._, ...), custom_call_target="tpu_custom_call" | custom-call | flops 1024 | bytes 1024 | tf_op jit(solution)/shard_map/dense_own/pallas_call | solution.py:285
  75.6 43.7 %dense_rest.1 = (bf16[640,768]{1,0:T(8,128)(2,1)}, bf16[128,768]{1,0:T(8,128)(2,1)}, bf16[1280,3072]{1,0:T(8,128)(2,1)}, bf16[1280,3072]{1,0:T(8,128)(2,1)}, bf1...) custom-call(s32[1]{0:T(128)} %bitcast.s0._, ...), custom_call_target="tpu_custom_call", output_to_operand_aliasing={{2}: (17, {}), {3}: (18, {}), {4}: (19, {}), {5}: (20, {}),... | custom-call | flops 1024 | bytes 1024 | tf_op jit(solution)/shard_map/dense_rest/pallas_call | solution.py:285
  119.3 13.3 %up_grad.1 = (bf16[16,16,4608]{2,1,0:T(8,128)(2,1)}, bf16[16,16,4608]{2,1,0:T(8,128)(2,1)}) custom-call(s32[1]{0:T(128)} %bitcast.10.me, bf16[1280,768]{1,0:T(8,128)(2,1)} %get-tuple-element.145.nlow, bf16[1280,3072]{1,0:T(8,128)(2,1)} %get-tuple-element.146.left.right, bf16[1280,3072]{1,0:T(8,128)(2,1)} %get-tuple-element.146.left.right), custom_call_target="tpu_custom_call" | custom-call | flops 1024 | bytes 1024 | tf_op jit(solution)/shard_map/up_grad/pallas_call | solution.py:320
  133.5 14.6 %down_grad.1 = (bf16[16,16,5888]{2,1,0:T(8,128)(2,1)}, bf16[16,16,5888]{2,1,0:T(8,128)(2,1)}) custom-call(s32[1]{0:T(128)} %bitcast.10.me, bf16[1280,3072]{1,0:T(8,128)(2,1)} %get-tuple-element.151.act, bf16[1280,768]{1,0:T(8,128)(2,1)} %get-tuple-element.152.dbr, bf16[1536,768]{1,0:T(8,128)(2,1)} %get-tuple-element.132.refs_0_.ctx, ...), custom_call_target="tpu_custom_call" | custom-call | flops 1024 | bytes 1024 | tf_op jit(solution)/shard_map/down_grad/pallas_call | solution.py:368
  149.4 1.7 collective-permute-start.5
  151.2 2.0 add_convert_fusion.2
  153.2 1.5 collective-permute-start.8
  154.7 2.0 add_convert_fusion.3
  156.7 1.6 collective-permute-start.7
  159.3 15.4 %back_first.1 = (bf16[512,768]{1,0:T(8,128)(2,1)}, bf16[512,768]{1,0:T(8,128)(2,1)}, bf16[512,768]{1,0:T(8,128)(2,1)}, bf16[256,768]{1,0:T(8,128)(2,1)}, bf16[256,768]{1,0:T(8,128)(2,1)}) custom-call(s32[1]{0:T(128)} %bitcast.s0._, s32[1]{0:T(128)S(6)} %copy.104.s1, s32[1]{0:T(128)S(6)} %copy.105.s2, s32[4]{0:T(128)} %s3.11, ...), custom_call_target="tpu_custom_call" | custom-call | flops 1024 | bytes 1024 | tf_op jit(solution)/shard_map/back_first/pallas_call | solution.py:430
  174.7 2.0 add_convert_fusion.10
  177.2 2.0 add_convert_fusion.9
  179.2 1.5 collective-permute-start.12
  180.7 2.1 add_convert_fusion.1
  183.3 2.2 add_convert_fusion
  186.0 17.3 %back_group_0.1 = (bf16[1024,512]{1,0:T(8,128)(2,1)}, bf16[1024,512]{1,0:T(8,128)(2,1)}, bf16[1024,512]{1,0:T(8,128)(2,1)}, bf16[16,16,2304]{2,1,0:T(8,128)(2,1)...) custom-call(s32[1]{0:T(128)} %bitcast.10.me, s32[1]{0:T(128)} %bitcast.s0._, s32[1]{0:T(128)S(6)} %copy.104.s1, ...), custom_call_target="tpu_custom_call" | custom-call | flops 1024 | bytes 1024 | tf_op jit(solution)/shard_map/back_group_0/pallas_call | solution.py:498
  203.8 2.2 add_convert_fusion.16
  206.0 1.8 collective-permute-start.16
  207.8 1.5 collective-permute-start.15
  209.3 2.0 add_convert_fusion.5
  211.7 2.0 add_convert_fusion.4
  213.8 10.9 %back_group_4.1 = (bf16[1024,256]{1,0:T(8,128)(2,1)}, bf16[1024,256]{1,0:T(8,128)(2,1)}, bf16[1024,256]{1,0:T(8,128)(2,1)}, bf16[16,16,1280]{2,1,0:T(8,128)(2,1)...) custom-call(s32[1]{0:T(128)} %bitcast.10.me, s32[1]{0:T(128)} %bitcast.s0._, s32[1]{0:T(128)S(6)} %copy.104.s1, ...), custom_call_target="tpu_custom_call" | custom-call | flops 1024 | bytes 1024 | tf_op jit(solution)/shard_map/back_group_4/pallas_call | solution.py:498
  227.0 2.8 collective-permute-start.33
  231.0 4.3 %collective-permute-done.17 = bf16[2,1,1,2,16,3072]{5,4,3,2,1,0:T(8,128)(2,1)S(1)} collective-permute-done((bf16[2,1,1,2,16,3072]{5,4,3,2,1,0:T(8,128)(2,1)}, bf16[2,1,1,2,16,3072]{5,4,3,2,1,0:T(8,128)(2,1)S(1)}, u32[]{:S(2)}, u32[]{:S(2)}) %collective-permute-start.17) | collective-permute-done | bytes 393248 | tf_op jit(solution)/shard_map/ppermute | solution.py:560
  236.6 1.8 add_convert_fusion.7
  239.1 1.8 add_convert_fusion.8
  240.8 1.5 collective-permute-start.31
  242.4 1.6 collective-permute-start.23
  244.4 8.0 %input_grad.1 = (bf16[384,768]{1,0:T(8,128)(2,1)}, bf16[384,768]{1,0:T(8,128)(2,1)}) custom-call(f32[1536,768]{1,0:T(8,128)} %get-tuple-element.198.dr1, bf16[1024,512]{1,0:T(8,128)(2,1)} %get-tuple-element.199.rest_0_, bf16[1024,512]{1,0:T(8,128)(2,1)} %get-tuple-element.200.rest_1_, bf16[1024,512]{1,0:T(8,128)(2,1)} %get-tuple-element.201.rest_2_, ...), custom_call_target="tpu_custom_call" | custom-call | flops 1024 | bytes 1024 | tf_op jit(solution)/shard_map/input_grad/pallas_call | solution.py:541
  255.1 1.6 select_bitcast_fusion.1
  257.4 1.8 add_convert_fusion.6
  259.2 1.5 collective-permute-start.27
  265.2 2.7 collective-permute-start.32
  271.5 1.5 collective-permute-start.25
  281.4 1.9 broadcast_select_fusion.1
  283.3 1.6 select_bitcast_fusion
  287.6 1.6 collective-permute-start.29
  290.4 1.7 collective-permute-done.29
  293.0 3.4 %collective-permute-start.30 = (bf16[1,1,1,1,16,3584]{5,4,3,2,1,0:T(8,128)(2,1)S(1)}, bf16[1,1,1,1,16,3584]{5,4,3,2,1,0:T(8,128)(2,1)S(1)}, u32[]{:S(2)}, u32[]{:S(2)}) collective-permute-start(bf16[1,1,1,1,16,3584]{5,4,3,2,1,0:T(8,128)(2,1)S(1)} %pad_maximum_fusion.13), channel_id=1, source_target_pairs={{0,16},{2,18},{4,20},{6,22},{8,24},{10,26},{12,28},{14,30},{16,0},... | collective-permute-start | bytes 344072 | tf_op jit(solution)/shard_map/ppermute | solution.py:560
  297.7 2.7 collective-permute-done.30
  (152 shorter events, 45.0 us)
Async XLA Ops:
  0.7 5.5 %copy-start.24 = (bf16[1,64,768]{2,1,0:T(8,128)(2,1)S(1)}, bf16[1,64,768]{2,1,0:T(8,128)(2,1)}, u32[]{:S(2)}) copy-start(bf16[1,64,768]{2,1,0:T(8,128)(2,1)} %param.24) | copy-start | bytes 294916
  0.7 5.5 %copy-start.18 = (bf16[1,128,768]{2,1,0:T(8,128)(2,1)S(1)}, bf16[1,128,768]{2,1,0:T(8,128)(2,1)}, u32[]{:S(2)}) copy-start(bf16[1,128,768]{2,1,0:T(8,128)(2,1)} %param.25) | copy-start | bytes 589828
  0.7 8.2 %copy-start.25 = (bf16[1,64,768]{2,1,0:T(8,128)(2,1)S(1)}, bf16[1,64,768]{2,1,0:T(8,128)(2,1)}, u32[]{:S(2)}) copy-start(bf16[1,64,768]{2,1,0:T(8,128)(2,1)} %param.45) | copy-start | bytes 294916
  0.7 8.2 %copy-start.19 = (bf16[1,128,768]{2,1,0:T(8,128)(2,1)S(1)}, bf16[1,128,768]{2,1,0:T(8,128)(2,1)}, u32[]{:S(2)}) copy-start(bf16[1,128,768]{2,1,0:T(8,128)(2,1)} %param.46) | copy-start | bytes 589828
  0.7 9.0 %copy-start.1 = (bf16[4,256,768]{2,1,0:T(8,128)(2,1)S(1)}, bf16[4,256,768]{2,1,0:T(8,128)(2,1)}, u32[]{:S(2)}) copy-start(bf16[4,256,768]{2,1,0:T(8,128)(2,1)} %refs_2_.1) | copy-start | bytes 4718596
  3.2 24.1 %collective-permute-start.1 = (bf16[256,768]{1,0:T(8,128)(2,1)S(1)}, bf16[256,768]{1,0:T(8,128)(2,1)}, u32[]{:S(2)}, u32[]{:S(2)}) collective-permute-start(bf16[256,768]{1,0:T(8,128)(2,1)S(1)} %get-tuple-element.233), channel_id=1, source_target_pairs={{0,1},{1,0},{2,3},{3,2},{4,5},{5,4},{6,7},{7,6},{8,9},{9,8},{10,11... | collective-permute-start | bytes 1179656 | tf_op jit(solution)/shard_map/ppermute | solution.py:555
  6.9 13.4 %collective-permute-start.2 = (bf16[128,768]{1,0:T(8,128)(2,1)S(1)}, bf16[128,768]{1,0:T(8,128)(2,1)S(1)}, u32[]{:S(2)}, u32[]{:S(2)}) collective-permute-start(bf16[128,768]{1,0:T(8,128)(2,1)S(1)} %get-tuple-element.251), channel_id=1, source_target_pairs={{0,1},{1,0},{2,3},{3,2},{4,5},{5,4},{6,7},{7,6},{8,9},{9,8},{10,11... | collective-permute-start | bytes 589832 | tf_op jit(solution)/shard_map/ppermute | solution.py:555
  6.9 30.3 %collective-permute-start = (bf16[256,768]{1,0:T(8,128)(2,1)S(1)}, bf16[256,768]{1,0:T(8,128)(2,1)S(1)}, u32[]{:S(2)}, u32[]{:S(2)}) collective-permute-start(bf16[256,768]{1,0:T(8,128)(2,1)S(1)} %get-tuple-element.234), channel_id=1, source_target_pairs={{0,1},{1,0},{2,3},{3,2},{4,5},{5,4},{6,7},{7,6},{8,9},{9,8},{10,11... | collective-permute-start | bytes 1179656 | tf_op jit(solution)/shard_map/ppermute | solution.py:555
  48.1 26.5 %collective-permute-start.3 = (bf16[640,768]{1,0:T(8,128)(2,1)S(1)}, bf16[640,768]{1,0:T(8,128)(2,1)S(1)}, u32[]{:S(2)}, u32[]{:S(2)}) collective-permute-start(bf16[640,768]{1,0:T(8,128)(2,1)S(1)} %pad_maximum_fusion.2), channel_id=1, source_target_pairs={{0,1},{1,0},{2,3},{3,2},{4,5},{5,4},{6,7},{7,6},{8,9},{9,8},{10,11... | collective-permute-start | bytes 2949128 | tf_op jit(solution)/shard_map/ppermute | solution.py:555
  119.3 13.3 %copy-start.10 = (bf16[640,768]{1,0:T(8,128)(2,1)S(1)}, bf16[640,768]{1,0:T(8,128)(2,1)}, u32[]{:S(2)}) copy-start(bf16[640,768]{1,0:T(8,128)(2,1)} %get-tuple-element.144) | copy-start | bytes 2949124
  132.6 18.5 %collective-permute-start.6 = (bf16[16,16,4608]{2,1,0:T(8,128)(2,1)}, bf16[16,16,4608]{2,1,0:T(8,128)(2,1)}, u32[]{:S(2)}, u32[]{:S(2)}) collective-permute-start(bf16[16,16,4608]{2,1,0:T(8,128)(2,1)} %get-tuple-element.147), channel_id=1, source_target_pairs={{0,2},{2,0},{4,6},{6,4},{8,10},{10,8},{12,14},{14,12},{16,18},{18,... | collective-permute-start | bytes 7077896 | tf_op jit(solution)/shard_map/ppermute | solution.py:560
  133.4 16.0 %collective-permute-start.4 = (bf16[256,768]{1,0:T(8,128)(2,1)}, bf16[256,768]{1,0:T(8,128)(2,1)}, u32[]{:S(2)}, u32[]{:S(2)}) collective-permute-start(bf16[256,768]{1,0:T(8,128)(2,1)} %slice.785), channel_id=1, source_target_pairs={{0,1},{1,0},{2,3},{3,2},{4,5},{5,4},{6,7},{7,6},{8,9},{9,8},{10,11... | collective-permute-start | bytes 1179656 | tf_op jit(solution)/shard_map/ppermute | solution.py:555
  133.5 17.7 %copy-start.3 = (bf16[16,16,4608]{2,1,0:T(8,128)(2,1)S(1)}, bf16[16,16,4608]{2,1,0:T(8,128)(2,1)}, u32[]{:S(2)}) copy-start(bf16[16,16,4608]{2,1,0:T(8,128)(2,1)} %get-tuple-element.157) | copy-start | bytes 7077892
  148.1 10.2 %copy-start.11 = (bf16[512,768]{1,0:T(8,128)(2,1)S(1)}, bf16[512,768]{1,0:T(8,128)(2,1)}, u32[]{:S(2)}) copy-start(bf16[512,768]{1,0:T(8,128)(2,1)} %get-tuple-element.167) | copy-start | bytes 2359300
  148.9 31.8 %collective-permute-start.9 = (bf16[16,16,5888]{2,1,0:T(8,128)(2,1)}, bf16[16,16,5888]{2,1,0:T(8,128)(2,1)}, u32[]{:S(2)}, u32[]{:S(2)}) collective-permute-start(bf16[16,16,5888]{2,1,0:T(8,128)(2,1)} %get-tuple-element.155), channel_id=1, source_target_pairs={{0,2},{2,0},{4,6},{6,4},{8,10},{10,8},{12,14},{14,12},{16,18},{18,... | collective-permute-start | bytes 9043976 | tf_op jit(solution)/shard_map/ppermute | solution.py:560
  149.4 25.3 %collective-permute-start.5 = (bf16[384,768]{1,0:T(8,128)(2,1)}, bf16[384,768]{1,0:T(8,128)(2,1)}, u32[]{:S(2)}, u32[]{:S(2)}) collective-permute-start(bf16[384,768]{1,0:T(8,128)(2,1)} %slice.784), channel_id=1, source_target_pairs={{0,1},{1,0},{2,3},{3,2},{4,5},{5,4},{6,7},{7,6},{8,9},{9,8},{10,11... | collective-permute-start | bytes 1769480 | tf_op jit(solution)/shard_map/ppermute | solution.py:555
  153.2 21.5 %collective-permute-start.8 = (bf16[2,2,1,2,16,2304]{5,4,3,2,1,0:T(8,128)(2,1)}, bf16[2,2,1,2,16,2304]{5,4,3,2,1,0:T(8,128)(2,1)}, u32[]{:S(2)}, u32[]{:S(2)}) collective-permute-start(bf16[2,2,1,2,16,2304]{5,4,3,2,1,0:T(8,128)(2,1)} %add_convert_fusion.2), channel_id=1, source_target_pairs={{0,4},{2,6},{4,0},{6,2},{8,12},{10,14},{12,8},{14,10},{16,20},{18,... | collective-permute-start | bytes 1769480 | tf_op jit(solution)/shard_map/ppermute | solution.py:560
  156.7 18.0 %collective-permute-start.7 = (bf16[2,1,2,2,16,2304]{5,4,3,2,1,0:T(8,128)(2,1)}, bf16[2,1,2,2,16,2304]{5,4,3,2,1,0:T(8,128)(2,1)}, u32[]{:S(2)}, u32[]{:S(2)}) collective-permute-start(bf16[2,1,2,2,16,2304]{5,4,3,2,1,0:T(8,128)(2,1)} %add_convert_fusion.3), channel_id=1, source_target_pairs={{0,8},{2,10},{4,12},{6,14},{8,0},{10,2},{12,4},{14,6},{16,24},{18,... | collective-permute-start | bytes 1769480 | tf_op jit(solution)/shard_map/ppermute | solution.py:560
  159.3 21.4 %copy-start.2 = (bf16[16,16,5888]{2,1,0:T(8,128)(2,1)S(1)}, bf16[16,16,5888]{2,1,0:T(8,128)(2,1)}, u32[]{:S(2)}) copy-start(bf16[16,16,5888]{2,1,0:T(8,128)(2,1)} %get-tuple-element.173) | copy-start | bytes 9043972
  176.7 26.7 %collective-permute-start.11 = (bf16[2,1,2,1,16,2304]{5,4,3,2,1,0:T(8,128)(2,1)}, bf16[2,1,2,1,16,2304]{5,4,3,2,1,0:T(8,128)(2,1)}, u32[]{:S(2)}, u32[]{:S(2)}) collective-permute-start(bf16[2,1,2,1,16,2304]{5,4,3,2,1,0:T(8,128)(2,1)} %add_convert_fusion.10), channel_id=1, source_target_pairs={{0,1},{1,0},{2,3},{3,2},{4,5},{5,4},{6,7},{7,6},{8,9},{9,8},{10,11... | collective-permute-start | bytes 884744 | tf_op jit(solution)/shard_map/ppermute | solution.py:555
  179.2 24.6 %collective-permute-start.12 = (bf16[2,2,1,1,16,2304]{5,4,3,2,1,0:T(8,128)(2,1)}, bf16[2,2,1,1,16,2304]{5,4,3,2,1,0:T(8,128)(2,1)}, u32[]{:S(2)}, u32[]{:S(2)}) collective-permute-start(bf16[2,2,1,1,16,2304]{5,4,3,2,1,0:T(8,128)(2,1)} %add_convert_fusion.9), channel_id=1, source_target_pairs={{0,1},{1,0},{2,3},{3,2},{4,5},{5,4},{6,7},{7,6},{8,9},{9,8},{10,11... | collective-permute-start | bytes 884744 | tf_op jit(solution)/shard_map/ppermute | solution.py:555
  182.8 25.0 %collective-permute-start.14 = (bf16[2,2,1,2,16,2816]{5,4,3,2,1,0:T(8,128)(2,1)}, bf16[2,2,1,2,16,2816]{5,4,3,2,1,0:T(8,128)(2,1)}, u32[]{:S(2)}, u32[]{:S(2)}) collective-permute-start(bf16[2,2,1,2,16,2816]{5,4,3,2,1,0:T(8,128)(2,1)} %add_convert_fusion.1), channel_id=1, source_target_pairs={{0,4},{2,6},{4,0},{6,2},{8,12},{10,14},{12,8},{14,10},{16,20},{18,... | collective-permute-start | bytes 2162696 | tf_op jit(solution)/shard_map/ppermute | solution.py:560
  185.6 25.7 %collective-permute-start.13 = (bf16[2,1,2,2,16,3072]{5,4,3,2,1,0:T(8,128)(2,1)}, bf16[2,1,2,2,16,3072]{5,4,3,2,1,0:T(8,128)(2,1)}, u32[]{:S(2)}, u32[]{:S(2)}) collective-permute-start(bf16[2,1,2,2,16,3072]{5,4,3,2,1,0:T(8,128)(2,1)} %add_convert_fusion), channel_id=1, source_target_pairs={{0,8},{2,10},{4,12},{6,14},{8,0},{10,2},{12,4},{14,6},{16,24},{18,... | collective-permute-start | bytes 2359304 | tf_op jit(solution)/shard_map/ppermute | solution.py:560
  203.3 27.7 %collective-permute-start.19 = (bf16[16,16,2304]{2,1,0:T(8,128)(2,1)}, bf16[16,16,2304]{2,1,0:T(8,128)(2,1)}, u32[]{:S(2)}, u32[]{:S(2)}) collective-permute-start(bf16[16,16,2304]{2,1,0:T(8,128)(2,1)} %get-tuple-element.196), channel_id=1, source_target_pairs={{0,2},{2,0},{4,6},{6,4},{8,10},{10,8},{12,14},{14,12},{16,18},{18,... | collective-permute-start | bytes 3538952 | tf_op jit(solution)/shard_map/ppermute | solution.py:560
  203.4 21.6 %collective-permute-start.10 = (bf16[256,768]{1,0:T(8,128)(2,1)}, bf16[256,768]{1,0:T(8,128)(2,1)}, u32[]{:S(2)}, u32[]{:S(2)}) collective-permute-start(bf16[256,768]{1,0:T(8,128)(2,1)} %get-tuple-element.181), channel_id=1, source_target_pairs={{0,1},{1,0},{2,3},{3,2},{4,5},{5,4},{6,7},{7,6},{8,9},{9,8},{10,11... | collective-permute-start | bytes 1179656 | tf_op jit(solution)/shard_map/ppermute | solution.py:555
  206.0 18.6 %collective-permute-start.16 = (bf16[2,1,1,1,16,2304]{5,4,3,2,1,0:T(8,128)(2,1)}, bf16[2,1,1,1,16,2304]{5,4,3,2,1,0:T(8,128)(2,1)}, u32[]{:S(2)}, u32[]{:S(2)}) collective-permute-start(bf16[2,1,1,1,16,2304]{5,4,3,2,1,0:T(8,128)(2,1)} %get-tuple-element.219), channel_id=1, source_target_pairs={{0,8},{2,10},{4,12},{6,14},{8,0},{10,2},{12,4},{14,6},{16,24},{18,... | collective-permute-start | bytes 442376 | tf_op jit(solution)/shard_map/ppermute | solution.py:560
  207.8 17.2 %collective-permute-start.15 = (bf16[2,1,1,1,16,2304]{5,4,3,2,1,0:T(8,128)(2,1)}, bf16[2,1,1,1,16,2304]{5,4,3,2,1,0:T(8,128)(2,1)}, u32[]{:S(2)}, u32[]{:S(2)}) collective-permute-start(bf16[2,1,1,1,16,2304]{5,4,3,2,1,0:T(8,128)(2,1)} %get-tuple-element.220), channel_id=1, source_target_pairs={{0,4},{2,6},{4,0},{6,2},{8,12},{10,14},{12,8},{14,10},{16,20},{18,... | collective-permute-start | bytes 442376 | tf_op jit(solution)/shard_map/ppermute | solution.py:560
  211.3 18.5 %collective-permute-start.18 = (bf16[2,1,1,2,16,2816]{5,4,3,2,1,0:T(8,128)(2,1)}, bf16[2,1,1,2,16,2816]{5,4,3,2,1,0:T(8,128)(2,1)}, u32[]{:S(2)}, u32[]{:S(2)}) collective-permute-start(bf16[2,1,1,2,16,2816]{5,4,3,2,1,0:T(8,128)(2,1)} %add_convert_fusion.5), channel_id=1, source_target_pairs={{0,8},{2,10},{4,12},{6,14},{8,0},{10,2},{12,4},{14,6},{16,24},{18,... | collective-permute-start | bytes 1081352 | tf_op jit(solution)/shard_map/ppermute | solution.py:560
  224.6 11.9 %copy-start.8 = (bf16[16,16,2304]{2,1,0:T(8,128)(2,1)S(1)}, bf16[16,16,2304]{2,1,0:T(8,128)(2,1)}, u32[]{:S(2)}) copy-start(bf16[16,16,2304]{2,1,0:T(8,128)(2,1)} %get-tuple-element.195) | copy-start | bytes 3538948
  224.7 10.6 %collective-permute-start.17 = (bf16[2,1,1,2,16,3072]{5,4,3,2,1,0:T(8,128)(2,1)}, bf16[2,1,1,2,16,3072]{5,4,3,2,1,0:T(8,128)(2,1)S(1)}, u32[]{:S(2)}, u32[]{:S(2)}) collective-permute-start(bf16[2,1,1,2,16,3072]{5,4,3,2,1,0:T(8,128)(2,1)} %add_convert_fusion.4), channel_id=1, source_target_pairs={{0,4},{2,6},{4,0},{6,2},{8,12},{10,14},{12,8},{14,10},{16,20},{18,... | collective-permute-start | bytes 1179656 | tf_op jit(solution)/shard_map/ppermute | solution.py:560
  227.0 25.4 %collective-permute-start.33 = (bf16[1,1,1,1,16,4608]{5,4,3,2,1,0:T(8,128)(2,1)}, bf16[1,1,1,1,16,4608]{5,4,3,2,1,0:T(8,128)(2,1)}, u32[]{:S(2)}, u32[]{:S(2)}) collective-permute-start(bf16[1,1,1,1,16,4608]{5,4,3,2,1,0:T(8,128)(2,1)} %pad_maximum_fusion.11), channel_id=1, source_target_pairs={{0,16},{2,18},{4,20},{6,22},{8,24},{10,26},{12,28},{14,30},{16,0},... | collective-permute-start | bytes 442376 | tf_op jit(solution)/shard_map/ppermute | solution.py:560
  229.8 27.6 %collective-permute-start.26 = (bf16[16,16,1280]{2,1,0:T(8,128)(2,1)}, bf16[16,16,1280]{2,1,0:T(8,128)(2,1)}, u32[]{:S(2)}, u32[]{:S(2)}) collective-permute-start(bf16[16,16,1280]{2,1,0:T(8,128)(2,1)} %get-tuple-element.211), channel_id=1, source_target_pairs={{0,2},{2,0},{4,6},{6,4},{8,10},{10,8},{12,14},{14,12},{16,18},{18,... | collective-permute-start | bytes 1966088 | tf_op jit(solution)/shard_map/ppermute | solution.py:560
  235.3 5.6 %copy-start.13 = (bf16[2,1,1,2,16,3072]{5,4,3,2,1,0:T(8,128)(2,1)}, bf16[2,1,1,2,16,3072]{5,4,3,2,1,0:T(8,128)(2,1)S(1)}, u32[]{:S(2)}) copy-start(bf16[2,1,1,2,16,3072]{5,4,3,2,1,0:T(8,128)(2,1)S(1)} %collective-permute-done.17) | copy-start | bytes 1179652
  240.8 22.2 %collective-permute-start.31 = (bf16[2,1,1,1,16,5888]{5,4,3,2,1,0:T(8,128)(2,1)}, bf16[2,1,1,1,16,5888]{5,4,3,2,1,0:T(8,128)(2,1)}, u32[]{:S(2)}, u32[]{:S(2)}) collective-permute-start(bf16[2,1,1,1,16,5888]{5,4,3,2,1,0:T(8,128)(2,1)} %pad_maximum_fusion.8), channel_id=1, source_target_pairs={{0,1},{1,0},{2,3},{3,2},{4,5},{5,4},{6,7},{7,6},{8,9},{9,8},{10,11... | collective-permute-start | bytes 1130504 | tf_op jit(solution)/shard_map/ppermute | solution.py:555
  242.4 18.4 %collective-permute-start.23 = (bf16[2,1,2,2,16,1152]{5,4,3,2,1,0:T(8,128)(2,1)}, bf16[2,1,2,2,16,1152]{5,4,3,2,1,0:T(8,128)(2,1)}, u32[]{:S(2)}, u32[]{:S(2)}) collective-permute-start(bf16[2,1,2,2,16,1152]{5,4,3,2,1,0:T(8,128)(2,1)} %add_convert_fusion.7), channel_id=1, source_target_pairs={{0,8},{2,10},{4,12},{6,14},{8,0},{10,2},{12,4},{14,6},{16,24},{18,... | collective-permute-start | bytes 884744 | tf_op jit(solution)/shard_map/ppermute | solution.py:560
  243.9 16.8 %collective-permute-start.21 = (bf16[2,2,1,2,16,1152]{5,4,3,2,1,0:T(8,128)(2,1)}, bf16[2,2,1,2,16,1152]{5,4,3,2,1,0:T(8,128)(2,1)}, u32[]{:S(2)}, u32[]{:S(2)}) collective-permute-start(bf16[2,2,1,2,16,1152]{5,4,3,2,1,0:T(8,128)(2,1)} %add_convert_fusion.8), channel_id=1, source_target_pairs={{0,4},{2,6},{4,0},{6,2},{8,12},{10,14},{12,8},{14,10},{16,20},{18,... | collective-permute-start | bytes 884744 | tf_op jit(solution)/shard_map/ppermute | solution.py:560
  253.8 9.2 %copy-start.14 = (bf16[2,1,1,2,16,3072]{5,4,3,2,1,0:T(8,128)(2,1)S(1)}, bf16[2,1,1,2,16,3072]{5,4,3,2,1,0:T(8,128)(2,1)}, u32[]{:S(2)}) copy-start(bf16[2,1,1,2,16,3072]{5,4,3,2,1,0:T(8,128)(2,1)} %copy-done.13) | copy-start | bytes 1179652
  254.6 26.8 %collective-permute-start.20 = (bf16[384,768]{1,0:T(8,128)(2,1)}, bf16[384,768]{1,0:T(8,128)(2,1)}, u32[]{:S(2)}, u32[]{:S(2)}) collective-permute-start(bf16[384,768]{1,0:T(8,128)(2,1)} %get-tuple-element.207), channel_id=1, source_target_pairs={{0,1},{1,0},{2,3},{3,2},{4,5},{5,4},{6,7},{7,6},{8,9},{9,8},{10,11... | collective-permute-start | bytes 1769480 | tf_op jit(solution)/shard_map/ppermute | solution.py:555
  259.2 20.2 %collective-permute-start.27 = (bf16[2,2,1,2,16,1280]{5,4,3,2,1,0:T(8,128)(2,1)}, bf16[2,2,1,2,16,1280]{5,4,3,2,1,0:T(8,128)(2,1)}, u32[]{:S(2)}, u32[]{:S(2)}) collective-permute-start(bf16[2,2,1,2,16,1280]{5,4,3,2,1,0:T(8,128)(2,1)} %add_convert_fusion.6), channel_id=1, source_target_pairs={{0,4},{2,6},{4,0},{6,2},{8,12},{10,14},{12,8},{14,10},{16,20},{18,... | collective-permute-start | bytes 983048 | tf_op jit(solution)/shard_map/ppermute | solution.py:560
  262.1 6.1 %collective-permute-start.22 = (bf16[2,1,1,2,16,1152]{5,4,3,2,1,0:T(8,128)(2,1)S(1)}, bf16[2,1,1,2,16,1152]{5,4,3,2,1,0:T(8,128)(2,1)S(1)}, u32[]{:S(2)}, u32[]{:S(2)}) collective-permute-start(bf16[2,1,1,2,16,1152]{5,4,3,2,1,0:T(8,128)(2,1)S(1)} %get-tuple-element.227), channel_id=1, source_target_pairs={{0,8},{2,10},{4,12},{6,14},{8,0},{10,2},{12,4},{14,6},{16,24},{18,... | collective-permute-start | bytes 442376 | tf_op jit(solution)/shard_map/ppermute | solution.py:560
  262.6 6.9 %collective-permute-start.24 = (bf16[2,1,1,2,16,1152]{5,4,3,2,1,0:T(8,128)(2,1)S(1)}, bf16[2,1,1,2,16,1152]{5,4,3,2,1,0:T(8,128)(2,1)S(1)}, u32[]{:S(2)}, u32[]{:S(2)}) collective-permute-start(bf16[2,1,1,2,16,1152]{5,4,3,2,1,0:T(8,128)(2,1)S(1)} %get-tuple-element.228), channel_id=1, source_target_pairs={{0,4},{2,6},{4,0},{6,2},{8,12},{10,14},{12,8},{14,10},{16,20},{18,... | collective-permute-start | bytes 442376 | tf_op jit(solution)/shard_map/ppermute | solution.py:560
  265.2 8.6 %collective-permute-start.32 = (bf16[1,1,1,1,16,5888]{5,4,3,2,1,0:T(8,128)(2,1)S(1)}, bf16[1,1,1,1,16,5888]{5,4,3,2,1,0:T(8,128)(2,1)S(1)}, u32[]{:S(2)}, u32[]{:S(2)}) collective-permute-start(bf16[1,1,1,1,16,5888]{5,4,3,2,1,0:T(8,128)(2,1)S(1)} %pad_maximum_fusion.10), channel_id=1, source_target_pairs={{0,16},{2,18},{4,20},{6,22},{8,24},{10,26},{12,28},{14,30},{16,0},... | collective-permute-start | bytes 565256 | tf_op jit(solution)/shard_map/ppermute | solution.py:560
  268.2 6.6 %copy-start.20 = (bf16[2,1,1,2,16,1152]{5,4,3,2,1,0:T(8,128)(2,1)}, bf16[2,1,1,2,16,1152]{5,4,3,2,1,0:T(8,128)(2,1)S(1)}, u32[]{:S(2)}) copy-start(bf16[2,1,1,2,16,1152]{5,4,3,2,1,0:T(8,128)(2,1)S(1)} %collective-permute-done.22) | copy-start | bytes 442372
  271.5 13.5 %collective-permute-start.25 = (bf16[2,1,1,1,16,2304]{5,4,3,2,1,0:T(8,128)(2,1)}, bf16[2,1,1,1,16,2304]{5,4,3,2,1,0:T(8,128)(2,1)}, u32[]{:S(2)}, u32[]{:S(2)}) collective-permute-start(bf16[2,1,1,1,16,2304]{5,4,3,2,1,0:T(8,128)(2,1)} %pad_maximum_fusion.12), channel_id=1, source_target_pairs={{0,1},{1,0},{2,3},{3,2},{4,5},{5,4},{6,7},{7,6},{8,9},{9,8},{10,11... | collective-permute-start | bytes 442376 | tf_op jit(solution)/shard_map/ppermute | solution.py:555
  276.1 5.3 %copy-start.9 = (bf16[384,768]{1,0:T(8,128)(2,1)S(1)}, bf16[384,768]{1,0:T(8,128)(2,1)}, u32[]{:S(2)}) copy-start(bf16[384,768]{1,0:T(8,128)(2,1)} %get-tuple-element.205) | copy-start | bytes 1769476
  280.6 6.0 %collective-permute-start.28 = (bf16[2,1,1,2,16,1280]{5,4,3,2,1,0:T(8,128)(2,1)S(1)}, bf16[2,1,1,2,16,1280]{5,4,3,2,1,0:T(8,128)(2,1)S(1)}, u32[]{:S(2)}, u32[]{:S(2)}) collective-permute-start(bf16[2,1,1,2,16,1280]{5,4,3,2,1,0:T(8,128)(2,1)S(1)} %add_convert_fusion.13), channel_id=1, source_target_pairs={{0,8},{2,10},{4,12},{6,14},{8,0},{10,2},{12,4},{14,6},{16,24},{18,... | collective-permute-start | bytes 491528 | tf_op jit(solution)/shard_map/ppermute | solution.py:560
  287.6 4.5 %collective-permute-start.29 = (bf16[2,1,1,1,16,1280]{5,4,3,2,1,0:T(8,128)(2,1)S(1)}, bf16[2,1,1,1,16,1280]{5,4,3,2,1,0:T(8,128)(2,1)S(1)}, u32[]{:S(2)}, u32[]{:S(2)}) collective-permute-start(bf16[2,1,1,1,16,1280]{5,4,3,2,1,0:T(8,128)(2,1)S(1)} %add_convert_fusion.20), channel_id=1, source_target_pairs={{0,1},{1,0},{2,3},{3,2},{4,5},{5,4},{6,7},{7,6},{8,9},{9,8},{10,11... | collective-permute-start | bytes 245768 | tf_op jit(solution)/shard_map/ppermute | solution.py:555
  293.0 7.4 %collective-permute-start.30 = (bf16[1,1,1,1,16,3584]{5,4,3,2,1,0:T(8,128)(2,1)S(1)}, bf16[1,1,1,1,16,3584]{5,4,3,2,1,0:T(8,128)(2,1)S(1)}, u32[]{:S(2)}, u32[]{:S(2)}) collective-permute-start(bf16[1,1,1,1,16,3584]{5,4,3,2,1,0:T(8,128)(2,1)S(1)} %pad_maximum_fusion.13), channel_id=1, source_target_pairs={{0,16},{2,18},{4,20},{6,22},{8,24},{10,26},{12,28},{14,30},{16,0},... | collective-permute-start | bytes 344072 | tf_op jit(solution)/shard_map/ppermute | solution.py:560
  (12 other events, 32.4 us)
where the time goes:
time: 310 us; the launch traced here: 304 us
  Pallas kernels  174 us (56%)
  other arithmetic  57.3 us (18%)
  starting transfers between devices  39.4 us (13%)
  waiting for transfers between devices  20.4 us (7%)
  local copies, waits for them, and re-layouts  10.6 us (3%)
    pallas_call x2, Pallas kernels, dense_steps(): pl.pallas_call(functools.partial(drop_first(dense_kernel), chunks=4, own=...  68.2 us
    pallas_call x2, Pallas kernels, group_backward(): pl.pallas_call(functools.partial(group_kernel, lengths=lengths, pairs=pai...  28.2 us
    convert_element_type x15, other arithmetic, send(): self.outgoing = self.total(half(1)).astype(bf16)  27.3 us
    pallas_call x3, Pallas kernels, attention_forward(): pl.pallas_call(functools.partial(forward_kernel, length=length, row=row,...  26.4 us
    ppermute x21, starting transfers between devices, swap_dp(): return lax.ppermute(v, 'dp', [(i, i ^ bit) for i in range(n)])  23.1 us
    ppermute x13, starting transfers between devices, swap_seq(): return lax.ppermute(v, 'seq', [(0, 1), (1, 0)])  16.3 us
    pallas_call x1, Pallas kernels, first_row_backward(): pl.pallas_call(functools.partial(first_row_kernel, length=length), grid=(...  15.4 us
    pallas_call x1, Pallas kernels, down_grad(): pl.pallas_call(down_grad_kernel, grid_spec=pltpu.PrefetchScalarGridSpec(n...  14.6 us
  transfers between devices with their start and end apart: 34, of which 7 were waited for; matrix products, arithmetic and copies ran while one was open for 19% of the time, Pallas kernels for 35%

commit v1 on v0

--- a/solution.py
+++ b/solution.py
@@ -21,7 +21,7 @@
 f32 = jnp.float32
 SDS = jax.ShapeDtypeStruct
 ANY = pl.BlockSpec(memory_space=pl.ANY)
-HINT = pl.CostEstimate(flops=1024, bytes_accessed=1024, transcendentals=0)
+LONG = pl.CostEstimate(flops=4 * 10**10, bytes_accessed=10**8, transcendentals=0)
 
 
 def dot(a, b):
@@ -160,7 +160,7 @@
         out_shape=[SDS((rows, D), bf16)] * 5 + [SDS((48, 512), f32), SDS((D, rows), bf16)],
         input_output_aliases={11 + i: i for i in range(7)} if chained else {},
         compiler_params=pltpu.CompilerParams(vmem_limit_bytes=VMEM_LIMIT),
-        cost_estimate=HINT,
+        cost_estimate=LONG,
         name=f"attend_{row}",
     )(*place, own, other, *weights, *extra)
 
@@ -212,7 +212,7 @@
     n2 = c2 * rs2
     result = (n2 * g2 + s2).astype(bf16)
     if own:
-        res_own[...] = result
+        res_own[0] = result
     else:
         size = result.shape[0]
 
@@ -262,8 +262,8 @@
         place = lambda i: 2 * i
         steps = mine
         up_specs = [pl.BlockSpec((1, tile, D), lambda i, s: (s[0] * mine + i, 0, 0))]
-        res_specs = [pl.BlockSpec((tile, D), lambda i, s: (i, 0))]
-        res_shapes = [SDS((mine * tile, D), bf16)]
+        res_specs = [pl.BlockSpec((1, tile, D), lambda i, s: (s[0] * mine + i, 0, 0))]
+        res_shapes = [SDS((2 * mine, tile, D), bf16)]
         extra, extra_specs, aliases = [], [], {}
     else:
         place = lambda i: jnp.minimum(2 * i + 1, 2 * mine)
@@ -297,7 +297,7 @@
         + [SDS((rows, D), f32), SDS((rows, D), bf16), SDS((16, D), f32)],
         input_output_aliases=aliases,
         compiler_params=pltpu.CompilerParams(vmem_limit_bytes=VMEM_LIMIT),
-        cost_estimate=HINT,
+        cost_estimate=LONG,
         name="dense_own" if own else "dense_rest",
     )(seq, ctx, x, *ups, *mats, *vecs, *extra)
 
@@ -332,7 +332,7 @@
         ),
         out_shape=[SDS((16, 16, 4608), bf16)] * 2,
         compiler_params=pltpu.CompilerParams(vmem_limit_bytes=VMEM_LIMIT),
-        cost_estimate=HINT,
+        cost_estimate=LONG,
         name="up_grad",
     )(me, nlow, dinn, dinn)
 
@@ -382,7 +382,7 @@
         ),
         out_shape=[SDS((16, 16, DOWN_WIDTH), bf16)] * 2,
         compiler_params=pltpu.CompilerParams(vmem_limit_bytes=VMEM_LIMIT),
-        cost_estimate=HINT,
+        cost_estimate=LONG,
         name="down_grad",
     )(me, act, dbr, ctx, datt, vec)
 
@@ -419,25 +419,30 @@
     backward_pairs(PAIRS, (s0, s1, s2, s3), 0, length, q_r, k_r, v_r, g_r, lse, 0, dq, dk, dv)
     ig = dr1[...] + dot_nt(dq[...], wq[...]) + dot_nt(dk[...], wk[...]) + dot_nt(dv[...], wv[...])
     ig = ig.astype(bf16)
-    ig_own[...] = ig[: length // 2]
+    ig_own[0] = ig[: length // 2]
     ig_other[...] = ig[length // 2 :]
 
 
 def first_row_backward(place, q, k, v, dctx, lse, dr1, weights, length):
-    tok = pl.BlockSpec((length, D), lambda i: (0, 0))
-    half = pl.BlockSpec((length // 2, D), lambda i: (0, 0))
-    full = pl.BlockSpec((D, D), lambda i: (0, 0))
+    tok = pl.BlockSpec((length, D), lambda i, *_: (0, 0))
+    half = length // 2
+    mine = place[3].shape[0] // 2
+    full = pl.BlockSpec((D, D), lambda i, *_: (0, 0))
     return pl.pallas_call(
         functools.partial(first_row_kernel, length=length),
-        grid=(1,),
-        in_specs=[pl.BlockSpec(memory_space=pltpu.SMEM)] * 4
-        + [tok] * 4
-        + [pl.BlockSpec((16, 512), lambda i: (0, 0)), tok]
-        + [full] * 3,
-        out_specs=[tok] * 3 + [half] * 2,
-        out_shape=[SDS((length, D), bf16)] * 3 + [SDS((length // 2, D), bf16)] * 2,
+        grid_spec=pltpu.PrefetchScalarGridSpec(
+            num_scalar_prefetch=4,
+            grid=(1,),
+            in_specs=[tok] * 4 + [pl.BlockSpec((16, 512), lambda i, *_: (0, 0)), tok] + [full] * 3,
+            out_specs=[tok] * 3
+            + [
+                pl.BlockSpec((1, half, D), lambda i, s, *_: (mine * s[0], 0, 0)),
+                pl.BlockSpec((half, D), lambda i, *_: (0, 0)),
+            ],
+        ),
+        out_shape=[SDS((length, D), bf16)] * 3 + [SDS((2 * mine, half, D), bf16), SDS((half, D), bf16)],
         compiler_params=pltpu.CompilerParams(vmem_limit_bytes=VMEM_LIMIT),
-        cost_estimate=HINT,
+        cost_estimate=LONG,
         name="back_first",
     )(*place, q, k, v, dctx, lse, dr1, *weights)
 
@@ -512,14 +517,14 @@
         + [SDS((16, 16, size), bf16)] * 2
         + [SDS((8, width), f32)],
         compiler_params=pltpu.CompilerParams(vmem_limit_bytes=VMEM_LIMIT),
-        cost_estimate=HINT,
+        cost_estimate=LONG,
         name=f"back_group_{first}",
     )(me, *place, q, k, v, dctx, lse, *before, xt, *extra)
 
 
-def input_grad_kernel(dr1, *rest, lengths, lanes):
+def input_grad_kernel(seq, dr1, *rest, lengths, lanes):
     groups = len(lanes)
-    blocks, (wq, wk, wv), (own, other) = rest[: 3 * groups], rest[3 * groups : 3 * groups + 3], rest[-2:]
+    blocks, (wq, wk, wv), (_, own, own_mid, other) = rest[: 3 * groups], rest[3 * groups : 3 * groups + 3], rest[-4:]
     long, mid = lengths
     n = slice(0, long + mid)
     total = dr1[...]
@@ -527,94 +532,205 @@
         for g, (low, high) in enumerate(lanes):
             total = total + dot_nt(blocks[3 * g + a][n, :], w[:, low:high])
     total = total.astype(bf16)
-    own[0 : long // 2, :] = total[0 : long // 2]
+    own[0] = total[0 : long // 2]
     other[0 : long // 2, :] = total[long // 2 : long]
-    own[long // 2 :, :] = total[long : long + mid // 2]
+    own_mid[...] = total[long : long + mid // 2]
     other[long // 2 :, :] = total[long + mid // 2 :]
 
 
-def input_grad(dr1, groups, lanes, weights, lengths):
+def input_grad(seq, dr1, groups, lanes, weights, lengths, before):
     long, mid = lengths
     flat = [a for g in groups for a in g]
-    whole = lambda a: pl.BlockSpec(a.shape, lambda i: (0, 0))
-    side = pl.BlockSpec(((long + mid) // 2, D), lambda i: (0, 0))
+    mine = before.shape[0] // 2
+    whole = lambda a: pl.BlockSpec(a.shape, lambda i, s: (0, 0))
+    ins = flat + list(weights)
     return pl.pallas_call(
         functools.partial(input_grad_kernel, lengths=lengths, lanes=lanes),
-        grid=(1,),
-        in_specs=[pl.BlockSpec((pl.Element(long + mid), pl.Element(D)), lambda i: (long, 0))]
-        + [whole(a) for a in flat + list(weights)],
-        out_specs=[side, side],
-        out_shape=[SDS(((long + mid) // 2, D), bf16)] * 2,
+        grid_spec=pltpu.PrefetchScalarGridSpec(
+            num_scalar_prefetch=1,
+            grid=(1,),
+            in_specs=[pl.BlockSpec((pl.Element(long + mid), pl.Element(D)), lambda i, s: (long, 0))]
+            + [whole(a) for a in ins]
+            + [ANY],
+            out_specs=[
+                pl.BlockSpec((1, long // 2, D), lambda i, s: (mine * s[0] + 1, 0, 0)),
+                pl.BlockSpec((mid // 2, D), lambda i, s: (0, 0)),
+                pl.BlockSpec(((long + mid) // 2, D), lambda i, s: (0, 0)),
+            ],
+        ),
+        out_shape=[SDS(before.shape, bf16), SDS((mid // 2, D), bf16), SDS(((long + mid) // 2, D), bf16)],
+        input_output_aliases={2 + len(ins): 0},
         compiler_params=pltpu.CompilerParams(vmem_limit_bytes=VMEM_LIMIT),
-        cost_estimate=HINT,
+        cost_estimate=LONG,
         name="input_grad",
-    )(dr1, *flat, *weights)
+    )(seq, dr1, *ins, before)
 
 
 def swap_seq(v):
     return lax.ppermute(v, "seq", [(0, 1), (1, 0)])
 
 
-def swap_dp(v, bit):
-    n = lax.axis_size("dp")
-    return lax.ppermute(v, "dp", [(i, i ^ bit) for i in range(n)])
-
-
-STEPS = {"x": (3, swap_seq), "y": (2, lambda v: swap_dp(v, 2)), "z": (1, lambda v: swap_dp(v, 4)), "w": (0, lambda v: swap_dp(v, 8))}
-
-
 def later(value, *others):
     return lax.optimization_barrier((value, *others))[0]
 
 
-class Halving:
+AXES = {"w": (0, 16), "z": (1, 8), "y": (2, 4), "x": (3, 1)}
+CORE = 2
+
+
+def swap(v, mask):
+    return lax.ppermute(v, ("dp", "seq"), [(i, i ^ mask) for i in range(BLOCKS)])
+
+
+class Payload:
     def __init__(self, groups, order):
         self.groups = groups
         self.order = order
 
-    def total(self, groups):
-        sums = [functools.reduce(lambda a, b: a + b, [p.astype(f32) for p in g]) for g in groups]
-        return jnp.concatenate(sums, axis=5)
-
-    def send(self):
-        axis, self.swap = STEPS[self.order[0]]
-        self.order = self.order[1:]
-        half = lambda i: [[lax.index_in_dim(p, i, axis, keepdims=True) for p in g] for g in self.groups]
-        self.outgoing = self.total(half(1)).astype(bf16)
-        self.groups = half(0)
+    def specs(self, bits):
+        todo = {AXES[a][0] for a in "".join(self.order)}
+        found = []
+        for width, arrays in self.groups:
+            for array, lane in arrays:
+                shape = tuple(2 if d in todo and d not in bits else 1 for d in range(4))
+                index = tuple(bits.get(d, 0) if array.shape[d] == 2 else 0 for d in range(4))
+                found.append((array, pl.BlockSpec(shape + (16, width), functools.partial(fixed, index + (0, lane)))))
+        return found
+
+    def receive(self, after=None):
+        for outgoing, mask in zip(self.outgoing, self.masks):
+            received = swap(outgoing, mask)
+            if after is not None:
+                received = later(received, after)
+            low = 0
+            for width, arrays in self.groups:
+                arrays.append((received, low // width))
+                low += width
         return self
 
-    def receive(self, after=None):
-        received = self.swap(self.outgoing)
-        if after is not None:
-            received = later(received, after)
+
+def fixed(index, *_):
+    return index
+
+
+def join(*sums):
+    return Payload([g for h in sums for g in h.groups], sums[0].order)
+
+
+def load_sum(refs):
+    total = refs[0][...].astype(f32)
+    for r in refs[1:]:
+        total = total + r[...].astype(f32)
+    return total
+
+
+def add_kernel(*refs, plan):
+    outs = refs[len(refs) - len(plan) :]
+    at = 0
+    for out, groups in zip(outs, plan):
         low = 0
-        for g in self.groups:
-            width = g[0].shape[5]
-            g.append(lax.slice_in_dim(received, low, low + width, axis=5))
+        for count, width in groups:
+            out[:, :, :, :, :, low : low + width] = load_sum(refs[at : at + count]).astype(bf16)
+            at += count
             low += width
-        return self
-
-    def result(self):
-        return self.total(self.groups).reshape(16, -1)
-
-
-def join(*sums):
-    return Halving([g for h in sums for g in h.groups], sums[0].order)
-
-
-def across_cores(pair, after, widths, orders):
-    send, keep = pair
-    received = swap_dp(send, 1)
-    if after is not None:
-        received = later(received, after)
+
+
+def send(*sums):
+    arrays, specs, plan, shapes = [], [], [], []
+    for h in sums:
+        step, rest = h.order[0], h.order[1:]
+        h.masks, h.count = [], 0
+        for which in range(1, 2 ** len(step)):
+            bits = {AXES[a][0]: which >> i & 1 for i, a in enumerate(step)}
+            h.masks.append(sum(AXES[a][1] for i, a in enumerate(step) if which >> i & 1))
+            found = h.specs(bits)
+            arrays += [f[0] for f in found]
+            specs += [f[1] for f in found]
+            plan.append([(len(g[1]), g[0]) for g in h.groups])
+            left = {AXES[a][0] for a in "".join(rest)}
+            shapes.append(tuple(2 if d in left else 1 for d in range(4)) + (16, sum(g[0] for g in h.groups)))
+            h.count += 1
+        h.order = rest
+    outs = pl.pallas_call(
+        functools.partial(add_kernel, plan=plan),
+        grid=(1,),
+        in_specs=specs,
+        out_specs=[pl.BlockSpec(n, functools.partial(fixed, (0,) * 6)) for n in shapes],
+        out_shape=[SDS(n, bf16) for n in shapes],
+        compiler_params=pltpu.CompilerParams(vmem_limit_bytes=VMEM_LIMIT),
+        cost_estimate=LONG,
+        name="add_parts",
+    )(*arrays)
+    at = 0
+    for h in sums:
+        h.outgoing = outs[at : at + h.count]
+        at += h.count
+
+
+def across_cores(pair, after, ranges, order):
+    leaving, keep = pair
+    received = later(swap(leaving, CORE), after)
     both = [v.reshape(2, 2, 2, 2, 16, -1) for v in (keep, received)]
-    parts = []
-    low = 0
-    for width, order in zip(widths, orders):
-        parts.append(Halving([[lax.slice_in_dim(v, low, low + width, axis=5) for v in both]], order).send())
-        low += width
-    return parts
+    return [
+        Payload([(width, [(v, lane) for v in both]) for width, lane in groups], axes) for axes, groups in zip(order, ranges)
+    ]
+
+
+def store_24(block, out, column, lanes=D):
+    for g in range(3):
+        for t in range(2):
+            piece = block[8 * t : 8 * t + 8, 384 * g : 384 * (g + 1)]
+            out[8 * g : 8 * g + 8, column + lanes // 2 * t : column + lanes // 2 * t + 384] = piece
+
+
+def last_dense_kernel(seq, *refs, plan):
+    (*ins, w_up, w_down, w_out, small) = refs
+    blocks = []
+    at = 0
+    for count in plan:
+        blocks.append(load_sum(ins[at : at + count])[0, 0, 0, 0])
+        at += count
+    up = jnp.concatenate(blocks[:2], axis=1)
+    down = jnp.concatenate(blocks[2:], axis=1)
+    for j in range(4):
+        store_24(up[:, 1152 * j : 1152 * (j + 1)], w_up, 384 * j, FF)
+    for g in range(6):
+        w_down[16 * g : 16 * (g + 1), :] = down[:, D * g : D * (g + 1)]
+    store_24(down[:, 4608:5760], w_out, 0)
+    small[...] = down[:, 5760:5888]
+
+
+def last_qkv_kernel(seq, *refs, plan):
+    (*ins, w_query, w_key, w_value, small, scr) = refs
+    blocks = []
+    at = 0
+    for count in plan:
+        blocks.append(load_sum(ins[at : at + count])[0, 0, 0, 0])
+        at += count
+    left, right, tail = blocks
+    for c in range(2):
+        store_24(left[:, 1152 * c : 1152 * (c + 1)], scr, D * c)
+    store_24(right, scr, 2 * D)
+    for a, out in enumerate((w_query, w_key, w_value)):
+        out[:, 0:512] = scr[:, 512 * a : 512 * (a + 1)]
+        out[:, 512:768] = scr[:, 2 * D + 256 * a : 2 * D + 256 * (a + 1)]
+    small[...] = tail
+
+
+def last_sums(kernel, seq, sums, shapes, scratch):
+    found = [f for h in sums for f in h.specs({})]
+    plan = [len(g[1]) for h in sums for g in h.groups]
+    return pl.pallas_call(
+        functools.partial(kernel, plan=plan),
+        grid=(1,),
+        in_specs=[pl.BlockSpec(memory_space=pltpu.SMEM)] + [f[1] for f in found],
+        out_specs=[pl.BlockSpec(n, functools.partial(fixed, (0, 0))) for n in shapes],
+        out_shape=[SDS(n, f32) for n in shapes],
+        scratch_shapes=[pltpu.VMEM(n, f32) for n in scratch],
+        compiler_params=pltpu.CompilerParams(vmem_limit_bytes=VMEM_LIMIT),
+        cost_estimate=LONG,
+        name="last_sums",
+    )(seq, *[f[0] for f in found])
 
 
 def rows_24(block):
@@ -636,16 +752,6 @@
     return [
         jnp.concatenate([left[:, 512 * a : 512 * (a + 1)], right[:, 256 * a : 256 * (a + 1)]], axis=1) for a in range(3)
     ]
-
-
-def finish_sums(up, down, qkv, me):
-    w_up = unpack_up(up)
-    w_down, w_out = unpack_down(down)
-    w_query, w_key, w_value = unpack_qkv(qkv)
-    vec = down[:8, 5760:5784]
-    b_up = lax.dynamic_slice(down, (8 + (me >> 3), 5760), (1, 96))[0]
-    bq, bv = qkv[1][0, 1152:1176], qkv[1][1, 1152:1176]
-    return w_query, bq, w_key, w_value, bv, w_out, vec, w_up, b_up, w_down
 
 
 def reduce_plain(up_pair, down_pair, qkv_pairs, vec, bg):
@@ -663,6 +769,49 @@
         scatter(qkv[0]), scatter(bg[0]), scatter(qkv[1]), scatter(qkv[2]), scatter(bg[1]), scatter(w_out),
         small, scatter(w_up), scatter(vec[8:12].reshape(FF)), scatter(w_down),
     )
+
+
+def give_back_kernel(seq, here, got, got_end, long_in, long, middle, short):
+    long[0] = got[...]
+
+    @pl.when(seq[0] == 0)
+    def _():
+        middle[0] = here[...]
+        short[0] = got_end[: short.shape[1], :]
+
+    @pl.when(seq[0] != 0)
+    def _():
+        middle[0] = got_end[...]
+        short[0] = here[: short.shape[1], :]
+
+
+def give_back(seq, long, here, got, short):
+    count, half, _ = long.shape
+    mid = here.shape[0]
+    other = lambda i, s: (count // 2 * (1 - s[0]) + i, 0, 0)
+    return pl.pallas_call(
+        give_back_kernel,
+        grid_spec=pltpu.PrefetchScalarGridSpec(
+            num_scalar_prefetch=1,
+            grid=(count // 2,),
+            in_specs=[
+                pl.BlockSpec((mid, D), lambda i, s: (0, 0)),
+                pl.BlockSpec((half, D), lambda i, s: (i, 0)),
+                pl.BlockSpec((mid, D), lambda i, s: (count // 2 * half // mid, 0)),
+                ANY,
+            ],
+            out_specs=[
+                pl.BlockSpec((1, half, D), other),
+                pl.BlockSpec((1, mid, D), lambda i, s: (0, 0, 0)),
+                pl.BlockSpec((1, short, D), lambda i, s: (0, 0, 0)),
+            ],
+        ),
+        out_shape=[SDS(long.shape, bf16), SDS((1, mid, D), bf16), SDS((1, short, D), bf16)],
+        input_output_aliases={4: 0},
+        compiler_params=pltpu.CompilerParams(vmem_limit_bytes=VMEM_LIMIT),
+        cost_estimate=LONG,
+        name="add_halves",
+    )(seq, here, got, got, long)
 
 
 def per_device(
@@ -719,72 +868,89 @@
     res_long, *before = dense(ups=[upstream_long], before=None)
     res_other, res_mid, act, dinn, nlow, dbr, datt, dr1, dctx, vec = dense(ups=[u_in, u_in, u_mid], before=before)
 
-    def give_back(own, got):
-        body = mine * half
-        here, there = (a[:body].reshape(mine, half, D) for a in (own, got))
-        long = jnp.concatenate([jnp.where(first, here, there), jnp.where(first, there, here)], axis=0)
-        low, middle = jnp.where(first, got[body:], own[body:]), jnp.where(first, own[body:], got[body:])
-        return low[None, :short], middle[None], long
-
-    body = half
-    first_got = swap_seq(res_other[:body])
     up_pair = up_grad(me_ref, nlow, dinn, tokens)
-    first_got = later(first_got, up_pair[0])
-    rest_got = swap_seq(later(res_other[body:], first_got))
+    part = half
+    res_got = [swap_seq(later(res_other[:part], up_pair[0]))]
     down_pair = down_grad(later(me_ref, up_pair[0]), act, dbr, ctx, datt, vec, tokens)
-
-    def ready(value, *sums):
-        return later(value, *[h.outgoing for h in sums])
-
-    after_sums = ready if fast else lambda value, *sums: value
-    at = lambda before, *sums: (after_sums(later(place[0], before), *sums), *place[1:])
-    up = down = wide_sum = []
+    res_got[0] = later(res_got[0], down_pair[0])
+    res_got.append(swap_seq(later(res_other[part:], res_got[0])))
+
+    def at(before, *sums, done=()):
+        going = [v for h in sums for v in h.outgoing] if fast else []
+        return (later(place[0], before, *going, *done), *place[1:])
+
+    up = down = all_sum = ()
     if fast:
-        up = across_cores(up_pair, down_pair[0], [2304, 2304], ["zxyw", "yxzw"])
-    *before, ig_own, ig_other = first_row_backward(
+        up = across_cores(
+            up_pair, down_pair[0], [[(2304, 0)], [(2304, 1)]], [["z", "x", "y", "w"], ["y", "x", "z", "w"]]
+        )
+        send(*up)
+    *before, ig_long, ig_other = first_row_backward(
         at(down_pair[0], *up), q, k, v, dctx, lse, dr1, qkv, 2 * half
     )
     if fast:
-        up = [h.receive(ig_own).send() for h in up]
-        down = across_cores(down_pair, ig_own, [3072, 2816], ["zyxw", "yzxw"])
-    rest_got = later(rest_got, ig_own)
+        for h in up:
+            h.receive(ig_other)
+        down = across_cores(
+            down_pair, ig_other, [[(2944, 0)], [(2944, 1)]], [["z", "y", "x", "w"], ["y", "z", "x", "w"]]
+        )
+        send(*up, *down)
+    res_got[1] = later(res_got[1], ig_other)
     later_rows = (2 * half, 2 * mid)
-    *wide, send, keep, bg = group_backward(
-        me_ref, at(ig_own, *up, *down), q, k, v, dctx, lse, before, xt, later_rows, 4, 0, None
+    *wide, leaving, keep, bg = group_backward(
+        me_ref, at(ig_other, *up, *down, done=res_got), q, k, v, dctx, lse, before, xt, later_rows, 4, 0, None
     )
-    wide_pair = (send, keep)
+    wide_pair = (leaving, keep)
     if fast:
-        up = [h.receive(bg).send() for h in up]
-        down = [h.receive(bg).send() for h in down]
+        for h in (*up, *down):
+            h.receive(bg)
+        send(*up, *down)
     ig_got = [swap_seq(later(ig_other, bg))]
-    *narrow, send, keep, bg_last = group_backward(
+    *narrow, leaving, keep, bg_last = group_backward(
         me_ref, at(bg, *up, *down), q, k, v, dctx, lse, before, xt, later_rows, 2, 4, bg
     )
-    narrow_pair = (send, keep)
+    narrow_pair = (leaving, keep)
     ig_got[0] = later(ig_got[0], bg_last)
     if fast:
-        up = [join(*[h.receive(bg_last) for h in up]).send()]
-        down = [join(*[h.receive(bg_last) for h in down]).send()]
-        wide_sum = across_cores(wide_pair, bg_last, [1152, 1152], ["yzxw", "zyxw"])
-    own, other = input_grad(
-        after_sums(later(dr1, ig_got[0]), *up, *down, *wide_sum), [wide, narrow], [(0, 512), (512, 768)], qkv, later_rows
+        for h in (*up, *down):
+            h.receive(bg_last)
+        up = (join(*up),)
+        down = (join(*down),)
+        send(*up, *down)
+        wide_sum = across_cores(wide_pair, bg_last, [[(2304, 0)]], [["yz", "xw"]])
+        narrow_sum = across_cores(narrow_pair, up[0].outgoing[0], [[(1152, 0), (128, 9)]], [["yz", "xw"]])
+        all_sum = (join(*wide_sum, *narrow_sum),)
+        send(*all_sum)
+    ig_long, ig_mid, ig_rest = input_grad(
+        at(bg_last, *up, *down, *all_sum)[0], later(dr1, ig_got[0]), [wide, narrow], [(0, 512), (512, 768)], qkv, later_rows, ig_long
     )
-    ig_got.append(swap_seq(other))
-    results = give_back(later(jnp.concatenate([res_long, res_mid], axis=0), own), jnp.concatenate([first_got, rest_got], axis=0))
+    ig_got.append(swap_seq(ig_rest))
     if fast:
-        up_block = up[0].receive(own).result()
-        down = down[0].receive(own).send()
-        wide_sum = [h.receive(own).send() for h in wide_sum]
-        (narrow_sum,) = across_cores(narrow_pair, own, [1280], ["yzxw"])
-        wide_sum = join(*[h.receive() for h in wide_sum]).send()
-        narrow_sum.receive().send()
-        down_block = down.receive().result()
-        narrow_sum.receive().send()
-        last = join(wide_sum.receive(), narrow_sum.receive()).send().receive().result()
-        done = finish_sums(up_block, down_block, [last[:, :2304], last[:, 2304:]], me)
+        up[0].receive(ig_rest)
+        down[0].receive(ig_rest)
+        send(*down)
+        all_sum[0].receive(down[0].outgoing[0])
+        send(*all_sum)
+        spare = all_sum[0].outgoing[0]
+        down[0].receive()
+        w_up, w_down, w_out, small = last_sums(
+            last_dense_kernel, later(place[0], spare), [*up, *down], [(24, FF), (96, D), (24, D), (16, 128)], []
+        )
+        all_sum[0].receive()
+        w_query, w_key, w_value, ends = last_sums(
+            last_qkv_kernel, place[0], all_sum, [(24, D)] * 3 + [(16, 128)], [(24, 3 * D)]
+        )
+        b_up = lax.dynamic_slice(small, (8 + (me >> 3), 0), (1, 96))[0]
+        done = w_query, ends[0, :24], w_key, w_value, ends[1, :24], w_out, small[:8, :24], w_up, b_up, w_down
     else:
+        spare = ig_rest
         done = reduce_plain(up_pair, down_pair, [wide_pair, narrow_pair], vec, jnp.concatenate([bg, bg_last], axis=1))
-    input_grads = give_back(jnp.concatenate([ig_own, own], axis=0), jnp.concatenate(ig_got, axis=0))
+    res_long, res_middle, res_short = give_back(
+        later(place[0], spare), res_long, res_mid, jnp.concatenate(res_got, axis=0), short
+    )
+    ig_long, ig_middle, ig_short = give_back(place[0], ig_long, ig_mid, jnp.concatenate(ig_got, axis=0), short)
+    results = (res_short, res_middle, res_long)
+    input_grads = (ig_short, ig_middle, ig_long)
     w_query, bq, w_key, w_value, bv, w_out, small, w_up, b_up, w_down = done
     return (
         *results, *input_grads,

time: 310 us -> 289 us (0.932)
  other arithmetic: 57.3 us -> 4.71 us
  Pallas kernels: 174 us -> 203 us
  local copies, waits for them, and re-layouts: 10.6 us -> 17.7 us
  starting transfers between devices: 39.4 us -> 33.4 us
    pallas_call x1 -> x12, Pallas kernels: 15.4 us -> 44.7 us  [the longest x7 20 us: send(): pl.pallas_call(functools.partial(add_kernel, plan=plan), grid=(1,), in_sp...]
    convert_element_type x15 -> x0, other arithmetic: 27.3 us -> none  [send(): self.outgoing = self.total(half(1)).astype(bf16)]
    another operation x8 -> x0, other arithmetic: 8.89 us -> none
    unnamed x52 -> x66, local copies, waits for them, and re-layouts: 3.08 us -> 11 us
    ppermute x13 -> x8, starting transfers between devices: 16.3 us -> 9.79 us  [swap_seq(): return lax.ppermute(v, 'seq', [(0, 1), (1, 0)])]
    add x5 -> x0, other arithmetic: 5.46 us -> none  [total(): a + b]
    broadcast_in_dim x4 -> x0, other arithmetic: 4.59 us -> none  [give_back(): return (low[None, :short], middle[None], long)]
    concatenate x11 -> x2, other arithmetic: 7.01 us -> 3.1 us  [the longest x1 2.08 us: per_device(): jnp.concatenate(ig_got, axis=0)]
  transfers between devices with their start and end apart: 34 -> 31, of which waited for: 7 -> 3; matrix products, arithmetic and copies ran while one was open for 19% -> 2% of each run, Pallas kernels for 35% -> 46%
where the time goes in v1:
time: 289 us; the launch traced here: 284 us
  Pallas kernels  203 us (70%)
  starting transfers between devices  33.4 us (12%)
  waiting for transfers between devices  22.4 us (8%)
  local copies, waits for them, and re-layouts  17.7 us (6%)
  other arithmetic  4.71 us (2%)
    pallas_call x2, Pallas kernels, dense_steps(): pl.pallas_call(functools.partial(drop_first(dense_kernel), chunks=4, own=...  68.1 us
    pallas_call x2, Pallas kernels, group_backward(): pl.pallas_call(functools.partial(group_kernel, lengths=lengths, pairs=pai...  28.5 us
    pallas_call x3, Pallas kernels, attention_forward(): pl.pallas_call(functools.partial(forward_kernel, length=length, row=row,...  26.4 us
    ppermute x23, starting transfers between devices, swap(): lax.ppermute(v, ('dp', 'seq'), [(i, i ^ mask) for i in range(BLOCKS)])  23.7 us
    pallas_call x7, Pallas kernels, send(): pl.pallas_call(functools.partial(add_kernel, plan=plan), grid=(1,), in_sp...  20 us
    pallas_call x1, Pallas kernels, first_row_backward(): pl.pallas_call(functools.partial(first_row_kernel, length=length), grid_s...  15.9 us
    pallas_call x1, Pallas kernels, down_grad(): pl.pallas_call(down_grad_kernel, grid_spec=pltpu.PrefetchScalarGridSpec(n...  14.4 us
    pallas_call x1, Pallas kernels, up_grad(): pl.pallas_call(up_grad_kernel, grid_spec=pltpu.PrefetchScalarGridSpec(num...  13.3 us
  transfers between devices with their start and end apart: 31, of which 3 were waited for; matrix products, arithmetic and copies ran while one was open for 2% of the time, Pallas kernels for 46%

profile of v1, /device:TPU:0, one launch (start us, length us, event | category | flops | bytes accessed | tf_op | source)
XLA Modules:
  0.0 284.1 jit_solution(15208179438171381230)
XLA Ops:
  0.7 2.7 dynamic-slice_bitcast_fusion
  3.4 2.9 %collective-permute-start.1 = (bf16[256,768]{1,0:T(8,128)(2,1)}, bf16[256,768]{1,0:T(8,128)(2,1)}, u32[]{:S(2)}, u32[]{:S(2)}) collective-permute-start(bf16[256,768]{1,0:T(8,128)(2,1)} %get-tuple-element.279), channel_id=1, source_target_pairs={{0,1},{1,0},{2,3},{3,2},{4,5},{5,4},{6,7},{7,6},{8,9},{9,8},{10,11... | collective-permute-start | bytes 1179656 | tf_op jit(solution)/shard_map/ppermute | solution.py:570
  7.1 2.0 collective-permute-start
  11.3 9.3 %collective-permute-done.2.xr = bf16[128,768]{1,0:T(8,128)(2,1)S(1)} collective-permute-done((bf16[128,768]{1,0:T(8,128)(2,1)}, bf16[128,768]{1,0:T(8,128)(2,1)S(1)}, u32[]{:S(2)}, u32[]{:S(2)}) %collective-permute-start.2) | collective-permute-done | bytes 196640 | tf_op jit(solution)/shard_map/ppermute | solution.py:570
  21.4 6.3 %attend_2.1 = (bf16[1536,768]{1,0:T(8,128)(2,1)}, bf16[1536,768]{1,0:T(8,128)(2,1)}, bf16[1536,768]{1,0:T(8,128)(2,1)}, bf16[1536,768]{1,0:T(8,128)(2,1)}, bf16[...) custom-call(s32[1]{0:T(128)} %bitcast.s0._.seq, s32[1]{0:T(128)S(6)} %copy.93.s1, ...), custom_call_target="tpu_custom_call" | custom-call | flops 40000000000 | bytes 100000000 | tf_op jit(solution)/shard_map/attend_2/pallas_call | solution.py:152
  27.7 9.9 %attend_0.1 = (bf16[1536,768]{1,0:T(8,128)(2,1)}, bf16[1536,768]{1,0:T(8,128)(2,1)}, bf16[1536,768]{1,0:T(8,128)(2,1)}, bf16[1536,768]{1,0:T(8,128)(2,1)}, bf16[...) custom-call(s32[1]{0:T(128)} %bitcast.s0._.seq, ...), custom_call_target="tpu_custom_call", output_to_operand_aliasing={{0}: (11, {}), {1}: (12, {}), {2}: (13, {}), {3}: (14, {}),... | custom-call | flops 40000000000 | bytes 100000000 | tf_op jit(solution)/shard_map/attend_0/pallas_call | solution.py:152
  38.4 10.1 %attend_1.1 = (bf16[1536,768]{1,0:T(8,128)(2,1)}, bf16[1536,768]{1,0:T(8,128)(2,1)}, bf16[1536,768]{1,0:T(8,128)(2,1)}, bf16[1536,768]{1,0:T(8,128)(2,1)}, bf16[...) custom-call(s32[1]{0:T(128)} %bitcast.s0._.seq, ...), custom_call_target="tpu_custom_call", output_to_operand_aliasing={{0}: (11, {}), {1}: (12, {}), {2}: (13, {}), {3}: (14, {}),... | custom-call | flops 40000000000 | bytes 100000000 | tf_op jit(solution)/shard_map/attend_1/pallas_call | solution.py:152
  48.5 2.1 collective-permute-start.3
  50.6 24.4 %dense_own.1 = (bf16[4,256,768]{2,1,0:T(8,128)(2,1)}, bf16[1280,3072]{1,0:T(8,128)(2,1)}, bf16[1280,3072]{1,0:T(8,128)(2,1)}, bf16[1280,768]{1,0:T(8,128)(2,1)},...) custom-call(s32[1]{0:T(128)} %bitcast.s0._.seq, ...), custom_call_target="tpu_custom_call" | custom-call | flops 40000000000 | bytes 100000000 | tf_op jit(solution)/shard_map/dense_own/pallas_call | solution.py:285
  75.0 0.9 copy-done.10
  76.0 43.7 %dense_rest.1 = (bf16[640,768]{1,0:T(8,128)(2,1)}, bf16[128,768]{1,0:T(8,128)(2,1)}, bf16[1280,3072]{1,0:T(8,128)(2,1)}, bf16[1280,3072]{1,0:T(8,128)(2,1)}, bf1...) custom-call(s32[1]{0:T(128)} %bitcast.s0._.seq, ...), custom_call_target="tpu_custom_call", output_to_operand_aliasing={{2}: (17, {}), {3}: (18, {}), {4}: (19, {}), {5}: (20, {}),... | custom-call | flops 40000000000 | bytes 100000000 | tf_op jit(solution)/shard_map/dense_rest/pallas_call | solution.py:285
  119.7 13.3 %up_grad.1 = (bf16[16,16,4608]{2,1,0:T(8,128)(2,1)}, bf16[16,16,4608]{2,1,0:T(8,128)(2,1)}) custom-call(s32[1]{0:T(128)} %bitcast.1.me, bf16[1280,768]{1,0:T(8,128)(2,1)} %get-tuple-element.176.nlow, bf16[1280,3072]{1,0:T(8,128)(2,1)} %get-tuple-element.177.left.right, bf16[1280,3072]{1,0:T(8,128)(2,1)} %get-tuple-element.177.left.right), custom_call_target="tpu_custom_call" | custom-call | flops 40000000000 | bytes 100000000 | tf_op jit(solution)/shard_map/up_grad/pallas_call | solution.py:320
  133.1 14.4 %down_grad.1 = (bf16[16,16,5888]{2,1,0:T(8,128)(2,1)}, bf16[16,16,5888]{2,1,0:T(8,128)(2,1)}) custom-call(s32[1]{0:T(128)} %bitcast.1.me, bf16[1280,3072]{1,0:T(8,128)(2,1)} %get-tuple-element.180.act, bf16[1280,768]{1,0:T(8,128)(2,1)} %get-tuple-element.181.dbr, bf16[1536,768]{1,0:T(8,128)(2,1)} %get-tuple-element.164.refs_0_.ctx, ...), custom_call_target="tpu_custom_call" | custom-call | flops 40000000000 | bytes 100000000 | tf_op jit(solution)/shard_map/down_grad/pallas_call | solution.py:368
  148.1 1.7 collective-permute-start.9
  149.8 2.7 add_parts.7
  152.6 1.5 collective-permute-start.6
  154.1 1.6 collective-permute-start.5
  155.7 15.9 %back_first.1 = (bf16[512,768]{1,0:T(8,128)(2,1)}, bf16[512,768]{1,0:T(8,128)(2,1)}, bf16[512,768]{1,0:T(8,128)(2,1)}, bf16[4,256,768]{2,1,0:T(8,128)(2,1)}, bf16[256,768]{1,0:T(8,128)(2,1)}) custom-call(s32[1]{0:T(128)} %bitcast.s0._.seq, s32[1]{0:T(128)S(6)} %copy.93.s1, s32[1]{0:T(128)S(6)} %copy.94.s2, s32[4]{0:T(128)} %s3.11, ...), custom_call_target="tpu_custom_call" | custom-call | flops 40000000000 | bytes 100000000 | tf_op jit(solution)/shard_map/back_first/pallas_call | solution.py:431
  171.6 1.0 pad_maximum_fusion.1.got.got_end
  173.6 3.9 %add_parts.8 = (bf16[2,1,2,1,16,2304]{5,4,3,2,1,0:T(8,128)(2,1)}, bf16[2,2,1,1,16,2304]{5,4,3,2,1,0:T(8,128)(2,1)}, bf16[2,1,2,2,16,2944]{5,4,3,2,1,0:T(8,128)(2,1)}, bf16[2,2,1,2,16,2944]{5,4,3,2,1,0:T(8,128)(2,1)}) custom-call(bf16[2,2,2,2,16,4608]{5,4,3,2,1,0:T(8,128)(2,1)} %bitcast.81, ...), custom_call_target="tpu_custom_call" | custom-call | flops 40000000000 | bytes 100000000 | tf_op jit(solution)/shard_map/add_parts/pallas_call | solution.py:654
  178.8 1.7 collective-permute-start.11
  180.5 17.4 %back_group_0.1 = (bf16[1024,512]{1,0:T(8,128)(2,1)}, bf16[1024,512]{1,0:T(8,128)(2,1)}, bf16[1024,512]{1,0:T(8,128)(2,1)}, bf16[16,16,2304]{2,1,0:T(8,128)(2,1)...) custom-call(s32[1]{0:T(128)} %bitcast.1.me, s32[1]{0:T(128)} %bitcast.s0._.seq, s32[1]{0:T(128)S(6)} %copy.93.s1, ...), custom_call_target="tpu_custom_call" | custom-call | flops 40000000000 | bytes 100000000 | tf_op jit(solution)/shard_map/back_group_0/pallas_call | solution.py:503
  199.5 0.9 copy-done.12
  200.4 3.2 %add_parts.9 = (bf16[2,1,1,1,16,2304]{5,4,3,2,1,0:T(8,128)(2,1)}, bf16[2,1,1,1,16,2304]{5,4,3,2,1,0:T(8,128)(2,1)}, bf16[2,1,1,2,16,2944]{5,4,3,2,1,0:T(8,128)(2,1)}, bf16[2,1,1,2,16,2944]{5,4,3,2,1,0:T(8,128)(2,1)}) custom-call(bf16[2,2,2,2,16,4608]{5,4,3,2,1,0:T(8,128)(2,1)} %bitcast.83, ...), custom_call_target="tpu_custom_call" | custom-call | flops 40000000000 | bytes 100000000 | tf_op jit(solution)/shard_map/add_parts/pallas_call | solution.py:654
  203.6 1.7 collective-permute-start.19
  205.3 1.5 collective-permute-start.18
  207.7 11.0 %back_group_4.1 = (bf16[1024,256]{1,0:T(8,128)(2,1)}, bf16[1024,256]{1,0:T(8,128)(2,1)}, bf16[1024,256]{1,0:T(8,128)(2,1)}, bf16[16,16,1280]{2,1,0:T(8,128)(2,1)...) custom-call(s32[1]{0:T(128)} %bitcast.1.me, s32[1]{0:T(128)} %bitcast.s0._.seq, s32[1]{0:T(128)S(6)} %copy.93.s1, ...), custom_call_target="tpu_custom_call" | custom-call | flops 40000000000 | bytes 100000000 | tf_op jit(solution)/shard_map/back_group_4/pallas_call | solution.py:503
  220.1 2.7 add_parts.10
  222.8 2.7 collective-permute-start.29
  225.5 1.5 collective-permute-start.21
  227.1 1.0 copy-done.8
  228.3 2.9 %add_parts.11 = (bf16[2,1,1,2,16,3584]{5,4,3,2,1,0:T(8,128)(2,1)}, bf16[2,1,1,2,16,3584]{5,4,3,2,1,0:T(8,128)(2,1)}, bf16[2,1,1,2,16,3584]{5,4,3,2,1,0:T(8,128)(2,1)}) custom-call(bf16[2,2,2,2,16,2304]{5,4,3,2,1,0:T(8,128)(2,1)} %bitcast.89, bf16[2,2,2,2,16,2304]{5,4,3,2,1,0:T(8,128)(2,1)} %bitcast.48, bf16[2,2,2,2,16,1280]{5,4,3,2,1,0:T(8,128)(2,1)} %bitcast.96, ...), custom_call_target="tpu_custom_call" | custom-call | flops 40000000000 | bytes 100000000 | tf_op jit(solution)/shard_map/add_parts/pallas_call | solution.py:654
  231.2 2.5 collective-permute-start.24
  234.7 7.9 %input_grad.1 = (bf16[4,256,768]{2,1,0:T(8,128)(2,1)}, bf16[128,768]{1,0:T(8,128)(2,1)}, bf16[384,768]{1,0:T(8,128)(2,1)}) custom-call(s32[1]{0:T(128)} %bitcast.s0._.seq, f32[1536,768]{1,0:T(8,128)} %get-tuple-element.243.dr1, bf16[1024,512]{1,0:T(8,128)(2,1)} %get-tuple-element.244.rest_0_, ...), custom_call_target="tpu_custom_call", output_to_operand_aliasing={{0}: (11, {})} | custom-call | flops 40000000000 | bytes 100000000 | tf_op jit(solution)/shard_map/input_grad/pallas_call | solution.py:547
  244.0 2.0 add_parts.12
  246.3 12.0 %collective-permute-done.23.refs_3_.refs_8_.refs_13_.refs_18_.refs_23_.refs_28_.refs_33_.refs_38_.refs_43_.refs_11_.refs_19_ = bf16[2,1,1,2,16,3584]{5,4,3,2,1,0:T(8,128)(2,1)S(1)} collective-permute-done((bf16[2,1,1,2,16,3584]{5,4,3,2,1,0:T(8,128)(2,1)}, bf16[2,1,1,2,16,3584]{5,4,3,2,1,0:T(8,128)(2,1)S(1)}, u32[]{:S(2)}, u32[]{:S(2)}) %collective-permute-start.23) | collective-permute-done | bytes 458784 | tf_op jit(solution)/shard_map/ppermute | solution.py:582
  259.8 2.4 add_parts.13
  262.8 1.2 collective-permute-start.27
  264.0 2.7 collective-permute-start.28
  266.7 2.2 add_halves.2
  269.6 2.5 last_sums.3
  272.1 1.4 slice_bitcast_fusion
  273.5 1.2 fusion
  274.8 1.0 collective-permute-done.28.refs_7_.refs_15_.refs_23_
  276.4 2.0 last_sums.2
  278.4 1.3 slice_bitcast_fusion.6
  279.7 2.1 pad_maximum_fusion.2.got.got_end
  281.7 2.2 add_halves.3
  (114 shorter events, 16.0 us)
Async XLA Ops:
  0.7 5.7 %copy-start.6 = (bf16[1,64,768]{2,1,0:T(8,128)(2,1)S(1)}, bf16[1,64,768]{2,1,0:T(8,128)(2,1)}, u32[]{:S(2)}) copy-start(bf16[1,64,768]{2,1,0:T(8,128)(2,1)} %param.24) | copy-start | bytes 294916
  0.7 5.7 %copy-start.4 = (bf16[1,128,768]{2,1,0:T(8,128)(2,1)S(1)}, bf16[1,128,768]{2,1,0:T(8,128)(2,1)}, u32[]{:S(2)}) copy-start(bf16[1,128,768]{2,1,0:T(8,128)(2,1)} %param.25) | copy-start | bytes 589828
  0.7 8.5 %copy-start.7 = (bf16[1,64,768]{2,1,0:T(8,128)(2,1)S(1)}, bf16[1,64,768]{2,1,0:T(8,128)(2,1)}, u32[]{:S(2)}) copy-start(bf16[1,64,768]{2,1,0:T(8,128)(2,1)} %param.45) | copy-start | bytes 294916
  0.7 8.5 %copy-start.5 = (bf16[1,128,768]{2,1,0:T(8,128)(2,1)S(1)}, bf16[1,128,768]{2,1,0:T(8,128)(2,1)}, u32[]{:S(2)}) copy-start(bf16[1,128,768]{2,1,0:T(8,128)(2,1)} %param.46) | copy-start | bytes 589828
  0.7 9.2 %copy-start.1 = (bf16[4,256,768]{2,1,0:T(8,128)(2,1)S(1)}, bf16[4,256,768]{2,1,0:T(8,128)(2,1)}, u32[]{:S(2)}) copy-start(bf16[4,256,768]{2,1,0:T(8,128)(2,1)} %refs_2_.1) | copy-start | bytes 4718596
  3.4 24.3 %collective-permute-start.1 = (bf16[256,768]{1,0:T(8,128)(2,1)}, bf16[256,768]{1,0:T(8,128)(2,1)}, u32[]{:S(2)}, u32[]{:S(2)}) collective-permute-start(bf16[256,768]{1,0:T(8,128)(2,1)} %get-tuple-element.279), channel_id=1, source_target_pairs={{0,1},{1,0},{2,3},{3,2},{4,5},{5,4},{6,7},{7,6},{8,9},{9,8},{10,11... | collective-permute-start | bytes 1179656 | tf_op jit(solution)/shard_map/ppermute | solution.py:570
  7.1 13.6 %collective-permute-start.2 = (bf16[128,768]{1,0:T(8,128)(2,1)}, bf16[128,768]{1,0:T(8,128)(2,1)S(1)}, u32[]{:S(2)}, u32[]{:S(2)}) collective-permute-start(bf16[128,768]{1,0:T(8,128)(2,1)} %get-tuple-element.285), channel_id=1, source_target_pairs={{0,1},{1,0},{2,3},{3,2},{4,5},{5,4},{6,7},{7,6},{8,9},{9,8},{10,11... | collective-permute-start | bytes 589832 | tf_op jit(solution)/shard_map/ppermute | solution.py:570
  7.1 30.5 %collective-permute-start = (bf16[256,768]{1,0:T(8,128)(2,1)}, bf16[256,768]{1,0:T(8,128)(2,1)S(1)}, u32[]{:S(2)}, u32[]{:S(2)}) collective-permute-start(bf16[256,768]{1,0:T(8,128)(2,1)} %get-tuple-element.280), channel_id=1, source_target_pairs={{0,1},{1,0},{2,3},{3,2},{4,5},{5,4},{6,7},{7,6},{8,9},{9,8},{10,11... | collective-permute-start | bytes 1179656 | tf_op jit(solution)/shard_map/ppermute | solution.py:570
  48.5 26.5 %collective-permute-start.3 = (bf16[640,768]{1,0:T(8,128)(2,1)S(1)}, bf16[640,768]{1,0:T(8,128)(2,1)S(1)}, u32[]{:S(2)}, u32[]{:S(2)}) collective-permute-start(bf16[640,768]{1,0:T(8,128)(2,1)S(1)} %pad_maximum_fusion), channel_id=1, source_target_pairs={{0,1},{1,0},{2,3},{3,2},{4,5},{5,4},{6,7},{7,6},{8,9},{9,8},{10,11... | collective-permute-start | bytes 2949128 | tf_op jit(solution)/shard_map/ppermute | solution.py:570
  119.7 13.3 %copy-start = (bf16[640,768]{1,0:T(8,128)(2,1)S(1)}, bf16[640,768]{1,0:T(8,128)(2,1)}, u32[]{:S(2)}) copy-start(bf16[640,768]{1,0:T(8,128)(2,1)} %get-tuple-element.204) | copy-start | bytes 2949124
  133.0 16.8 %collective-permute-start.4 = (bf16[16,16,4608]{2,1,0:T(8,128)(2,1)}, bf16[16,16,4608]{2,1,0:T(8,128)(2,1)}, u32[]{:S(2)}, u32[]{:S(2)}) collective-permute-start(bf16[16,16,4608]{2,1,0:T(8,128)(2,1)} %get-tuple-element.178), channel_id=1, source_target_pairs={{0,2},{1,3},{2,0},{3,1},{4,6},{5,7},{6,4},{7,5},{8,10},{9,11},{10,... | collective-permute-start | bytes 7077896 | tf_op jit(solution)/shard_map/ppermute | solution.py:582
  133.0 15.1 %collective-permute-start.8 = (bf16[256,768]{1,0:T(8,128)(2,1)S(1)}, bf16[256,768]{1,0:T(8,128)(2,1)S(1)}, u32[]{:S(2)}, u32[]{:S(2)}) collective-permute-start(bf16[256,768]{1,0:T(8,128)(2,1)S(1)} %slice.53), channel_id=1, source_target_pairs={{0,1},{1,0},{2,3},{3,2},{4,5},{5,4},{6,7},{7,6},{8,9},{9,8},{10,11... | collective-permute-start | bytes 1179656 | tf_op jit(solution)/shard_map/ppermute | solution.py:570
  147.5 25.1 %collective-permute-start.7 = (bf16[16,16,5888]{2,1,0:T(8,128)(2,1)}, bf16[16,16,5888]{2,1,0:T(8,128)(2,1)}, u32[]{:S(2)}, u32[]{:S(2)}) collective-permute-start(bf16[16,16,5888]{2,1,0:T(8,128)(2,1)} %get-tuple-element.184), channel_id=1, source_target_pairs={{0,2},{1,3},{2,0},{3,1},{4,6},{5,7},{6,4},{7,5},{8,10},{9,11},{10,... | collective-permute-start | bytes 9043976 | tf_op jit(solution)/shard_map/ppermute | solution.py:582
  148.1 23.5 %collective-permute-start.9 = (bf16[384,768]{1,0:T(8,128)(2,1)S(1)}, bf16[384,768]{1,0:T(8,128)(2,1)S(1)}, u32[]{:S(2)}, u32[]{:S(2)}) collective-permute-start(bf16[384,768]{1,0:T(8,128)(2,1)S(1)} %slice.54), channel_id=1, source_target_pairs={{0,1},{1,0},{2,3},{3,2},{4,5},{5,4},{6,7},{7,6},{8,9},{9,8},{10,11... | collective-permute-start | bytes 1769480 | tf_op jit(solution)/shard_map/ppermute | solution.py:570
  152.6 20.1 %collective-permute-start.6 = (bf16[2,2,1,2,16,2304]{5,4,3,2,1,0:T(8,128)(2,1)}, bf16[2,2,1,2,16,2304]{5,4,3,2,1,0:T(8,128)(2,1)S(1)}, u32[]{:S(2)}, u32[]{:S(2)}) collective-permute-start(bf16[2,2,1,2,16,2304]{5,4,3,2,1,0:T(8,128)(2,1)} %get-tuple-element.188), channel_id=1, source_target_pairs={{0,4},{1,5},{2,6},{3,7},{4,0},{5,1},{6,2},{7,3},{8,12},{9,13},{10,... | collective-permute-start | bytes 1769480 | tf_op jit(solution)/shard_map/ppermute | solution.py:582
  154.1 18.5 %collective-permute-start.5 = (bf16[2,1,2,2,16,2304]{5,4,3,2,1,0:T(8,128)(2,1)}, bf16[2,1,2,2,16,2304]{5,4,3,2,1,0:T(8,128)(2,1)S(1)}, u32[]{:S(2)}, u32[]{:S(2)}) collective-permute-start(bf16[2,1,2,2,16,2304]{5,4,3,2,1,0:T(8,128)(2,1)} %get-tuple-element.187), channel_id=1, source_target_pairs={{0,8},{1,9},{2,10},{3,11},{4,12},{5,13},{6,14},{7,15},{8,0},{9,1},... | collective-permute-start | bytes 1769480 | tf_op jit(solution)/shard_map/ppermute | solution.py:582
  172.6 1.0 copy-start.15
  177.5 20.9 %collective-permute-start.14 = (bf16[2,2,1,2,16,2944]{5,4,3,2,1,0:T(8,128)(2,1)}, bf16[2,2,1,2,16,2944]{5,4,3,2,1,0:T(8,128)(2,1)S(1)}, u32[]{:S(2)}, u32[]{:S(2)}) collective-permute-start(bf16[2,2,1,2,16,2944]{5,4,3,2,1,0:T(8,128)(2,1)} %get-tuple-element.203), channel_id=1, source_target_pairs={{0,4},{1,5},{2,6},{3,7},{4,0},{5,1},{6,2},{7,3},{8,12},{9,13},{10,... | collective-permute-start | bytes 2261000 | tf_op jit(solution)/shard_map/ppermute | solution.py:582
  178.0 20.4 %collective-permute-start.13 = (bf16[2,1,2,2,16,2944]{5,4,3,2,1,0:T(8,128)(2,1)}, bf16[2,1,2,2,16,2944]{5,4,3,2,1,0:T(8,128)(2,1)S(1)}, u32[]{:S(2)}, u32[]{:S(2)}) collective-permute-start(bf16[2,1,2,2,16,2944]{5,4,3,2,1,0:T(8,128)(2,1)} %get-tuple-element.202), channel_id=1, source_target_pairs={{0,8},{1,9},{2,10},{3,11},{4,12},{5,13},{6,14},{7,15},{8,0},{9,1},... | collective-permute-start | bytes 2261000 | tf_op jit(solution)/shard_map/ppermute | solution.py:582
  178.5 19.9 %collective-permute-start.12 = (bf16[2,2,1,1,16,2304]{5,4,3,2,1,0:T(8,128)(2,1)}, bf16[2,2,1,1,16,2304]{5,4,3,2,1,0:T(8,128)(2,1)S(1)}, u32[]{:S(2)}, u32[]{:S(2)}) collective-permute-start(bf16[2,2,1,1,16,2304]{5,4,3,2,1,0:T(8,128)(2,1)} %get-tuple-element.201), channel_id=1, source_target_pairs={{0,1},{1,0},{2,3},{3,2},{4,5},{5,4},{6,7},{7,6},{8,9},{9,8},{10,11... | collective-permute-start | bytes 884744 | tf_op jit(solution)/shard_map/ppermute | solution.py:582
  178.8 19.6 %collective-permute-start.11 = (bf16[2,1,2,1,16,2304]{5,4,3,2,1,0:T(8,128)(2,1)}, bf16[2,1,2,1,16,2304]{5,4,3,2,1,0:T(8,128)(2,1)S(1)}, u32[]{:S(2)}, u32[]{:S(2)}) collective-permute-start(bf16[2,1,2,1,16,2304]{5,4,3,2,1,0:T(8,128)(2,1)} %get-tuple-element.200), channel_id=1, source_target_pairs={{0,1},{1,0},{2,3},{3,2},{4,5},{5,4},{6,7},{7,6},{8,9},{9,8},{10,11... | collective-permute-start | bytes 884744 | tf_op jit(solution)/shard_map/ppermute | solution.py:582
  180.5 17.5 %copy-start.19 = (bf16[256,768]{1,0:T(8,128)(2,1)S(1)}, bf16[256,768]{1,0:T(8,128)(2,1)}, u32[]{:S(2)}) copy-start(bf16[256,768]{1,0:T(8,128)(2,1)} %get-tuple-element.241) | copy-start | bytes 1179652
  198.0 20.7 %collective-permute-start.22 = (bf16[256,768]{1,0:T(8,128)(2,1)S(1)}, bf16[256,768]{1,0:T(8,128)(2,1)S(1)}, u32[]{:S(2)}, u32[]{:S(2)}) collective-permute-start(bf16[256,768]{1,0:T(8,128)(2,1)S(1)} %copy-done.19), channel_id=1, source_target_pairs={{0,1},{1,0},{2,3},{3,2},{4,5},{5,4},{6,7},{7,6},{8,9},{9,8},{10,11... | collective-permute-start | bytes 1179656 | tf_op jit(solution)/shard_map/ppermute | solution.py:570
  198.4 1.1 copy-start.11
  203.6 15.7 %collective-permute-start.19 = (bf16[2,1,1,2,16,2944]{5,4,3,2,1,0:T(8,128)(2,1)}, bf16[2,1,1,2,16,2944]{5,4,3,2,1,0:T(8,128)(2,1)S(1)}, u32[]{:S(2)}, u32[]{:S(2)}) collective-permute-start(bf16[2,1,1,2,16,2944]{5,4,3,2,1,0:T(8,128)(2,1)} %get-tuple-element.224), channel_id=1, source_target_pairs={{0,8},{1,9},{2,10},{3,11},{4,12},{5,13},{6,14},{7,15},{8,0},{9,1},... | collective-permute-start | bytes 1130504 | tf_op jit(solution)/shard_map/ppermute | solution.py:582
  205.3 14.0 %collective-permute-start.18 = (bf16[2,1,1,2,16,2944]{5,4,3,2,1,0:T(8,128)(2,1)}, bf16[2,1,1,2,16,2944]{5,4,3,2,1,0:T(8,128)(2,1)}, u32[]{:S(2)}, u32[]{:S(2)}) collective-permute-start(bf16[2,1,1,2,16,2944]{5,4,3,2,1,0:T(8,128)(2,1)} %get-tuple-element.223), channel_id=1, source_target_pairs={{0,4},{1,5},{2,6},{3,7},{4,0},{5,1},{6,2},{7,3},{8,12},{9,13},{10,... | collective-permute-start | bytes 1130504 | tf_op jit(solution)/shard_map/ppermute | solution.py:582
  206.9 12.0 %collective-permute-start.17 = (bf16[2,1,1,1,16,2304]{5,4,3,2,1,0:T(8,128)(2,1)}, bf16[2,1,1,1,16,2304]{5,4,3,2,1,0:T(8,128)(2,1)S(1)}, u32[]{:S(2)}, u32[]{:S(2)}) collective-permute-start(bf16[2,1,1,1,16,2304]{5,4,3,2,1,0:T(8,128)(2,1)} %get-tuple-element.222), channel_id=1, source_target_pairs={{0,8},{1,9},{2,10},{3,11},{4,12},{5,13},{6,14},{7,15},{8,0},{9,1},... | collective-permute-start | bytes 442376 | tf_op jit(solution)/shard_map/ppermute | solution.py:582
  207.3 11.4 %copy-start.9 = (bf16[16,16,2304]{2,1,0:T(8,128)(2,1)S(1)}, bf16[16,16,2304]{2,1,0:T(8,128)(2,1)}, u32[]{:S(2)}) copy-start(bf16[16,16,2304]{2,1,0:T(8,128)(2,1)} %get-tuple-element.215) | copy-start | bytes 3538948
  207.3 12.0 %collective-permute-start.16 = (bf16[2,1,1,1,16,2304]{5,4,3,2,1,0:T(8,128)(2,1)}, bf16[2,1,1,1,16,2304]{5,4,3,2,1,0:T(8,128)(2,1)S(1)}, u32[]{:S(2)}, u32[]{:S(2)}) collective-permute-start(bf16[2,1,1,1,16,2304]{5,4,3,2,1,0:T(8,128)(2,1)} %get-tuple-element.221), channel_id=1, source_target_pairs={{0,4},{1,5},{2,6},{3,7},{4,0},{5,1},{6,2},{7,3},{8,12},{9,13},{10,... | collective-permute-start | bytes 442376 | tf_op jit(solution)/shard_map/ppermute | solution.py:582
  218.7 4.1 %copy-start.2 = (bf16[256,768]{1,0:T(8,128)(2,1)}, bf16[256,768]{1,0:T(8,128)(2,1)S(1)}, u32[]{:S(2)}) copy-start(bf16[256,768]{1,0:T(8,128)(2,1)S(1)} %collective-permute-done.22) | copy-start | bytes 1179652
  218.7 8.3 %collective-permute-start.10 = (bf16[16,16,2304]{2,1,0:T(8,128)(2,1)S(1)}, bf16[16,16,2304]{2,1,0:T(8,128)(2,1)S(1)}, u32[]{:S(2)}, u32[]{:S(2)}) collective-permute-start(bf16[16,16,2304]{2,1,0:T(8,128)(2,1)S(1)} %copy-done.9), channel_id=1, source_target_pairs={{0,2},{1,3},{2,0},{3,1},{4,6},{5,7},{6,4},{7,5},{8,10},{9,11},{10,... | collective-permute-start | bytes 3538952 | tf_op jit(solution)/shard_map/ppermute | solution.py:582
  218.8 8.2 %collective-permute-start.15 = (bf16[16,16,1280]{2,1,0:T(8,128)(2,1)}, bf16[16,16,1280]{2,1,0:T(8,128)(2,1)S(1)}, u32[]{:S(2)}, u32[]{:S(2)}) collective-permute-start(bf16[16,16,1280]{2,1,0:T(8,128)(2,1)} %get-tuple-element.229), channel_id=1, source_target_pairs={{0,2},{1,3},{2,0},{3,1},{4,6},{5,7},{6,4},{7,5},{8,10},{9,11},{10,... | collective-permute-start | bytes 1966088 | tf_op jit(solution)/shard_map/ppermute | solution.py:582
  222.8 19.8 %collective-permute-start.29 = (bf16[1,1,1,1,16,4608]{5,4,3,2,1,0:T(8,128)(2,1)}, bf16[1,1,1,1,16,4608]{5,4,3,2,1,0:T(8,128)(2,1)S(1)}, u32[]{:S(2)}, u32[]{:S(2)}) collective-permute-start(bf16[1,1,1,1,16,4608]{5,4,3,2,1,0:T(8,128)(2,1)} %get-tuple-element.234), channel_id=1, source_target_pairs={{0,16},{1,17},{2,18},{3,19},{4,20},{5,21},{6,22},{7,23},{8,24},{9,... | collective-permute-start | bytes 442376 | tf_op jit(solution)/shard_map/ppermute | solution.py:582
  225.5 17.7 %collective-permute-start.21 = (bf16[2,1,1,1,16,5888]{5,4,3,2,1,0:T(8,128)(2,1)}, bf16[2,1,1,1,16,5888]{5,4,3,2,1,0:T(8,128)(2,1)S(1)}, u32[]{:S(2)}, u32[]{:S(2)}) collective-permute-start(bf16[2,1,1,1,16,5888]{5,4,3,2,1,0:T(8,128)(2,1)} %get-tuple-element.237), channel_id=1, source_target_pairs={{0,1},{1,0},{2,3},{3,2},{4,5},{5,4},{6,7},{7,6},{8,9},{9,8},{10,11... | collective-permute-start | bytes 1130504 | tf_op jit(solution)/shard_map/ppermute | solution.py:582
  227.0 1.0 copy-start.8
  227.0 1.3 copy-start.13
  231.2 15.1 %collective-permute-start.24 = (bf16[2,1,1,2,16,3584]{5,4,3,2,1,0:T(8,128)(2,1)}, bf16[2,1,1,2,16,3584]{5,4,3,2,1,0:T(8,128)(2,1)S(1)}, u32[]{:S(2)}, u32[]{:S(2)}) collective-permute-start(bf16[2,1,1,2,16,3584]{5,4,3,2,1,0:T(8,128)(2,1)} %get-tuple-element.239), channel_id=1, source_target_pairs={{0,12},{1,13},{2,14},{3,15},{4,8},{5,9},{6,10},{7,11},{8,4},{9,5},... | collective-permute-start | bytes 1376264 | tf_op jit(solution)/shard_map/ppermute | solution.py:582
  233.8 24.5 %collective-permute-start.23 = (bf16[2,1,1,2,16,3584]{5,4,3,2,1,0:T(8,128)(2,1)}, bf16[2,1,1,2,16,3584]{5,4,3,2,1,0:T(8,128)(2,1)S(1)}, u32[]{:S(2)}, u32[]{:S(2)}) collective-permute-start(bf16[2,1,1,2,16,3584]{5,4,3,2,1,0:T(8,128)(2,1)} %get-tuple-element.238), channel_id=1, source_target_pairs={{0,8},{1,9},{2,10},{3,11},{4,12},{5,13},{6,14},{7,15},{8,0},{9,1},... | collective-permute-start | bytes 1376264 | tf_op jit(solution)/shard_map/ppermute | solution.py:582
  234.2 24.1 %collective-permute-start.20 = (bf16[2,1,1,2,16,3584]{5,4,3,2,1,0:T(8,128)(2,1)}, bf16[2,1,1,2,16,3584]{5,4,3,2,1,0:T(8,128)(2,1)S(1)}, u32[]{:S(2)}, u32[]{:S(2)}) collective-permute-start(bf16[2,1,1,2,16,3584]{5,4,3,2,1,0:T(8,128)(2,1)} %get-tuple-element.236), channel_id=1, source_target_pairs={{0,4},{1,5},{2,6},{3,7},{4,0},{5,1},{6,2},{7,3},{8,12},{9,13},{10,... | collective-permute-start | bytes 1376264 | tf_op jit(solution)/shard_map/ppermute | solution.py:582
  242.6 3.4 %copy-start.29 = (bf16[1,1,1,1,16,4608]{5,4,3,2,1,0:T(8,128)(2,1)}, bf16[1,1,1,1,16,4608]{5,4,3,2,1,0:T(8,128)(2,1)S(1)}, u32[]{:S(2)}) copy-start(bf16[1,1,1,1,16,4608]{5,4,3,2,1,0:T(8,128)(2,1)S(1)} %collective-permute-done.29.refs_5_.refs_11_) | copy-start | bytes 442372
  242.6 37.1 %collective-permute-start.25 = (bf16[384,768]{1,0:T(8,128)(2,1)}, bf16[384,768]{1,0:T(8,128)(2,1)}, u32[]{:S(2)}, u32[]{:S(2)}) collective-permute-start(bf16[384,768]{1,0:T(8,128)(2,1)} %get-tuple-element.251), channel_id=1, source_target_pairs={{0,1},{1,0},{2,3},{3,2},{4,5},{5,4},{6,7},{7,6},{8,9},{9,8},{10,11... | collective-permute-start | bytes 1769480 | tf_op jit(solution)/shard_map/ppermute | solution.py:570
  246.0 22.9 %collective-permute-start.30 = (bf16[1,1,1,1,16,5888]{5,4,3,2,1,0:T(8,128)(2,1)}, bf16[1,1,1,1,16,5888]{5,4,3,2,1,0:T(8,128)(2,1)S(1)}, u32[]{:S(2)}, u32[]{:S(2)}) collective-permute-start(bf16[1,1,1,1,16,5888]{5,4,3,2,1,0:T(8,128)(2,1)} %add_parts.12), channel_id=1, source_target_pairs={{0,16},{1,17},{2,18},{3,19},{4,20},{5,21},{6,22},{7,23},{8,24},{9,... | collective-permute-start | bytes 565256 | tf_op jit(solution)/shard_map/ppermute | solution.py:582
  246.3 12.0 %copy-start.16 = (bf16[2,1,1,2,16,3584]{5,4,3,2,1,0:T(8,128)(2,1)}, bf16[2,1,1,2,16,3584]{5,4,3,2,1,0:T(8,128)(2,1)S(1)}, u32[]{:S(2)}) copy-start(bf16[2,1,1,2,16,3584]{5,4,3,2,1,0:T(8,128)(2,1)S(1)} %collective-permute-done.24.refs_4_.refs_9_.refs_14_.refs_19_.refs_24_.refs_29_.refs_34_.refs_39_.refs_44_.refs_12_.refs_20_) | copy-start | bytes 1376260
  262.3 12.5 %collective-permute-start.26 = (bf16[1,1,1,1,16,3584]{5,4,3,2,1,0:T(8,128)(2,1)}, bf16[1,1,1,1,16,3584]{5,4,3,2,1,0:T(8,128)(2,1)S(1)}, u32[]{:S(2)}, u32[]{:S(2)}) collective-permute-start(bf16[1,1,1,1,16,3584]{5,4,3,2,1,0:T(8,128)(2,1)} %get-tuple-element.256), channel_id=1, source_target_pairs={{0,1},{1,0},{2,3},{3,2},{4,5},{5,4},{6,7},{7,6},{8,9},{9,8},{10,11... | collective-permute-start | bytes 344072 | tf_op jit(solution)/shard_map/ppermute | solution.py:582
  262.8 11.9 %collective-permute-start.27 = (bf16[1,1,1,1,16,3584]{5,4,3,2,1,0:T(8,128)(2,1)}, bf16[1,1,1,1,16,3584]{5,4,3,2,1,0:T(8,128)(2,1)S(1)}, u32[]{:S(2)}, u32[]{:S(2)}) collective-permute-start(bf16[1,1,1,1,16,3584]{5,4,3,2,1,0:T(8,128)(2,1)} %get-tuple-element.268), channel_id=1, source_target_pairs={{0,16},{1,17},{2,18},{3,19},{4,20},{5,21},{6,22},{7,23},{8,24},{9,... | collective-permute-start | bytes 344072 | tf_op jit(solution)/shard_map/ppermute | solution.py:582
  264.0 11.7 %collective-permute-start.28 = (bf16[1,1,1,1,16,3584]{5,4,3,2,1,0:T(8,128)(2,1)}, bf16[1,1,1,1,16,3584]{5,4,3,2,1,0:T(8,128)(2,1)S(1)}, u32[]{:S(2)}, u32[]{:S(2)}) collective-permute-start(bf16[1,1,1,1,16,3584]{5,4,3,2,1,0:T(8,128)(2,1)} %get-tuple-element.269), channel_id=1, source_target_pairs={{0,17},{1,16},{2,19},{3,18},{4,21},{5,20},{6,23},{7,22},{8,25},{9,... | collective-permute-start | bytes 344072 | tf_op jit(solution)/shard_map/ppermute | solution.py:582
  274.7 4.9 %copy-start.3 = (bf16[256,768]{1,0:T(8,128)(2,1)S(1)}, bf16[256,768]{1,0:T(8,128)(2,1)}, u32[]{:S(2)}) copy-start(bf16[256,768]{1,0:T(8,128)(2,1)} %copy-done.2) | copy-start | bytes 1179652
  274.7 1.0 copy-start.30
  (16 other events, 12.5 us)

commit v2 on v1

--- a/solution.py
+++ b/solution.py
@@ -16,6 +16,7 @@
 SHORT_HALF = 64
 BLOCKS = 32
 VMEM_LIMIT = 60 * 2**20
+SMALL_LIMIT = 12 * 2**20
 
 bf16 = jnp.bfloat16
 f32 = jnp.float32
@@ -159,7 +160,7 @@
         out_specs=[tok] * 5 + [lse, turned],
         out_shape=[SDS((rows, D), bf16)] * 5 + [SDS((48, 512), f32), SDS((D, rows), bf16)],
         input_output_aliases={11 + i: i for i in range(7)} if chained else {},
-        compiler_params=pltpu.CompilerParams(vmem_limit_bytes=VMEM_LIMIT),
+        compiler_params=pltpu.CompilerParams(vmem_limit_bytes=57 * 2**20),
         cost_estimate=LONG,
         name=f"attend_{row}",
     )(*place, own, other, *weights, *extra)
@@ -516,7 +517,7 @@
         out_shape=[SDS((2 * long, width), bf16)] * 3
         + [SDS((16, 16, size), bf16)] * 2
         + [SDS((8, width), f32)],
-        compiler_params=pltpu.CompilerParams(vmem_limit_bytes=VMEM_LIMIT),
+        compiler_params=pltpu.CompilerParams(vmem_limit_bytes=45 * 2**20),
         cost_estimate=LONG,
         name=f"back_group_{first}",
     )(me, *place, q, k, v, dctx, lse, *before, xt, *extra)
@@ -560,7 +561,7 @@
         ),
         out_shape=[SDS(before.shape, bf16), SDS((mid // 2, D), bf16), SDS(((long + mid) // 2, D), bf16)],
         input_output_aliases={2 + len(ins): 0},
-        compiler_params=pltpu.CompilerParams(vmem_limit_bytes=VMEM_LIMIT),
+        compiler_params=pltpu.CompilerParams(vmem_limit_bytes=24 * 2**20),
         cost_estimate=LONG,
         name="input_grad",
     )(seq, dr1, *ins, before)
@@ -657,7 +658,7 @@
         in_specs=specs,
         out_specs=[pl.BlockSpec(n, functools.partial(fixed, (0,) * 6)) for n in shapes],
         out_shape=[SDS(n, bf16) for n in shapes],
-        compiler_params=pltpu.CompilerParams(vmem_limit_bytes=VMEM_LIMIT),
+        compiler_params=pltpu.CompilerParams(vmem_limit_bytes=SMALL_LIMIT),
         cost_estimate=LONG,
         name="add_parts",
     )(*arrays)
@@ -727,7 +728,7 @@
         out_specs=[pl.BlockSpec(n, functools.partial(fixed, (0, 0))) for n in shapes],
         out_shape=[SDS(n, f32) for n in shapes],
         scratch_shapes=[pltpu.VMEM(n, f32) for n in scratch],
-        compiler_params=pltpu.CompilerParams(vmem_limit_bytes=VMEM_LIMIT),
+        compiler_params=pltpu.CompilerParams(vmem_limit_bytes=SMALL_LIMIT),
         cost_estimate=LONG,
         name="last_sums",
     )(seq, *[f[0] for f in found])
@@ -771,8 +772,8 @@
     )
 
 
-def give_back_kernel(seq, here, got, got_end, long_in, long, middle, short):
-    long[0] = got[...]
+def give_back_kernel(seq, here, got_first, got, got_end, long_in, long, middle, short):
+    long[0] = jnp.where(pl.program_id(0) == 0, got_first[...], got[...])
 
     @pl.when(seq[0] == 0)
     def _():
@@ -788,30 +789,31 @@
 def give_back(seq, long, here, got, short):
     count, half, _ = long.shape
     mid = here.shape[0]
-    other = lambda i, s: (count // 2 * (1 - s[0]) + i, 0, 0)
+    mine = count // 2
     return pl.pallas_call(
         give_back_kernel,
         grid_spec=pltpu.PrefetchScalarGridSpec(
             num_scalar_prefetch=1,
-            grid=(count // 2,),
+            grid=(mine,),
             in_specs=[
                 pl.BlockSpec((mid, D), lambda i, s: (0, 0)),
-                pl.BlockSpec((half, D), lambda i, s: (i, 0)),
-                pl.BlockSpec((mid, D), lambda i, s: (count // 2 * half // mid, 0)),
+                pl.BlockSpec((half, D), lambda i, s: (0, 0)),
+                pl.BlockSpec((half, D), lambda i, s: (jnp.maximum(i - 1, 0), 0)),
+                pl.BlockSpec((mid, D), lambda i, s: ((mine - 1) * half // mid, 0)),
                 ANY,
             ],
             out_specs=[
-                pl.BlockSpec((1, half, D), other),
+                pl.BlockSpec((1, half, D), lambda i, s: (mine * (1 - s[0]) + i, 0, 0)),
                 pl.BlockSpec((1, mid, D), lambda i, s: (0, 0, 0)),
                 pl.BlockSpec((1, short, D), lambda i, s: (0, 0, 0)),
             ],
         ),
         out_shape=[SDS(long.shape, bf16), SDS((1, mid, D), bf16), SDS((1, short, D), bf16)],
-        input_output_aliases={4: 0},
-        compiler_params=pltpu.CompilerParams(vmem_limit_bytes=VMEM_LIMIT),
+        input_output_aliases={5: 0},
+        compiler_params=pltpu.CompilerParams(vmem_limit_bytes=SMALL_LIMIT),
         cost_estimate=LONG,
         name="add_halves",
-    )(seq, here, got, got, long)
+    )(seq, here, got[0], got[1], got[1], long)
 
 
 def per_device(
@@ -847,7 +849,7 @@
     x_mid, x_mid_out = middle_rows(tokens_middle, tokens_short)
     x_mid_in = swap_seq(x_mid_out)
     x_own, x_out = own_rows(tokens_long), other_rows(tokens_long)
-    x_in = [swap_seq(x_out[i]) for i in range(mine)]
+    x_in = [swap_seq(later(x_out[0], x_mid_in))]
     u_mid, u_mid_out = middle_rows(upstream_middle, upstream_short)
     u_out = jnp.concatenate([other_rows(upstream_long).reshape(mine * half, D), u_mid_out], axis=0)
 
@@ -855,6 +857,7 @@
     qkv = [query_weight, key_weight, value_weight]
     projections = qkv + [query_bias, value_bias]
     chain = attention_forward(place, x_mid, x_mid_in, projections, mine, 2 * mid, mine * half // mid, None, rows)
+    x_in += [swap_seq(later(x_out[i], chain[5])) for i in range(1, mine)]
     for i in range(mine):
         chain = attention_forward(place, x_own[i], x_in[i], projections, i, 2 * half, i, chain, rows)
     x, q, k, v, ctx, lse, xt = chain
@@ -932,23 +935,25 @@
         all_sum[0].receive(down[0].outgoing[0])
         send(*all_sum)
         spare = all_sum[0].outgoing[0]
+    else:
+        spare = ig_rest
+    res_long, res_middle, res_short = give_back(
+        later(place[0], spare), res_long, res_mid, res_got, short
+    )
+    ig_long, ig_middle, ig_short = give_back(place[0], ig_long, ig_mid, ig_got, short)
+    if fast:
         down[0].receive()
         w_up, w_down, w_out, small = last_sums(
             last_dense_kernel, later(place[0], spare), [*up, *down], [(24, FF), (96, D), (24, D), (16, 128)], []
         )
-        all_sum[0].receive()
+        all_sum[0].receive(ig_middle)
         w_query, w_key, w_value, ends = last_sums(
             last_qkv_kernel, place[0], all_sum, [(24, D)] * 3 + [(16, 128)], [(24, 3 * D)]
         )
         b_up = lax.dynamic_slice(small, (8 + (me >> 3), 0), (1, 96))[0]
         done = w_query, ends[0, :24], w_key, w_value, ends[1, :24], w_out, small[:8, :24], w_up, b_up, w_down
     else:
-        spare = ig_rest
         done = reduce_plain(up_pair, down_pair, [wide_pair, narrow_pair], vec, jnp.concatenate([bg, bg_last], axis=1))
-    res_long, res_middle, res_short = give_back(
-        later(place[0], spare), res_long, res_mid, jnp.concatenate(res_got, axis=0), short
-    )
-    ig_long, ig_middle, ig_short = give_back(place[0], ig_long, ig_mid, jnp.concatenate(ig_got, axis=0), short)
     results = (res_short, res_middle, res_long)
     input_grads = (ig_short, ig_middle, ig_long)
     w_query, bq, w_key, w_value, bv, w_out, small, w_up, b_up, w_down = done

time: 289 us -> 275 us (0.952)
  Pallas kernels: 203 us -> 181 us
  local copies, waits for them, and re-layouts: 17.7 us -> 24.4 us
  waiting for transfers between devices: 22.4 us -> 25.3 us
    pallas_call x7, Pallas kernels: 20 us -> 8.25 us  [send(): pl.pallas_call(functools.partial(add_kernel, plan=plan), grid=(1,), in_sp...]
    unnamed x66 -> x102, local copies, waits for them, and re-layouts: 11 us -> 19.8 us
    ppermute x23, waiting for transfers between devices: 13.1 us -> 21.7 us  [swap(): lax.ppermute(v, ('dp', 'seq'), [(i, i ^ mask) for i in range(BLOCKS)])]
    ppermute x8, waiting for transfers between devices: 9.37 us -> 3.6 us  [swap_seq(): return lax.ppermute(v, 'seq', [(0, 1), (1, 0)])]
    pallas_call x2, Pallas kernels: 28.5 us -> 24 us  [group_backward(): pl.pallas_call(functools.partial(group_kernel, lengths=lengths, pairs=pai...]
    pallas_call x1, Pallas kernels: 7.87 us -> 3.78 us  [input_grad(): pl.pallas_call(functools.partial(input_grad_kernel, lengths=lengths, lane...]
    concatenate x2 -> x0, other arithmetic: 3.1 us -> none  [the longest x1 2.08 us: per_device(): jnp.concatenate(ig_got, axis=0)]
  transfers between devices with their start and end apart: 31 -> 31, of which waited for: 3 -> 5; matrix products, arithmetic and copies ran while one was open for 2% -> 2% of each run, Pallas kernels for 46% -> 41%
where the time goes in v2:
time: 275 us; the launch traced here: 271 us
  Pallas kernels  181 us (66%)
  starting transfers between devices  33.5 us (12%)
  waiting for transfers between devices  25.3 us (9%)
  local copies, waits for them, and re-layouts  24.4 us (9%)
  other arithmetic  3.54 us (1%)
  between operations  2.81 us (1%)
    pallas_call x2, Pallas kernels, dense_steps(): pl.pallas_call(functools.partial(drop_first(dense_kernel), chunks=4, own=...  68.2 us
    pallas_call x3, Pallas kernels, attention_forward(): pl.pallas_call(functools.partial(forward_kernel, length=length, row=row,...  26.3 us
    pallas_call x2, Pallas kernels, group_backward(): pl.pallas_call(functools.partial(group_kernel, lengths=lengths, pairs=pai...  24 us
    ppermute x23, starting transfers between devices, swap(): lax.ppermute(v, ('dp', 'seq'), [(i, i ^ mask) for i in range(BLOCKS)])  23.6 us
    ppermute x23, waiting for transfers between devices, swap(): lax.ppermute(v, ('dp', 'seq'), [(i, i ^ mask) for i in range(BLOCKS)])  21.7 us
    unnamed x102, local copies, waits for them, and re-layouts  19.8 us
    pallas_call x1, Pallas kernels, first_row_backward(): pl.pallas_call(functools.partial(first_row_kernel, length=length), grid_s...  15.9 us
    pallas_call x1, Pallas kernels, down_grad(): pl.pallas_call(down_grad_kernel, grid_spec=pltpu.PrefetchScalarGridSpec(n...  14.4 us
  transfers between devices with their start and end apart: 31, of which 5 were waited for; matrix products, arithmetic and copies ran while one was open for 2% of the time, Pallas kernels for 41%

profile of v2, /device:TPU:0, one launch (start us, length us, event | category | flops | bytes accessed | tf_op | source)
XLA Modules:
  0.0 270.8 jit_solution(12053892211651953590)
XLA Ops:
  0.7 1.8 pad_select_fusion.2
  2.5 2.9 %collective-permute-start = (bf16[128,768]{1,0:T(8,128)(2,1)S(1)}, bf16[128,768]{1,0:T(8,128)(2,1)S(1)}, u32[]{:S(2)}, u32[]{:S(2)}) collective-permute-start(bf16[128,768]{1,0:T(8,128)(2,1)S(1)} %get-tuple-element.295), channel_id=1, source_target_pairs={{0,1},{1,0},{2,3},{3,2},{4,5},{5,4},{6,7},{7,6},{8,9},{9,8},{10,11... | collective-permute-start | bytes 589832 | tf_op jit(solution)/shard_map/ppermute | solution.py:571
  5.5 1.2 constant_dynamic-slice_fusion.1
  6.7 1.6 pad_select_fusion
  10.7 1.4 collective-permute-start.2
  12.1 6.3 %attend_2.1 = (bf16[1536,768]{1,0:T(8,128)(2,1)}, bf16[1536,768]{1,0:T(8,128)(2,1)}, bf16[1536,768]{1,0:T(8,128)(2,1)}, bf16[1536,768]{1,0:T(8,128)(2,1)}, bf16[...) custom-call(s32[1]{0:T(128)} %bitcast.s0._.seq, s32[1]{0:T(128)S(6)} %copy.93.s1, ...), custom_call_target="tpu_custom_call" | custom-call | flops 40000000000 | bytes 100000000 | tf_op jit(solution)/shard_map/attend_2/pallas_call | solution.py:153
  19.1 3.6 %collective-permute-done.2.xr = bf16[256,768]{1,0:T(8,128)(2,1)S(1)} collective-permute-done((bf16[256,768]{1,0:T(8,128)(2,1)S(1)}, bf16[256,768]{1,0:T(8,128)(2,1)S(1)}, u32[]{:S(2)}, u32[]{:S(2)}) %collective-permute-start.2) | collective-permute-done | bytes 393248 | tf_op jit(solution)/shard_map/ppermute | solution.py:571
  23.4 9.9 %attend_0.1 = (bf16[1536,768]{1,0:T(8,128)(2,1)}, bf16[1536,768]{1,0:T(8,128)(2,1)}, bf16[1536,768]{1,0:T(8,128)(2,1)}, bf16[1536,768]{1,0:T(8,128)(2,1)}, bf16[...) custom-call(s32[1]{0:T(128)} %bitcast.s0._.seq, ...), custom_call_target="tpu_custom_call", output_to_operand_aliasing={{0}: (11, {}), {1}: (12, {}), {2}: (13, {}), {3}: (14, {}),... | custom-call | flops 40000000000 | bytes 100000000 | tf_op jit(solution)/shard_map/attend_0/pallas_call | solution.py:153
  34.0 10.1 %attend_1.1 = (bf16[1536,768]{1,0:T(8,128)(2,1)}, bf16[1536,768]{1,0:T(8,128)(2,1)}, bf16[1536,768]{1,0:T(8,128)(2,1)}, bf16[1536,768]{1,0:T(8,128)(2,1)}, bf16[...) custom-call(s32[1]{0:T(128)} %bitcast.s0._.seq, ...), custom_call_target="tpu_custom_call", output_to_operand_aliasing={{0}: (11, {}), {1}: (12, {}), {2}: (13, {}), {3}: (14, {}),... | custom-call | flops 40000000000 | bytes 100000000 | tf_op jit(solution)/shard_map/attend_1/pallas_call | solution.py:153
  44.8 24.4 %dense_own.1 = (bf16[4,256,768]{2,1,0:T(8,128)(2,1)}, bf16[1280,3072]{1,0:T(8,128)(2,1)}, bf16[1280,3072]{1,0:T(8,128)(2,1)}, bf16[1280,768]{1,0:T(8,128)(2,1)},...) custom-call(s32[1]{0:T(128)} %bitcast.s0._.seq, ...), custom_call_target="tpu_custom_call" | custom-call | flops 40000000000 | bytes 100000000 | tf_op jit(solution)/shard_map/dense_own/pallas_call | solution.py:286
  70.2 43.7 %dense_rest.1 = (bf16[640,768]{1,0:T(8,128)(2,1)}, bf16[128,768]{1,0:T(8,128)(2,1)}, bf16[1280,3072]{1,0:T(8,128)(2,1)}, bf16[1280,3072]{1,0:T(8,128)(2,1)}, bf1...) custom-call(s32[1]{0:T(128)} %bitcast.s0._.seq, ...), custom_call_target="tpu_custom_call", output_to_operand_aliasing={{2}: (17, {}), {3}: (18, {}), {4}: (19, {}), {5}: (20, {}),... | custom-call | flops 40000000000 | bytes 100000000 | tf_op jit(solution)/shard_map/dense_rest/pallas_call | solution.py:286
  113.9 13.3 %up_grad.1 = (bf16[16,16,4608]{2,1,0:T(8,128)(2,1)}, bf16[16,16,4608]{2,1,0:T(8,128)(2,1)}) custom-call(s32[1]{0:T(128)} %bitcast.1.me, bf16[1280,768]{1,0:T(8,128)(2,1)} %get-tuple-element.183.nlow, bf16[1280,3072]{1,0:T(8,128)(2,1)} %get-tuple-element.184.left.right, bf16[1280,3072]{1,0:T(8,128)(2,1)} %get-tuple-element.184.left.right), custom_call_target="tpu_custom_call" | custom-call | flops 40000000000 | bytes 100000000 | tf_op jit(solution)/shard_map/up_grad/pallas_call | solution.py:321
  127.3 1.5 collective-permute-start.8
  128.7 14.4 %down_grad.1 = (bf16[16,16,5888]{2,1,0:T(8,128)(2,1)}, bf16[16,16,5888]{2,1,0:T(8,128)(2,1)}) custom-call(s32[1]{0:T(128)} %bitcast.1.me, bf16[1280,3072]{1,0:T(8,128)(2,1)} %get-tuple-element.187.act, bf16[1280,768]{1,0:T(8,128)(2,1)} %get-tuple-element.188.dbr, bf16[1536,768]{1,0:T(8,128)(2,1)} %get-tuple-element.171.refs_0_.ctx, ...), custom_call_target="tpu_custom_call" | custom-call | flops 40000000000 | bytes 100000000 | tf_op jit(solution)/shard_map/down_grad/pallas_call | solution.py:369
  144.8 1.7 copy-done.18
  146.5 2.4 add_parts.7
  148.9 1.5 collective-permute-start.6
  150.5 1.6 collective-permute-start.5
  152.1 15.9 %back_first.1 = (bf16[512,768]{1,0:T(8,128)(2,1)}, bf16[512,768]{1,0:T(8,128)(2,1)}, bf16[512,768]{1,0:T(8,128)(2,1)}, bf16[4,256,768]{2,1,0:T(8,128)(2,1)}, bf16[256,768]{1,0:T(8,128)(2,1)}) custom-call(s32[1]{0:T(128)} %bitcast.s0._.seq, s32[1]{0:T(128)S(6)} %copy.93.s1, s32[1]{0:T(128)S(6)} %copy.94.s2, s32[4]{0:T(128)} %s3.11, ...), custom_call_target="tpu_custom_call" | custom-call | flops 40000000000 | bytes 100000000 | tf_op jit(solution)/shard_map/back_first/pallas_call | solution.py:432
  168.0 1.8 copy-done.14
  169.9 1.7 copy-done.19
  171.5 1.9 add_parts.8
  174.4 1.4 collective-permute-start.12
  176.7 14.3 %back_group_0.1 = (bf16[1024,512]{1,0:T(8,128)(2,1)S(1)}, bf16[1024,512]{1,0:T(8,128)(2,1)S(1)}, bf16[1024,512]{1,0:T(8,128)(2,1)S(1)}, bf16[16,16,2304]{2,1,0:T...) custom-call(s32[1]{0:T(128)} %bitcast.1.me, s32[1]{0:T(128)} %bitcast.s0._.seq, s32[1]{0:T(128)S(6)} %copy.93.s1, ...), custom_call_target="tpu_custom_call" | custom-call | flops 40000000000 | bytes 100000000 | tf_op jit(solution)/shard_map/back_group_0/pallas_call | solution.py:504
  191.1 1.5 collective-permute-start.22
  192.6 2.0 copy-done.15
  194.6 1.7 copy-done.20
  196.3 1.5 add_parts.9
  197.8 1.6 collective-permute-start.19
  199.4 1.5 collective-permute-start.18
  201.9 1.7 copy-done.27
  203.6 1.1 copy-done.36
  205.8 9.6 %back_group_4.1 = (bf16[1024,256]{1,0:T(8,128)(2,1)S(1)}, bf16[1024,256]{1,0:T(8,128)(2,1)S(1)}, bf16[1024,256]{1,0:T(8,128)(2,1)S(1)}, bf16[16,16,1280]{2,1,0:T...) custom-call(s32[1]{0:T(128)} %bitcast.1.me, s32[1]{0:T(128)} %bitcast.s0._.seq, s32[1]{0:T(128)S(6)} %copy.93.s1, ...), custom_call_target="tpu_custom_call" | custom-call | flops 40000000000 | bytes 100000000 | tf_op jit(solution)/shard_map/back_group_4/pallas_call | solution.py:504
  216.9 1.9 copy-done.16
  218.8 1.7 copy-done.21
  220.5 1.4 add_parts.10
  221.9 2.7 collective-permute-start.29
  224.5 1.4 collective-permute-start.21
  226.6 2.7 %collective-permute-start.24 = (bf16[2,1,1,2,16,3584]{5,4,3,2,1,0:T(8,128)(2,1)S(1)}, bf16[2,1,1,2,16,3584]{5,4,3,2,1,0:T(8,128)(2,1)S(1)}, u32[]{:S(2)}, u32[]{:S(2)}) collective-permute-start(bf16[2,1,1,2,16,3584]{5,4,3,2,1,0:T(8,128)(2,1)S(1)} %get-tuple-element.246), channel_id=1, source_target_pairs={{0,12},{1,13},{2,14},{3,15},{4,8},{5,9},{6,10},{7,11},{8,4},{9,5},... | collective-permute-start | bytes 1376264 | tf_op jit(solution)/shard_map/ppermute | solution.py:583
  230.2 3.8 %input_grad.1 = (bf16[4,256,768]{2,1,0:T(8,128)(2,1)}, bf16[128,768]{1,0:T(8,128)(2,1)S(1)}, bf16[384,768]{1,0:T(8,128)(2,1)}) custom-call(s32[1]{0:T(128)} %bitcast.s0._.seq, f32[1536,768]{1,0:T(8,128)S(1)} %bitcast.118, bf16[1024,512]{1,0:T(8,128)(2,1)S(1)} %copy-done.29, bf16[1024,512]{1,0:T(8,128)(2,1)S(1)} %copy-done.31, ...), custom_call_target="tpu_custom_call", output_to_operand_aliasing={{0}: (11, {})} | custom-call | flops 40000000000 | bytes 100000000 | tf_op jit(solution)/shard_map/input_grad/pallas_call | solution.py:548
  235.6 11.0 %collective-permute-done.24.refs_4_.refs_9_.refs_14_.refs_19_.refs_24_.refs_29_.refs_34_.refs_39_.refs_44_.refs_12_.refs_20_ = bf16[2,1,1,2,16,3584]{5,4,3,2,1,0:T(8,128)(2,1)S(1)} collective-permute-done((bf16[2,1,1,2,16,3584]{5,4,3,2,1,0:T(8,128)(2,1)S(1)}, bf16[2,1,1,2,16,3584]{5,4,3,2,1,0:T(8,128)(2,1)S(1)}, u32[]{:S(2)}, u32[]{:S(2)}) %collective-permute-start.24) | collective-permute-done | bytes 458784 | tf_op jit(solution)/shard_map/ppermute | solution.py:583
  246.6 8.9 %collective-permute-done.23.refs_3_.refs_8_.refs_13_.refs_18_.refs_23_.refs_28_.refs_33_.refs_38_.refs_43_.refs_11_.refs_19_ = bf16[2,1,1,2,16,3584]{5,4,3,2,1,0:T(8,128)(2,1)S(1)} collective-permute-done((bf16[2,1,1,2,16,3584]{5,4,3,2,1,0:T(8,128)(2,1)S(1)}, bf16[2,1,1,2,16,3584]{5,4,3,2,1,0:T(8,128)(2,1)S(1)}, u32[]{:S(2)}, u32[]{:S(2)}) %collective-permute-start.23) | collective-permute-done | bytes 458784 | tf_op jit(solution)/shard_map/ppermute | solution.py:583
  256.5 1.5 collective-permute-start.28
  258.0 2.2 collective-permute-start.27
  260.3 2.3 add_halves.2
  262.6 2.0 last_sums.3
  265.6 2.1 add_halves.3
  267.8 1.5 collective-permute-done.27.refs_6_.refs_14_.refs_22_
  (149 shorter events, 18.4 us)
Async XLA Ops:
  0.7 6.0 %copy-start.43 = (bf16[1,128,768]{2,1,0:T(8,128)(2,1)S(1)}, bf16[1,128,768]{2,1,0:T(8,128)(2,1)}, u32[]{:S(2)}) copy-start(bf16[1,128,768]{2,1,0:T(8,128)(2,1)} %param.46) | copy-start | bytes 589828
  0.7 9.0 %copy-start.41 = (bf16[4,256,768]{2,1,0:T(8,128)(2,1)S(1)}, bf16[4,256,768]{2,1,0:T(8,128)(2,1)}, u32[]{:S(2)}) copy-start(bf16[4,256,768]{2,1,0:T(8,128)(2,1)} %param.26) | copy-start | bytes 4718596
  2.5 8.1 %collective-permute-start = (bf16[128,768]{1,0:T(8,128)(2,1)S(1)}, bf16[128,768]{1,0:T(8,128)(2,1)S(1)}, u32[]{:S(2)}, u32[]{:S(2)}) collective-permute-start(bf16[128,768]{1,0:T(8,128)(2,1)S(1)} %get-tuple-element.295), channel_id=1, source_target_pairs={{0,1},{1,0},{2,3},{3,2},{4,5},{5,4},{6,7},{7,6},{8,9},{9,8},{10,11... | collective-permute-start | bytes 589832 | tf_op jit(solution)/shard_map/ppermute | solution.py:571
  10.7 12.0 %collective-permute-start.2 = (bf16[256,768]{1,0:T(8,128)(2,1)S(1)}, bf16[256,768]{1,0:T(8,128)(2,1)S(1)}, u32[]{:S(2)}, u32[]{:S(2)}) collective-permute-start(bf16[256,768]{1,0:T(8,128)(2,1)S(1)} %get-tuple-element.157), channel_id=1, source_target_pairs={{0,1},{1,0},{2,3},{3,2},{4,5},{5,4},{6,7},{7,6},{8,9},{9,8},{10,11... | collective-permute-start | bytes 1179656 | tf_op jit(solution)/shard_map/ppermute | solution.py:571
  18.4 14.9 %collective-permute-start.1 = (bf16[256,768]{1,0:T(8,128)(2,1)S(1)}, bf16[256,768]{1,0:T(8,128)(2,1)S(1)}, u32[]{:S(2)}, u32[]{:S(2)}) collective-permute-start(bf16[256,768]{1,0:T(8,128)(2,1)S(1)} %get-tuple-element.156), channel_id=1, source_target_pairs={{0,1},{1,0},{2,3},{3,2},{4,5},{5,4},{6,7},{7,6},{8,9},{9,8},{10,11... | collective-permute-start | bytes 1179656 | tf_op jit(solution)/shard_map/ppermute | solution.py:571
  44.2 25.0 %collective-permute-start.3 = (bf16[640,768]{1,0:T(8,128)(2,1)S(1)}, bf16[640,768]{1,0:T(8,128)(2,1)S(1)}, u32[]{:S(2)}, u32[]{:S(2)}) collective-permute-start(bf16[640,768]{1,0:T(8,128)(2,1)S(1)} %pad_maximum_fusion), channel_id=1, source_target_pairs={{0,1},{1,0},{2,3},{3,2},{4,5},{5,4},{6,7},{7,6},{8,9},{9,8},{10,11... | collective-permute-start | bytes 2949128 | tf_op jit(solution)/shard_map/ppermute | solution.py:571
  113.9 13.3 %copy-start.42 = (bf16[640,768]{1,0:T(8,128)(2,1)S(1)}, bf16[640,768]{1,0:T(8,128)(2,1)}, u32[]{:S(2)}) copy-start(bf16[640,768]{1,0:T(8,128)(2,1)} %get-tuple-element.211) | copy-start | bytes 2949124
  127.2 17.6 %collective-permute-start.4 = (bf16[16,16,4608]{2,1,0:T(8,128)(2,1)}, bf16[16,16,4608]{2,1,0:T(8,128)(2,1)}, u32[]{:S(2)}, u32[]{:S(2)}) collective-permute-start(bf16[16,16,4608]{2,1,0:T(8,128)(2,1)} %get-tuple-element.185), channel_id=1, source_target_pairs={{0,2},{1,3},{2,0},{3,1},{4,6},{5,7},{6,4},{7,5},{8,10},{9,11},{10,... | collective-permute-start | bytes 7077896 | tf_op jit(solution)/shard_map/ppermute | solution.py:583
  127.3 16.9 %collective-permute-start.8 = (bf16[256,768]{1,0:T(8,128)(2,1)S(1)}, bf16[256,768]{1,0:T(8,128)(2,1)S(1)}, u32[]{:S(2)}, u32[]{:S(2)}) collective-permute-start(bf16[256,768]{1,0:T(8,128)(2,1)S(1)} %slice.53), channel_id=1, source_target_pairs={{0,1},{1,0},{2,3},{3,2},{4,5},{5,4},{6,7},{7,6},{8,9},{9,8},{10,11... | collective-permute-start | bytes 1179656 | tf_op jit(solution)/shard_map/ppermute | solution.py:571
  144.0 24.0 %collective-permute-start.7 = (bf16[16,16,5888]{2,1,0:T(8,128)(2,1)}, bf16[16,16,5888]{2,1,0:T(8,128)(2,1)S(1)}, u32[]{:S(2)}, u32[]{:S(2)}) collective-permute-start(bf16[16,16,5888]{2,1,0:T(8,128)(2,1)} %get-tuple-element.191), channel_id=1, source_target_pairs={{0,2},{1,3},{2,0},{3,1},{4,6},{5,7},{6,4},{7,5},{8,10},{9,11},{10,... | collective-permute-start | bytes 9043976 | tf_op jit(solution)/shard_map/ppermute | solution.py:583
  144.2 23.8 %collective-permute-start.9 = (bf16[384,768]{1,0:T(8,128)(2,1)}, bf16[384,768]{1,0:T(8,128)(2,1)}, u32[]{:S(2)}, u32[]{:S(2)}) collective-permute-start(bf16[384,768]{1,0:T(8,128)(2,1)} %slice.54), channel_id=1, source_target_pairs={{0,1},{1,0},{2,3},{3,2},{4,5},{5,4},{6,7},{7,6},{8,9},{9,8},{10,11... | collective-permute-start | bytes 1769480 | tf_op jit(solution)/shard_map/ppermute | solution.py:571
  148.9 19.0 %collective-permute-start.6 = (bf16[2,2,1,2,16,2304]{5,4,3,2,1,0:T(8,128)(2,1)}, bf16[2,2,1,2,16,2304]{5,4,3,2,1,0:T(8,128)(2,1)S(1)}, u32[]{:S(2)}, u32[]{:S(2)}) collective-permute-start(bf16[2,2,1,2,16,2304]{5,4,3,2,1,0:T(8,128)(2,1)} %get-tuple-element.195), channel_id=1, source_target_pairs={{0,4},{1,5},{2,6},{3,7},{4,0},{5,1},{6,2},{7,3},{8,12},{9,13},{10,... | collective-permute-start | bytes 1769480 | tf_op jit(solution)/shard_map/ppermute | solution.py:583
  150.5 17.5 %collective-permute-start.5 = (bf16[2,1,2,2,16,2304]{5,4,3,2,1,0:T(8,128)(2,1)}, bf16[2,1,2,2,16,2304]{5,4,3,2,1,0:T(8,128)(2,1)}, u32[]{:S(2)}, u32[]{:S(2)}) collective-permute-start(bf16[2,1,2,2,16,2304]{5,4,3,2,1,0:T(8,128)(2,1)} %get-tuple-element.194), channel_id=1, source_target_pairs={{0,8},{1,9},{2,10},{3,11},{4,12},{5,13},{6,14},{7,15},{8,0},{9,1},... | collective-permute-start | bytes 1769480 | tf_op jit(solution)/shard_map/ppermute | solution.py:583
  171.5 5.1 %copy-start.40 = (f32[48,512]{1,0:T(8,128)S(1)}, f32[48,512]{1,0:T(8,128)}, u32[]{:S(2)}) copy-start(f32[48,512]{1,0:T(8,128)} %get-tuple-element.173.lse) | copy-start | bytes 294916
  173.4 19.1 %collective-permute-start.14 = (bf16[2,2,1,2,16,2944]{5,4,3,2,1,0:T(8,128)(2,1)S(1)}, bf16[2,2,1,2,16,2944]{5,4,3,2,1,0:T(8,128)(2,1)S(1)}, u32[]{:S(2)}, u32[]{:S(2)}) collective-permute-start(bf16[2,2,1,2,16,2944]{5,4,3,2,1,0:T(8,128)(2,1)S(1)} %get-tuple-element.210), channel_id=1, source_target_pairs={{0,4},{1,5},{2,6},{3,7},{4,0},{5,1},{6,2},{7,3},{8,12},{9,13},{10,... | collective-permute-start | bytes 2261000 | tf_op jit(solution)/shard_map/ppermute | solution.py:583
  174.0 18.6 %collective-permute-start.13 = (bf16[2,1,2,2,16,2944]{5,4,3,2,1,0:T(8,128)(2,1)S(1)}, bf16[2,1,2,2,16,2944]{5,4,3,2,1,0:T(8,128)(2,1)S(1)}, u32[]{:S(2)}, u32[]{:S(2)}) collective-permute-start(bf16[2,1,2,2,16,2944]{5,4,3,2,1,0:T(8,128)(2,1)S(1)} %get-tuple-element.209), channel_id=1, source_target_pairs={{0,8},{1,9},{2,10},{3,11},{4,12},{5,13},{6,14},{7,15},{8,0},{9,1},... | collective-permute-start | bytes 2261000 | tf_op jit(solution)/shard_map/ppermute | solution.py:583
  174.4 18.1 %collective-permute-start.12 = (bf16[2,2,1,1,16,2304]{5,4,3,2,1,0:T(8,128)(2,1)S(1)}, bf16[2,2,1,1,16,2304]{5,4,3,2,1,0:T(8,128)(2,1)S(1)}, u32[]{:S(2)}, u32[]{:S(2)}) collective-permute-start(bf16[2,2,1,1,16,2304]{5,4,3,2,1,0:T(8,128)(2,1)S(1)} %get-tuple-element.208), channel_id=1, source_target_pairs={{0,1},{1,0},{2,3},{3,2},{4,5},{5,4},{6,7},{7,6},{8,9},{9,8},{10,11... | collective-permute-start | bytes 884744 | tf_op jit(solution)/shard_map/ppermute | solution.py:583
  175.8 16.7 %collective-permute-start.11 = (bf16[2,1,2,1,16,2304]{5,4,3,2,1,0:T(8,128)(2,1)S(1)}, bf16[2,1,2,1,16,2304]{5,4,3,2,1,0:T(8,128)(2,1)S(1)}, u32[]{:S(2)}, u32[]{:S(2)}) collective-permute-start(bf16[2,1,2,1,16,2304]{5,4,3,2,1,0:T(8,128)(2,1)S(1)} %get-tuple-element.207), channel_id=1, source_target_pairs={{0,1},{1,0},{2,3},{3,2},{4,5},{5,4},{6,7},{7,6},{8,9},{9,8},{10,11... | collective-permute-start | bytes 884744 | tf_op jit(solution)/shard_map/ppermute | solution.py:583
  176.7 14.4 %copy-start.45 = (bf16[256,768]{1,0:T(8,128)(2,1)S(1)}, bf16[256,768]{1,0:T(8,128)(2,1)}, u32[]{:S(2)}) copy-start(bf16[256,768]{1,0:T(8,128)(2,1)} %get-tuple-element.248) | copy-start | bytes 1179652
  191.0 6.7 %copy-start.23 = (bf16[16,16,2304]{2,1,0:T(8,128)(2,1)}, bf16[16,16,2304]{2,1,0:T(8,128)(2,1)S(1)}, u32[]{:S(2)}) copy-start(bf16[16,16,2304]{2,1,0:T(8,128)(2,1)S(1)} %get-tuple-element.221) | copy-start | bytes 3538948
  191.0 6.7 %copy-start.28 = (bf16[1024,512]{1,0:T(8,128)(2,1)}, bf16[1024,512]{1,0:T(8,128)(2,1)S(1)}, u32[]{:S(2)}) copy-start(bf16[1024,512]{1,0:T(8,128)(2,1)S(1)} %get-tuple-element.251.rest_0_) | copy-start | bytes 3145732
  191.0 6.7 %copy-start.30 = (bf16[1024,512]{1,0:T(8,128)(2,1)}, bf16[1024,512]{1,0:T(8,128)(2,1)S(1)}, u32[]{:S(2)}) copy-start(bf16[1024,512]{1,0:T(8,128)(2,1)S(1)} %get-tuple-element.252.rest_1_) | copy-start | bytes 3145732
  191.0 6.7 %copy-start.32 = (bf16[1024,512]{1,0:T(8,128)(2,1)}, bf16[1024,512]{1,0:T(8,128)(2,1)S(1)}, u32[]{:S(2)}) copy-start(bf16[1024,512]{1,0:T(8,128)(2,1)S(1)} %get-tuple-element.253.rest_2_) | copy-start | bytes 3145732
  191.1 25.3 %collective-permute-start.22 = (bf16[256,768]{1,0:T(8,128)(2,1)S(1)}, bf16[256,768]{1,0:T(8,128)(2,1)S(1)}, u32[]{:S(2)}, u32[]{:S(2)}) collective-permute-start(bf16[256,768]{1,0:T(8,128)(2,1)S(1)} %copy-done.45), channel_id=1, source_target_pairs={{0,1},{1,0},{2,3},{3,2},{4,5},{5,4},{6,7},{7,6},{8,9},{9,8},{10,11... | collective-permute-start | bytes 1179656 | tf_op jit(solution)/shard_map/ppermute | solution.py:571
  192.5 24.3 %copy-start.7 = (bf16[2,2,1,1,16,2304]{5,4,3,2,1,0:T(8,128)(2,1)}, bf16[2,2,1,1,16,2304]{5,4,3,2,1,0:T(8,128)(2,1)S(1)}, u32[]{:S(2)}) copy-start(bf16[2,2,1,1,16,2304]{5,4,3,2,1,0:T(8,128)(2,1)S(1)} %collective-permute-done.12.refs_7_.refs_8_.refs_9_) | copy-start | bytes 884740
  192.5 24.4 %copy-start.9 = (bf16[2,1,2,1,16,2304]{5,4,3,2,1,0:T(8,128)(2,1)}, bf16[2,1,2,1,16,2304]{5,4,3,2,1,0:T(8,128)(2,1)S(1)}, u32[]{:S(2)}) copy-start(bf16[2,1,2,1,16,2304]{5,4,3,2,1,0:T(8,128)(2,1)S(1)} %collective-permute-done.11.refs_3_) | copy-start | bytes 884740
  197.8 19.1 %collective-permute-start.19 = (bf16[2,1,1,2,16,2944]{5,4,3,2,1,0:T(8,128)(2,1)S(1)}, bf16[2,1,1,2,16,2944]{5,4,3,2,1,0:T(8,128)(2,1)S(1)}, u32[]{:S(2)}, u32[]{:S(2)}) collective-permute-start(bf16[2,1,1,2,16,2944]{5,4,3,2,1,0:T(8,128)(2,1)S(1)} %get-tuple-element.231), channel_id=1, source_target_pairs={{0,8},{1,9},{2,10},{3,11},{4,12},{5,13},{6,14},{7,15},{8,0},{9,1},... | collective-permute-start | bytes 1130504 | tf_op jit(solution)/shard_map/ppermute | solution.py:583
  199.4 17.4 %collective-permute-start.18 = (bf16[2,1,1,2,16,2944]{5,4,3,2,1,0:T(8,128)(2,1)S(1)}, bf16[2,1,1,2,16,2944]{5,4,3,2,1,0:T(8,128)(2,1)S(1)}, u32[]{:S(2)}, u32[]{:S(2)}) collective-permute-start(bf16[2,1,1,2,16,2944]{5,4,3,2,1,0:T(8,128)(2,1)S(1)} %get-tuple-element.230), channel_id=1, source_target_pairs={{0,4},{1,5},{2,6},{3,7},{4,0},{5,1},{6,2},{7,3},{8,12},{9,13},{10,... | collective-permute-start | bytes 1130504 | tf_op jit(solution)/shard_map/ppermute | solution.py:583
  200.9 15.4 %collective-permute-start.17 = (bf16[2,1,1,1,16,2304]{5,4,3,2,1,0:T(8,128)(2,1)S(1)}, bf16[2,1,1,1,16,2304]{5,4,3,2,1,0:T(8,128)(2,1)S(1)}, u32[]{:S(2)}, u32[]{:S(2)}) collective-permute-start(bf16[2,1,1,1,16,2304]{5,4,3,2,1,0:T(8,128)(2,1)S(1)} %get-tuple-element.229), channel_id=1, source_target_pairs={{0,8},{1,9},{2,10},{3,11},{4,12},{5,13},{6,14},{7,15},{8,0},{9,1},... | collective-permute-start | bytes 442376 | tf_op jit(solution)/shard_map/ppermute | solution.py:583
  201.4 15.5 %collective-permute-start.16 = (bf16[2,1,1,1,16,2304]{5,4,3,2,1,0:T(8,128)(2,1)S(1)}, bf16[2,1,1,1,16,2304]{5,4,3,2,1,0:T(8,128)(2,1)S(1)}, u32[]{:S(2)}, u32[]{:S(2)}) collective-permute-start(bf16[2,1,1,1,16,2304]{5,4,3,2,1,0:T(8,128)(2,1)S(1)} %get-tuple-element.228), channel_id=1, source_target_pairs={{0,4},{1,5},{2,6},{3,7},{4,0},{5,1},{6,2},{7,3},{8,12},{9,13},{10,... | collective-permute-start | bytes 442376 | tf_op jit(solution)/shard_map/ppermute | solution.py:583
  216.3 5.5 %copy-start.5 = (bf16[256,768]{1,0:T(8,128)(2,1)}, bf16[256,768]{1,0:T(8,128)(2,1)S(1)}, u32[]{:S(2)}) copy-start(bf16[256,768]{1,0:T(8,128)(2,1)S(1)} %collective-permute-done.22.got_first) | copy-start | bytes 1179652
  216.3 9.5 %collective-permute-start.10 = (bf16[16,16,2304]{2,1,0:T(8,128)(2,1)S(1)}, bf16[16,16,2304]{2,1,0:T(8,128)(2,1)S(1)}, u32[]{:S(2)}, u32[]{:S(2)}) collective-permute-start(bf16[16,16,2304]{2,1,0:T(8,128)(2,1)S(1)} %get-tuple-element.222), channel_id=1, source_target_pairs={{0,2},{1,3},{2,0},{3,1},{4,6},{5,7},{6,4},{7,5},{8,10},{9,11},{10,... | collective-permute-start | bytes 3538952 | tf_op jit(solution)/shard_map/ppermute | solution.py:583
  216.4 9.5 %collective-permute-start.15 = (bf16[16,16,1280]{2,1,0:T(8,128)(2,1)S(1)}, bf16[16,16,1280]{2,1,0:T(8,128)(2,1)S(1)}, u32[]{:S(2)}, u32[]{:S(2)}) collective-permute-start(bf16[16,16,1280]{2,1,0:T(8,128)(2,1)S(1)} %get-tuple-element.236), channel_id=1, source_target_pairs={{0,2},{1,3},{2,0},{3,1},{4,6},{5,7},{6,4},{7,5},{8,10},{9,11},{10,... | collective-permute-start | bytes 1966088 | tf_op jit(solution)/shard_map/ppermute | solution.py:583
  220.5 5.4 %copy-start.24 = (bf16[16,16,2304]{2,1,0:T(8,128)(2,1)S(1)}, bf16[16,16,2304]{2,1,0:T(8,128)(2,1)}, u32[]{:S(2)}) copy-start(bf16[16,16,2304]{2,1,0:T(8,128)(2,1)} %copy-done.23) | copy-start | bytes 3538948
  220.5 5.4 %copy-start.26 = (bf16[16,16,1280]{2,1,0:T(8,128)(2,1)S(1)}, bf16[16,16,1280]{2,1,0:T(8,128)(2,1)}, u32[]{:S(2)}) copy-start(bf16[16,16,1280]{2,1,0:T(8,128)(2,1)} %copy-done.25) | copy-start | bytes 1966084
  220.5 9.7 %slice-start = ((s8[4718592]{0:T(1024)(128)(4,1)}), s8[4194304]{0:T(1024)(128)(4,1)S(1)}, s32[]{:S(2)}) async-start(s8[4718592]{0:T(1024)(128)(4,1)} %bitcast.117), calls=%async_computation | async-start | bytes 8388608
  221.9 12.2 %collective-permute-start.29 = (bf16[1,1,1,1,16,4608]{5,4,3,2,1,0:T(8,128)(2,1)S(1)}, bf16[1,1,1,1,16,4608]{5,4,3,2,1,0:T(8,128)(2,1)S(1)}, u32[]{:S(2)}, u32[]{:S(2)}) collective-permute-start(bf16[1,1,1,1,16,4608]{5,4,3,2,1,0:T(8,128)(2,1)S(1)} %get-tuple-element.241), channel_id=1, source_target_pairs={{0,16},{1,17},{2,18},{3,19},{4,20},{5,21},{6,22},{7,23},{8,24},{9,... | collective-permute-start | bytes 442376 | tf_op jit(solution)/shard_map/ppermute | solution.py:583
  224.5 10.5 %collective-permute-start.21 = (bf16[2,1,1,1,16,5888]{5,4,3,2,1,0:T(8,128)(2,1)S(1)}, bf16[2,1,1,1,16,5888]{5,4,3,2,1,0:T(8,128)(2,1)S(1)}, u32[]{:S(2)}, u32[]{:S(2)}) collective-permute-start(bf16[2,1,1,1,16,5888]{5,4,3,2,1,0:T(8,128)(2,1)S(1)} %get-tuple-element.244), channel_id=1, source_target_pairs={{0,1},{1,0},{2,3},{3,2},{4,5},{5,4},{6,7},{7,6},{8,9},{9,8},{10,11... | collective-permute-start | bytes 1130504 | tf_op jit(solution)/shard_map/ppermute | solution.py:583
  226.6 20.0 %collective-permute-start.24 = (bf16[2,1,1,2,16,3584]{5,4,3,2,1,0:T(8,128)(2,1)S(1)}, bf16[2,1,1,2,16,3584]{5,4,3,2,1,0:T(8,128)(2,1)S(1)}, u32[]{:S(2)}, u32[]{:S(2)}) collective-permute-start(bf16[2,1,1,2,16,3584]{5,4,3,2,1,0:T(8,128)(2,1)S(1)} %get-tuple-element.246), channel_id=1, source_target_pairs={{0,12},{1,13},{2,14},{3,15},{4,8},{5,9},{6,10},{7,11},{8,4},{9,5},... | collective-permute-start | bytes 1376264 | tf_op jit(solution)/shard_map/ppermute | solution.py:583
  229.3 26.2 %collective-permute-start.23 = (bf16[2,1,1,2,16,3584]{5,4,3,2,1,0:T(8,128)(2,1)S(1)}, bf16[2,1,1,2,16,3584]{5,4,3,2,1,0:T(8,128)(2,1)S(1)}, u32[]{:S(2)}, u32[]{:S(2)}) collective-permute-start(bf16[2,1,1,2,16,3584]{5,4,3,2,1,0:T(8,128)(2,1)S(1)} %get-tuple-element.245), channel_id=1, source_target_pairs={{0,8},{1,9},{2,10},{3,11},{4,12},{5,13},{6,14},{7,15},{8,0},{9,1},... | collective-permute-start | bytes 1376264 | tf_op jit(solution)/shard_map/ppermute | solution.py:583
  229.7 25.8 %collective-permute-start.20 = (bf16[2,1,1,2,16,3584]{5,4,3,2,1,0:T(8,128)(2,1)S(1)}, bf16[2,1,1,2,16,3584]{5,4,3,2,1,0:T(8,128)(2,1)S(1)}, u32[]{:S(2)}, u32[]{:S(2)}) collective-permute-start(bf16[2,1,1,2,16,3584]{5,4,3,2,1,0:T(8,128)(2,1)S(1)} %get-tuple-element.243), channel_id=1, source_target_pairs={{0,4},{1,5},{2,6},{3,7},{4,0},{5,1},{6,2},{7,3},{8,12},{9,13},{10,... | collective-permute-start | bytes 1376264 | tf_op jit(solution)/shard_map/ppermute | solution.py:583
  234.0 31.6 %collective-permute-start.25 = (bf16[384,768]{1,0:T(8,128)(2,1)}, bf16[384,768]{1,0:T(8,128)(2,1)}, u32[]{:S(2)}, u32[]{:S(2)}) collective-permute-start(bf16[384,768]{1,0:T(8,128)(2,1)} %get-tuple-element.258), channel_id=1, source_target_pairs={{0,1},{1,0},{2,3},{3,2},{4,5},{5,4},{6,7},{7,6},{8,9},{9,8},{10,11... | collective-permute-start | bytes 1769480 | tf_op jit(solution)/shard_map/ppermute | solution.py:571
  235.2 25.1 %copy-start.4 = (bf16[256,768]{1,0:T(8,128)(2,1)S(1)}, bf16[256,768]{1,0:T(8,128)(2,1)}, u32[]{:S(2)}) copy-start(bf16[256,768]{1,0:T(8,128)(2,1)} %copy-done.3) | copy-start | bytes 1179652
  235.2 25.1 %copy-start.39 = (bf16[128,768]{1,0:T(8,128)(2,1)S(1)}, bf16[128,768]{1,0:T(8,128)(2,1)}, u32[]{:S(2)}) copy-start(bf16[128,768]{1,0:T(8,128)(2,1)} %get-tuple-element.265.here) | copy-start | bytes 589828
  235.2 27.4 %collective-permute-start.30 = (bf16[1,1,1,1,16,5888]{5,4,3,2,1,0:T(8,128)(2,1)S(1)}, bf16[1,1,1,1,16,5888]{5,4,3,2,1,0:T(8,128)(2,1)S(1)}, u32[]{:S(2)}, u32[]{:S(2)}) collective-permute-start(bf16[1,1,1,1,16,5888]{5,4,3,2,1,0:T(8,128)(2,1)S(1)} %add_parts.12), channel_id=1, source_target_pairs={{0,16},{1,17},{2,18},{3,19},{4,20},{5,21},{6,22},{7,23},{8,24},{9,... | collective-permute-start | bytes 565256 | tf_op jit(solution)/shard_map/ppermute | solution.py:583
  255.8 13.4 %collective-permute-start.26 = (bf16[1,1,1,1,16,3584]{5,4,3,2,1,0:T(8,128)(2,1)S(1)}, bf16[1,1,1,1,16,3584]{5,4,3,2,1,0:T(8,128)(2,1)S(1)}, u32[]{:S(2)}, u32[]{:S(2)}) collective-permute-start(bf16[1,1,1,1,16,3584]{5,4,3,2,1,0:T(8,128)(2,1)S(1)} %get-tuple-element.263), channel_id=1, source_target_pairs={{0,1},{1,0},{2,3},{3,2},{4,5},{5,4},{6,7},{7,6},{8,9},{9,8},{10,11... | collective-permute-start | bytes 344072 | tf_op jit(solution)/shard_map/ppermute | solution.py:583
  256.5 11.2 %collective-permute-start.28 = (bf16[1,1,1,1,16,3584]{5,4,3,2,1,0:T(8,128)(2,1)S(1)}, bf16[1,1,1,1,16,3584]{5,4,3,2,1,0:T(8,128)(2,1)S(1)}, u32[]{:S(2)}, u32[]{:S(2)}) collective-permute-start(bf16[1,1,1,1,16,3584]{5,4,3,2,1,0:T(8,128)(2,1)S(1)} %get-tuple-element.278), channel_id=1, source_target_pairs={{0,17},{1,16},{2,19},{3,18},{4,21},{5,20},{6,23},{7,22},{8,25},{9,... | collective-permute-start | bytes 344072 | tf_op jit(solution)/shard_map/ppermute | solution.py:583
  258.0 11.2 %collective-permute-start.27 = (bf16[1,1,1,1,16,3584]{5,4,3,2,1,0:T(8,128)(2,1)S(1)}, bf16[1,1,1,1,16,3584]{5,4,3,2,1,0:T(8,128)(2,1)S(1)}, u32[]{:S(2)}, u32[]{:S(2)}) collective-permute-start(bf16[1,1,1,1,16,3584]{5,4,3,2,1,0:T(8,128)(2,1)S(1)} %get-tuple-element.276), channel_id=1, source_target_pairs={{0,16},{1,17},{2,18},{3,19},{4,20},{5,21},{6,22},{7,23},{8,24},{9,... | collective-permute-start | bytes 344072 | tf_op jit(solution)/shard_map/ppermute | solution.py:583
  (34 other events, 98.2 us)

commit v3 on v2

--- a/solution.py
+++ b/solution.py
@@ -186,7 +186,7 @@
         res_own, act, dinn, nlow_o, dbr, datt, dr1_o, dctx, vec, slope_s = refs[10:]
     else:
         vec_in = refs[10]
-        res_other, res_mid, act, dinn, nlow_o, dbr, datt, dr1_o, dctx, vec, slope_s = refs[18:]
+        res_first, res_rest, res_mid, act, dinn, nlow_o, dbr, datt, dr1_o, dctx, vec, slope_s = refs[18:]
 
     @pl.when(step == 0)
     def _():
@@ -217,14 +217,18 @@
     else:
         size = result.shape[0]
 
-        @pl.when(jnp.logical_not(last))
+        @pl.when(step == 0)
         def _():
-            res_other[pl.ds(pl.multiple_of(step * size, size), size), :] = result
+            res_first[...] = result
+
+        @pl.when((step > 0) & jnp.logical_not(last))
+        def _():
+            res_rest[pl.ds(pl.multiple_of((step - 1) * size, size), size), :] = result
 
         @pl.when(last)
         def _():
             res_mid[...] = result[: size // 2]
-            res_other[res_other.shape[0] - size // 2 :, :] = result[size // 2 :]
+            res_rest[res_rest.shape[0] - size // 2 :, :] = result[size // 2 :]
 
     upstream = up.astype(f32)
     u = upstream * g2
@@ -274,13 +278,14 @@
             pl.BlockSpec((half, D), lambda i, s: (jnp.minimum(2 * i + 1, 2 * mine), 0)),
             whole(half),
         ]
-        res_specs = [whole(tokens // 2), whole(half)]
-        res_shapes = [SDS((tokens // 2, D), bf16), SDS((half, D), bf16)]
+        sizes = (tile, tokens // 2 - tile, half)
+        res_specs = [whole(n) for n in sizes]
+        res_shapes = [SDS((n, D), bf16) for n in sizes]
         *arrays, vec = before
         extra = [vec] + arrays
         extra_specs = [whole(16)] + [ANY] * len(arrays)
         first = 1 + 2 + len(ups) + len(mats) + len(vecs) + 1
-        aliases = {first + i: 2 + i for i in range(len(arrays))}
+        aliases = {first + i: 3 + i for i in range(len(arrays))}
     tok = pl.BlockSpec((tile, D), lambda i, s: (place(i), 0))
     ffs = pl.BlockSpec((tile, FF), lambda i, s: (place(i), 0))
     return pl.pallas_call(
@@ -584,9 +589,10 @@
 
 
 class Payload:
-    def __init__(self, groups, order):
+    def __init__(self, groups, order, whole=False):
         self.groups = groups
         self.order = order
+        self.whole = whole
 
     def specs(self, bits):
         todo = {AXES[a][0] for a in "".join(self.order)}
@@ -641,15 +647,16 @@
     for h in sums:
         step, rest = h.order[0], h.order[1:]
         h.masks, h.count = [], 0
-        for which in range(1, 2 ** len(step)):
+        left = {AXES[a][0] for a in "".join(rest)}
+        shape = tuple(2 if d in left else 1 for d in range(4)) + (16, sum(g[0] for g in h.groups))
+        for which in range(0 if h.whole else 1, 2 ** len(step)):
             bits = {AXES[a][0]: which >> i & 1 for i, a in enumerate(step)}
             h.masks.append(sum(AXES[a][1] for i, a in enumerate(step) if which >> i & 1))
             found = h.specs(bits)
             arrays += [f[0] for f in found]
             specs += [f[1] for f in found]
             plan.append([(len(g[1]), g[0]) for g in h.groups])
-            left = {AXES[a][0] for a in "".join(rest)}
-            shapes.append(tuple(2 if d in left else 1 for d in range(4)) + (16, sum(g[0] for g in h.groups)))
+            shapes.append(shape)
             h.count += 1
         h.order = rest
     outs = pl.pallas_call(
@@ -666,6 +673,13 @@
     for h in sums:
         h.outgoing = outs[at : at + h.count]
         at += h.count
+        if h.whole:
+            h.whole = False
+            stays, h.outgoing, h.masks = h.outgoing[0], h.outgoing[1:], h.masks[1:]
+            low = 0
+            for n, (width, _) in enumerate(h.groups):
+                h.groups[n] = (width, [(stays, low // width)])
+                low += width
 
 
 def across_cores(pair, after, ranges, order):
@@ -673,7 +687,8 @@
     received = later(swap(leaving, CORE), after)
     both = [v.reshape(2, 2, 2, 2, 16, -1) for v in (keep, received)]
     return [
-        Payload([(width, [(v, lane) for v in both]) for width, lane in groups], axes) for axes, groups in zip(order, ranges)
+        Payload([(width, [(v, lane) for v in both]) for width, lane in groups], axes, len(axes[0]) == 1)
+        for axes, groups in zip(order, ranges)
     ]
 
 
@@ -849,7 +864,7 @@
     x_mid, x_mid_out = middle_rows(tokens_middle, tokens_short)
     x_mid_in = swap_seq(x_mid_out)
     x_own, x_out = own_rows(tokens_long), other_rows(tokens_long)
-    x_in = [swap_seq(later(x_out[0], x_mid_in))]
+    x_in = [swap_seq(x_out[0])]
     u_mid, u_mid_out = middle_rows(upstream_middle, upstream_short)
     u_out = jnp.concatenate([other_rows(upstream_long).reshape(mine * half, D), u_mid_out], axis=0)
 
@@ -869,14 +884,13 @@
         vecs=[up_bias, output_bias, attention_gain, attention_shift, down_bias, output_gain, output_shift],
     )
     res_long, *before = dense(ups=[upstream_long], before=None)
-    res_other, res_mid, act, dinn, nlow, dbr, datt, dr1, dctx, vec = dense(ups=[u_in, u_in, u_mid], before=before)
+    res_first, res_rest, res_mid, act, dinn, nlow, dbr, datt, dr1, dctx, vec = dense(ups=[u_in, u_in, u_mid], before=before)
 
     up_pair = up_grad(me_ref, nlow, dinn, tokens)
-    part = half
-    res_got = [swap_seq(later(res_other[:part], up_pair[0]))]
+    res_got = [swap_seq(later(res_first, up_pair[0]))]
     down_pair = down_grad(later(me_ref, up_pair[0]), act, dbr, ctx, datt, vec, tokens)
     res_got[0] = later(res_got[0], down_pair[0])
-    res_got.append(swap_seq(later(res_other[part:], res_got[0])))
+    res_got.append(swap_seq(later(res_rest, res_got[0])))
 
     def at(before, *sums, done=()):
         going = [v for h in sums for v in h.outgoing] if fast else []

time: 275 us -> 266 us (0.967)
  local copies, waits for them, and re-layouts: 24.4 us -> 19.1 us
    unnamed x102 -> x106, local copies, waits for them, and re-layouts: 19.8 us -> 15 us
  transfers between devices with their start and end apart: 31 -> 31, of which waited for: 5 -> 6; matrix products, arithmetic and copies ran while one was open for 2% -> 2% of each run, Pallas kernels for 41% -> 42%
where the time goes in v3:
time: 266 us; the launch traced here: 262 us
  Pallas kernels  180 us (68%)
  starting transfers between devices  33.8 us (13%)
  waiting for transfers between devices  22.7 us (9%)
  local copies, waits for them, and re-layouts  19.1 us (7%)
  between operations  2.77 us (1%)
  other arithmetic  2.71 us (1%)
    pallas_call x2, Pallas kernels, dense_steps(): pl.pallas_call(functools.partial(drop_first(dense_kernel), chunks=4, own=...  67.8 us
    pallas_call x3, Pallas kernels, attention_forward(): pl.pallas_call(functools.partial(forward_kernel, length=length, row=row,...  26.3 us
    pallas_call x2, Pallas kernels, group_backward(): pl.pallas_call(functools.partial(group_kernel, lengths=lengths, pairs=pai...  24.1 us
    ppermute x23, starting transfers between devices, swap(): lax.ppermute(v, ('dp', 'seq'), [(i, i ^ mask) for i in range(BLOCKS)])  23.3 us
    ppermute x23, waiting for transfers between devices, swap(): lax.ppermute(v, ('dp', 'seq'), [(i, i ^ mask) for i in range(BLOCKS)])  21.8 us
    pallas_call x1, Pallas kernels, first_row_backward(): pl.pallas_call(functools.partial(first_row_kernel, length=length), grid_s...  15.9 us
    unnamed x106, local copies, waits for them, and re-layouts  15 us
    pallas_call x1, Pallas kernels, down_grad(): pl.pallas_call(down_grad_kernel, grid_spec=pltpu.PrefetchScalarGridSpec(n...  14.4 us
  transfers between devices with their start and end apart: 31, of which 6 were waited for; matrix products, arithmetic and copies ran while one was open for 2% of the time, Pallas kernels for 42%

profile of v3, /device:TPU:0, one launch (start us, length us, event | category | flops | bytes accessed | tf_op | source)
XLA Modules:
  0.0 261.6 jit_solution(8633932701973446055)
XLA Ops:
  0.7 1.9 pad_select_fusion.2
  2.6 2.9 %collective-permute-start = (bf16[128,768]{1,0:T(8,128)(2,1)}, bf16[128,768]{1,0:T(8,128)(2,1)}, u32[]{:S(2)}, u32[]{:S(2)}) collective-permute-start(bf16[128,768]{1,0:T(8,128)(2,1)} %get-tuple-element.303), channel_id=1, source_target_pairs={{0,1},{1,0},{2,3},{3,2},{4,5},{5,4},{6,7},{7,6},{8,9},{9,8},{10,11... | collective-permute-start | bytes 589832 | tf_op jit(solution)/shard_map/ppermute | solution.py:576
  5.5 2.5 dynamic-slice_bitcast_fusion
  11.2 6.3 %attend_2.1 = (bf16[1536,768]{1,0:T(8,128)(2,1)}, bf16[1536,768]{1,0:T(8,128)(2,1)}, bf16[1536,768]{1,0:T(8,128)(2,1)}, bf16[1536,768]{1,0:T(8,128)(2,1)}, bf16[...) custom-call(s32[1]{0:T(128)} %bitcast.s0._.seq, s32[1]{0:T(128)S(6)} %copy.93.s1, ...), custom_call_target="tpu_custom_call" | custom-call | flops 40000000000 | bytes 100000000 | tf_op jit(solution)/shard_map/attend_2/pallas_call | solution.py:153
  17.5 2.5 collective-permute-start.1
  20.0 9.9 %attend_0.1 = (bf16[1536,768]{1,0:T(8,128)(2,1)}, bf16[1536,768]{1,0:T(8,128)(2,1)}, bf16[1536,768]{1,0:T(8,128)(2,1)}, bf16[1536,768]{1,0:T(8,128)(2,1)}, bf16[...) custom-call(s32[1]{0:T(128)} %bitcast.s0._.seq, ...), custom_call_target="tpu_custom_call", output_to_operand_aliasing={{0}: (11, {}), {1}: (12, {}), {2}: (13, {}), {3}: (14, {}),... | custom-call | flops 40000000000 | bytes 100000000 | tf_op jit(solution)/shard_map/attend_0/pallas_call | solution.py:153
  30.7 10.1 %attend_1.1 = (bf16[1536,768]{1,0:T(8,128)(2,1)}, bf16[1536,768]{1,0:T(8,128)(2,1)}, bf16[1536,768]{1,0:T(8,128)(2,1)}, bf16[1536,768]{1,0:T(8,128)(2,1)}, bf16[...) custom-call(s32[1]{0:T(128)} %bitcast.s0._.seq, ...), custom_call_target="tpu_custom_call", output_to_operand_aliasing={{0}: (11, {}), {1}: (12, {}), {2}: (13, {}), {3}: (14, {}),... | custom-call | flops 40000000000 | bytes 100000000 | tf_op jit(solution)/shard_map/attend_1/pallas_call | solution.py:153
  40.8 1.1 collective-permute-start.3
  41.9 24.4 %dense_own.1 = (bf16[4,256,768]{2,1,0:T(8,128)(2,1)}, bf16[1280,3072]{1,0:T(8,128)(2,1)}, bf16[1280,3072]{1,0:T(8,128)(2,1)}, bf16[1280,768]{1,0:T(8,128)(2,1)},...) custom-call(s32[1]{0:T(128)} %bitcast.s0._.seq, ...), custom_call_target="tpu_custom_call" | custom-call | flops 40000000000 | bytes 100000000 | tf_op jit(solution)/shard_map/dense_own/pallas_call | solution.py:291
  67.3 43.4 %dense_rest.1 = (bf16[256,768]{1,0:T(8,128)(2,1)}, bf16[384,768]{1,0:T(8,128)(2,1)}, bf16[128,768]{1,0:T(8,128)(2,1)}, bf16[1280,3072]{1,0:T(8,128)(2,1)}, bf16[...) custom-call(s32[1]{0:T(128)} %bitcast.s0._.seq, ...), custom_call_target="tpu_custom_call", output_to_operand_aliasing={{3}: (17, {}), {4}: (18, {}), {5}: (19, {}), {6}: (20, {}),... | custom-call | flops 40000000000 | bytes 100000000 | tf_op jit(solution)/shard_map/dense_rest/pallas_call | solution.py:291
  110.7 13.2 %up_grad.1 = (bf16[16,16,4608]{2,1,0:T(8,128)(2,1)}, bf16[16,16,4608]{2,1,0:T(8,128)(2,1)}) custom-call(s32[1]{0:T(128)} %bitcast.1.me, bf16[1280,768]{1,0:T(8,128)(2,1)} %get-tuple-element.186.nlow, bf16[1280,3072]{1,0:T(8,128)(2,1)} %get-tuple-element.187.left.right, bf16[1280,3072]{1,0:T(8,128)(2,1)} %get-tuple-element.187.left.right), custom_call_target="tpu_custom_call" | custom-call | flops 40000000000 | bytes 100000000 | tf_op jit(solution)/shard_map/up_grad/pallas_call | solution.py:326
  124.0 1.0 collective-permute-start.8
  125.0 14.4 %down_grad.1 = (bf16[16,16,5888]{2,1,0:T(8,128)(2,1)}, bf16[16,16,5888]{2,1,0:T(8,128)(2,1)}) custom-call(s32[1]{0:T(128)} %bitcast.1.me, bf16[1280,3072]{1,0:T(8,128)(2,1)} %get-tuple-element.190.act, bf16[1280,768]{1,0:T(8,128)(2,1)} %get-tuple-element.191.dbr, bf16[1536,768]{1,0:T(8,128)(2,1)} %get-tuple-element.174.refs_0_.ctx, ...), custom_call_target="tpu_custom_call" | custom-call | flops 40000000000 | bytes 100000000 | tf_op jit(solution)/shard_map/down_grad/pallas_call | solution.py:374
  140.3 1.1 collective-permute-start.9
  141.4 1.7 copy-done.15
  143.1 2.9 %add_parts.7 = (bf16[2,1,2,2,16,2304]{5,4,3,2,1,0:T(8,128)(2,1)S(1)}, bf16[2,1,2,2,16,2304]{5,4,3,2,1,0:T(8,128)(2,1)}, bf16[2,2,1,2,16,2304]{5,4,3,2,1,0:T(8,128)(2,1)S(1)}, bf16[2,2,1,2,16,2304]{5,4,3,2,1,0:T(8,128)(2,1)}) custom-call(bf16[2,2,2,2,16,4608]{5,4,3,2,1,0:T(8,128)(2,1)S(1)} %bitcast.74, ...), custom_call_target="tpu_custom_call" | custom-call | flops 40000000000 | bytes 100000000 | tf_op jit(solution)/shard_map/add_parts/pallas_call | solution.py:662
  147.6 1.5 collective-permute-start.6
  149.2 1.6 collective-permute-start.5
  150.7 15.9 %back_first.1 = (bf16[512,768]{1,0:T(8,128)(2,1)}, bf16[512,768]{1,0:T(8,128)(2,1)}, bf16[512,768]{1,0:T(8,128)(2,1)}, bf16[4,256,768]{2,1,0:T(8,128)(2,1)}, bf16[256,768]{1,0:T(8,128)(2,1)}) custom-call(s32[1]{0:T(128)} %bitcast.s0._.seq, s32[1]{0:T(128)S(6)} %copy.93.s1, s32[1]{0:T(128)S(6)} %copy.94.s2, s32[4]{0:T(128)} %s3.11, ...), custom_call_target="tpu_custom_call" | custom-call | flops 40000000000 | bytes 100000000 | tf_op jit(solution)/shard_map/back_first/pallas_call | solution.py:437
  166.7 1.8 copy-done.14
  168.5 1.1 copy-done.32
  169.6 1.1 copy-done.37
  170.7 2.2 add_parts.8
  174.8 1.1 collective-permute-start.11
  176.0 14.4 %back_group_0.1 = (bf16[1024,512]{1,0:T(8,128)(2,1)S(1)}, bf16[1024,512]{1,0:T(8,128)(2,1)S(1)}, bf16[1024,512]{1,0:T(8,128)(2,1)S(1)}, bf16[16,16,2304]{2,1,0:T...) custom-call(s32[1]{0:T(128)} %bitcast.1.me, s32[1]{0:T(128)} %bitcast.s0._.seq, s32[1]{0:T(128)S(6)} %copy.93.s1, ...), custom_call_target="tpu_custom_call" | custom-call | flops 40000000000 | bytes 100000000 | tf_op jit(solution)/shard_map/back_group_0/pallas_call | solution.py:509
  190.4 1.0 collective-permute-start.22
  191.5 1.4 add_parts.9
  193.0 1.7 collective-permute-start.19
  194.6 1.5 collective-permute-start.18
  197.1 9.7 %back_group_4.1 = (bf16[1024,256]{1,0:T(8,128)(2,1)S(1)}, bf16[1024,256]{1,0:T(8,128)(2,1)S(1)}, bf16[1024,256]{1,0:T(8,128)(2,1)S(1)}, bf16[16,16,1280]{2,1,0:T...) custom-call(s32[1]{0:T(128)} %bitcast.1.me, s32[1]{0:T(128)} %bitcast.s0._.seq, s32[1]{0:T(128)S(6)} %copy.93.s1, ...), custom_call_target="tpu_custom_call" | custom-call | flops 40000000000 | bytes 100000000 | tf_op jit(solution)/shard_map/back_group_4/pallas_call | solution.py:509
  207.4 1.1 copy-done.20
  208.6 1.1 copy-done.23
  209.7 1.1 copy-done.34
  210.8 1.1 copy-done.39
  211.8 1.3 add_parts.10
  213.1 2.7 %collective-permute-start.29 = (bf16[1,1,1,1,16,4608]{5,4,3,2,1,0:T(8,128)(2,1)S(1)}, bf16[1,1,1,1,16,4608]{5,4,3,2,1,0:T(8,128)(2,1)S(1)}, u32[]{:S(2)}, u32[]{:S(2)}) collective-permute-start(bf16[1,1,1,1,16,4608]{5,4,3,2,1,0:T(8,128)(2,1)S(1)} %get-tuple-element.249), channel_id=1, source_target_pairs={{0,16},{1,17},{2,18},{3,19},{4,20},{5,21},{6,22},{7,23},{8,24},{9,... | collective-permute-start | bytes 442376 | tf_op jit(solution)/shard_map/ppermute | solution.py:588
  215.8 1.1 collective-permute-start.21
  217.6 2.6 collective-permute-start.24
  221.2 4.0 %input_grad.1 = (bf16[4,256,768]{2,1,0:T(8,128)(2,1)}, bf16[128,768]{1,0:T(8,128)(2,1)S(1)}, bf16[384,768]{1,0:T(8,128)(2,1)}) custom-call(s32[1]{0:T(128)} %bitcast.s0._.seq, f32[1536,768]{1,0:T(8,128)S(1)} %bitcast.100, bf16[1024,512]{1,0:T(8,128)(2,1)S(1)} %get-tuple-element.259.rest_0_, ...), custom_call_target="tpu_custom_call", output_to_operand_aliasing={{0}: (11, {})} | custom-call | flops 40000000000 | bytes 100000000 | tf_op jit(solution)/shard_map/input_grad/pallas_call | solution.py:553
  226.9 10.9 %collective-permute-done.24.refs_4_.refs_9_.refs_14_.refs_19_.refs_24_.refs_29_.refs_34_.refs_39_.refs_44_.refs_12_.refs_20_ = bf16[2,1,1,2,16,3584]{5,4,3,2,1,0:T(8,128)(2,1)S(1)} collective-permute-done((bf16[2,1,1,2,16,3584]{5,4,3,2,1,0:T(8,128)(2,1)S(1)}, bf16[2,1,1,2,16,3584]{5,4,3,2,1,0:T(8,128)(2,1)S(1)}, u32[]{:S(2)}, u32[]{:S(2)}) %collective-permute-start.24) | collective-permute-done | bytes 458784 | tf_op jit(solution)/shard_map/ppermute | solution.py:588
  237.7 8.8 %collective-permute-done.23.refs_3_.refs_8_.refs_13_.refs_18_.refs_23_.refs_28_.refs_33_.refs_38_.refs_43_.refs_11_.refs_19_ = bf16[2,1,1,2,16,3584]{5,4,3,2,1,0:T(8,128)(2,1)S(1)} collective-permute-done((bf16[2,1,1,2,16,3584]{5,4,3,2,1,0:T(8,128)(2,1)S(1)}, bf16[2,1,1,2,16,3584]{5,4,3,2,1,0:T(8,128)(2,1)S(1)}, u32[]{:S(2)}, u32[]{:S(2)}) %collective-permute-start.23) | collective-permute-done | bytes 458784 | tf_op jit(solution)/shard_map/ppermute | solution.py:588
  246.9 1.0 collective-permute-start.26
  247.9 1.0 collective-permute-start.28
  248.9 2.4 collective-permute-start.27
  251.4 1.1 add_halves.2
  253.2 1.9 last_sums.3
  256.1 2.1 add_halves.3
  258.7 1.4 collective-permute-done.27.refs_6_.refs_14_.refs_22_
  (151 shorter events, 16.8 us)
Async XLA Ops:
  0.7 7.4 %copy-start.46 = (bf16[1,64,768]{2,1,0:T(8,128)(2,1)S(1)}, bf16[1,64,768]{2,1,0:T(8,128)(2,1)}, u32[]{:S(2)}) copy-start(bf16[1,64,768]{2,1,0:T(8,128)(2,1)} %param.45) | copy-start | bytes 294916
  0.7 7.4 %copy-start.45 = (bf16[1,128,768]{2,1,0:T(8,128)(2,1)S(1)}, bf16[1,128,768]{2,1,0:T(8,128)(2,1)}, u32[]{:S(2)}) copy-start(bf16[1,128,768]{2,1,0:T(8,128)(2,1)} %param.46) | copy-start | bytes 589828
  0.7 8.2 %copy-start.43 = (bf16[4,256,768]{2,1,0:T(8,128)(2,1)S(1)}, bf16[4,256,768]{2,1,0:T(8,128)(2,1)}, u32[]{:S(2)}) copy-start(bf16[4,256,768]{2,1,0:T(8,128)(2,1)} %refs_2_.1) | copy-start | bytes 4718596
  2.6 8.6 %collective-permute-start = (bf16[128,768]{1,0:T(8,128)(2,1)}, bf16[128,768]{1,0:T(8,128)(2,1)}, u32[]{:S(2)}, u32[]{:S(2)}) collective-permute-start(bf16[128,768]{1,0:T(8,128)(2,1)} %get-tuple-element.303), channel_id=1, source_target_pairs={{0,1},{1,0},{2,3},{3,2},{4,5},{5,4},{6,7},{7,6},{8,9},{9,8},{10,11... | collective-permute-start | bytes 589832 | tf_op jit(solution)/shard_map/ppermute | solution.py:576
  8.1 12.0 %collective-permute-start.2 = (bf16[256,768]{1,0:T(8,128)(2,1)}, bf16[256,768]{1,0:T(8,128)(2,1)}, u32[]{:S(2)}, u32[]{:S(2)}) collective-permute-start(bf16[256,768]{1,0:T(8,128)(2,1)} %get-tuple-element.297), channel_id=1, source_target_pairs={{0,1},{1,0},{2,3},{3,2},{4,5},{5,4},{6,7},{7,6},{8,9},{9,8},{10,11... | collective-permute-start | bytes 1179656 | tf_op jit(solution)/shard_map/ppermute | solution.py:576
  11.2 6.3 %copy-start.44 = (bf16[256,768]{1,0:T(8,128)(2,1)S(1)}, bf16[256,768]{1,0:T(8,128)(2,1)}, u32[]{:S(2)}) copy-start(bf16[256,768]{1,0:T(8,128)(2,1)} %get-tuple-element.160) | copy-start | bytes 1179652
  17.5 12.4 %collective-permute-start.1 = (bf16[256,768]{1,0:T(8,128)(2,1)S(1)}, bf16[256,768]{1,0:T(8,128)(2,1)S(1)}, u32[]{:S(2)}, u32[]{:S(2)}) collective-permute-start(bf16[256,768]{1,0:T(8,128)(2,1)S(1)} %copy-done.44), channel_id=1, source_target_pairs={{0,1},{1,0},{2,3},{3,2},{4,5},{5,4},{6,7},{7,6},{8,9},{9,8},{10,11... | collective-permute-start | bytes 1179656 | tf_op jit(solution)/shard_map/ppermute | solution.py:576
  40.8 25.5 %collective-permute-start.3 = (bf16[640,768]{1,0:T(8,128)(2,1)S(1)}, bf16[640,768]{1,0:T(8,128)(2,1)S(1)}, u32[]{:S(2)}, u32[]{:S(2)}) collective-permute-start(bf16[640,768]{1,0:T(8,128)(2,1)S(1)} %pad_maximum_fusion), channel_id=1, source_target_pairs={{0,1},{1,0},{2,3},{3,2},{4,5},{5,4},{6,7},{7,6},{8,9},{9,8},{10,11... | collective-permute-start | bytes 2949128 | tf_op jit(solution)/shard_map/ppermute | solution.py:576
  110.7 13.3 %copy-start.49 = (bf16[256,768]{1,0:T(8,128)(2,1)S(1)}, bf16[256,768]{1,0:T(8,128)(2,1)}, u32[]{:S(2)}) copy-start(bf16[256,768]{1,0:T(8,128)(2,1)} %get-tuple-element.217) | copy-start | bytes 1179652
  124.0 17.5 %collective-permute-start.4 = (bf16[16,16,4608]{2,1,0:T(8,128)(2,1)}, bf16[16,16,4608]{2,1,0:T(8,128)(2,1)}, u32[]{:S(2)}, u32[]{:S(2)}) collective-permute-start(bf16[16,16,4608]{2,1,0:T(8,128)(2,1)} %get-tuple-element.188), channel_id=1, source_target_pairs={{0,2},{1,3},{2,0},{3,1},{4,6},{5,7},{6,4},{7,5},{8,10},{9,11},{10,... | collective-permute-start | bytes 7077896 | tf_op jit(solution)/shard_map/ppermute | solution.py:588
  124.0 15.6 %collective-permute-start.8 = (bf16[256,768]{1,0:T(8,128)(2,1)S(1)}, bf16[256,768]{1,0:T(8,128)(2,1)S(1)}, u32[]{:S(2)}, u32[]{:S(2)}) collective-permute-start(bf16[256,768]{1,0:T(8,128)(2,1)S(1)} %copy-done.49), channel_id=1, source_target_pairs={{0,1},{1,0},{2,3},{3,2},{4,5},{5,4},{6,7},{7,6},{8,9},{9,8},{10,11... | collective-permute-start | bytes 1179656 | tf_op jit(solution)/shard_map/ppermute | solution.py:576
  139.3 27.3 %collective-permute-start.7 = (bf16[16,16,5888]{2,1,0:T(8,128)(2,1)}, bf16[16,16,5888]{2,1,0:T(8,128)(2,1)S(1)}, u32[]{:S(2)}, u32[]{:S(2)}) collective-permute-start(bf16[16,16,5888]{2,1,0:T(8,128)(2,1)} %get-tuple-element.194), channel_id=1, source_target_pairs={{0,2},{1,3},{2,0},{3,1},{4,6},{5,7},{6,4},{7,5},{8,10},{9,11},{10,... | collective-permute-start | bytes 9043976 | tf_op jit(solution)/shard_map/ppermute | solution.py:588
  140.3 26.3 %collective-permute-start.9 = (bf16[384,768]{1,0:T(8,128)(2,1)}, bf16[384,768]{1,0:T(8,128)(2,1)S(1)}, u32[]{:S(2)}, u32[]{:S(2)}) collective-permute-start(bf16[384,768]{1,0:T(8,128)(2,1)} %get-tuple-element.220), channel_id=1, source_target_pairs={{0,1},{1,0},{2,3},{3,2},{4,5},{5,4},{6,7},{7,6},{8,9},{9,8},{10,11... | collective-permute-start | bytes 1769480 | tf_op jit(solution)/shard_map/ppermute | solution.py:576
  147.6 19.0 %collective-permute-start.6 = (bf16[2,2,1,2,16,2304]{5,4,3,2,1,0:T(8,128)(2,1)}, bf16[2,2,1,2,16,2304]{5,4,3,2,1,0:T(8,128)(2,1)}, u32[]{:S(2)}, u32[]{:S(2)}) collective-permute-start(bf16[2,2,1,2,16,2304]{5,4,3,2,1,0:T(8,128)(2,1)} %get-tuple-element.198), channel_id=1, source_target_pairs={{0,4},{1,5},{2,6},{3,7},{4,0},{5,1},{6,2},{7,3},{8,12},{9,13},{10,... | collective-permute-start | bytes 1769480 | tf_op jit(solution)/shard_map/ppermute | solution.py:588
  149.2 17.5 %collective-permute-start.5 = (bf16[2,1,2,2,16,2304]{5,4,3,2,1,0:T(8,128)(2,1)}, bf16[2,1,2,2,16,2304]{5,4,3,2,1,0:T(8,128)(2,1)}, u32[]{:S(2)}, u32[]{:S(2)}) collective-permute-start(bf16[2,1,2,2,16,2304]{5,4,3,2,1,0:T(8,128)(2,1)} %get-tuple-element.197), channel_id=1, source_target_pairs={{0,8},{1,9},{2,10},{3,11},{4,12},{5,13},{6,14},{7,15},{8,0},{9,1},... | collective-permute-start | bytes 1769480 | tf_op jit(solution)/shard_map/ppermute | solution.py:588
  172.9 18.6 %copy-start.19 = (bf16[2,1,2,2,16,2944]{5,4,3,2,1,0:T(8,128)(2,1)}, bf16[2,1,2,2,16,2944]{5,4,3,2,1,0:T(8,128)(2,1)S(1)}, u32[]{:S(2)}) copy-start(bf16[2,1,2,2,16,2944]{5,4,3,2,1,0:T(8,128)(2,1)S(1)} %get-tuple-element.232.refs_6_.refs_8_.refs_0_.refs_10_) | copy-start | bytes 2260996
  172.9 18.5 %copy-start.22 = (bf16[2,2,1,2,16,2944]{5,4,3,2,1,0:T(8,128)(2,1)}, bf16[2,2,1,2,16,2944]{5,4,3,2,1,0:T(8,128)(2,1)S(1)}, u32[]{:S(2)}) copy-start(bf16[2,2,1,2,16,2944]{5,4,3,2,1,0:T(8,128)(2,1)S(1)} %get-tuple-element.234.refs_8_.refs_11_.refs_4_.refs_15_) | copy-start | bytes 2260996
  172.9 18.5 %collective-permute-start.14 = (bf16[2,2,1,2,16,2944]{5,4,3,2,1,0:T(8,128)(2,1)S(1)}, bf16[2,2,1,2,16,2944]{5,4,3,2,1,0:T(8,128)(2,1)S(1)}, u32[]{:S(2)}, u32[]{:S(2)}) collective-permute-start(bf16[2,2,1,2,16,2944]{5,4,3,2,1,0:T(8,128)(2,1)S(1)} %get-tuple-element.215), channel_id=1, source_target_pairs={{0,4},{1,5},{2,6},{3,7},{4,0},{5,1},{6,2},{7,3},{8,12},{9,13},{10,... | collective-permute-start | bytes 2261000 | tf_op jit(solution)/shard_map/ppermute | solution.py:588
  173.5 18.0 %collective-permute-start.13 = (bf16[2,1,2,2,16,2944]{5,4,3,2,1,0:T(8,128)(2,1)S(1)}, bf16[2,1,2,2,16,2944]{5,4,3,2,1,0:T(8,128)(2,1)S(1)}, u32[]{:S(2)}, u32[]{:S(2)}) collective-permute-start(bf16[2,1,2,2,16,2944]{5,4,3,2,1,0:T(8,128)(2,1)S(1)} %get-tuple-element.214), channel_id=1, source_target_pairs={{0,8},{1,9},{2,10},{3,11},{4,12},{5,13},{6,14},{7,15},{8,0},{9,1},... | collective-permute-start | bytes 2261000 | tf_op jit(solution)/shard_map/ppermute | solution.py:588
  173.9 17.4 %collective-permute-start.12 = (bf16[2,2,1,1,16,2304]{5,4,3,2,1,0:T(8,128)(2,1)S(1)}, bf16[2,2,1,1,16,2304]{5,4,3,2,1,0:T(8,128)(2,1)S(1)}, u32[]{:S(2)}, u32[]{:S(2)}) collective-permute-start(bf16[2,2,1,1,16,2304]{5,4,3,2,1,0:T(8,128)(2,1)S(1)} %get-tuple-element.213), channel_id=1, source_target_pairs={{0,1},{1,0},{2,3},{3,2},{4,5},{5,4},{6,7},{7,6},{8,9},{9,8},{10,11... | collective-permute-start | bytes 884744 | tf_op jit(solution)/shard_map/ppermute | solution.py:588
  174.8 16.5 %collective-permute-start.11 = (bf16[2,1,2,1,16,2304]{5,4,3,2,1,0:T(8,128)(2,1)S(1)}, bf16[2,1,2,1,16,2304]{5,4,3,2,1,0:T(8,128)(2,1)S(1)}, u32[]{:S(2)}, u32[]{:S(2)}) collective-permute-start(bf16[2,1,2,1,16,2304]{5,4,3,2,1,0:T(8,128)(2,1)S(1)} %get-tuple-element.212), channel_id=1, source_target_pairs={{0,1},{1,0},{2,3},{3,2},{4,5},{5,4},{6,7},{7,6},{8,9},{9,8},{10,11... | collective-permute-start | bytes 884744 | tf_op jit(solution)/shard_map/ppermute | solution.py:588
  176.0 14.4 %copy-start.48 = (bf16[256,768]{1,0:T(8,128)(2,1)S(1)}, bf16[256,768]{1,0:T(8,128)(2,1)}, u32[]{:S(2)}) copy-start(bf16[256,768]{1,0:T(8,128)(2,1)} %get-tuple-element.256) | copy-start | bytes 1179652
  176.0 15.5 %copy-start.33 = (bf16[2,1,2,2,16,2304]{5,4,3,2,1,0:T(8,128)(2,1)S(1)}, bf16[2,1,2,2,16,2304]{5,4,3,2,1,0:T(8,128)(2,1)}, u32[]{:S(2)}) copy-start(bf16[2,1,2,2,16,2304]{5,4,3,2,1,0:T(8,128)(2,1)} %copy-done.31) | copy-start | bytes 1769476
  176.0 15.5 %copy-start.38 = (bf16[2,2,1,2,16,2304]{5,4,3,2,1,0:T(8,128)(2,1)S(1)}, bf16[2,2,1,2,16,2304]{5,4,3,2,1,0:T(8,128)(2,1)}, u32[]{:S(2)}) copy-start(bf16[2,2,1,2,16,2304]{5,4,3,2,1,0:T(8,128)(2,1)} %copy-done.36) | copy-start | bytes 1769476
  190.4 16.4 %collective-permute-start.22 = (bf16[256,768]{1,0:T(8,128)(2,1)S(1)}, bf16[256,768]{1,0:T(8,128)(2,1)S(1)}, u32[]{:S(2)}, u32[]{:S(2)}) collective-permute-start(bf16[256,768]{1,0:T(8,128)(2,1)S(1)} %copy-done.48), channel_id=1, source_target_pairs={{0,1},{1,0},{2,3},{3,2},{4,5},{5,4},{6,7},{7,6},{8,9},{9,8},{10,11... | collective-permute-start | bytes 1179656 | tf_op jit(solution)/shard_map/ppermute | solution.py:576
  191.4 16.0 %copy-start.7 = (bf16[2,2,1,1,16,2304]{5,4,3,2,1,0:T(8,128)(2,1)}, bf16[2,2,1,1,16,2304]{5,4,3,2,1,0:T(8,128)(2,1)S(1)}, u32[]{:S(2)}) copy-start(bf16[2,2,1,1,16,2304]{5,4,3,2,1,0:T(8,128)(2,1)S(1)} %collective-permute-done.12.refs_5_.refs_6_.refs_7_) | copy-start | bytes 884740
  191.4 16.0 %copy-start.9 = (bf16[2,1,2,1,16,2304]{5,4,3,2,1,0:T(8,128)(2,1)}, bf16[2,1,2,1,16,2304]{5,4,3,2,1,0:T(8,128)(2,1)S(1)}, u32[]{:S(2)}) copy-start(bf16[2,1,2,1,16,2304]{5,4,3,2,1,0:T(8,128)(2,1)S(1)} %collective-permute-done.11.refs_2_) | copy-start | bytes 884740
  193.0 14.4 %collective-permute-start.19 = (bf16[2,1,1,2,16,2944]{5,4,3,2,1,0:T(8,128)(2,1)S(1)}, bf16[2,1,1,2,16,2944]{5,4,3,2,1,0:T(8,128)(2,1)S(1)}, u32[]{:S(2)}, u32[]{:S(2)}) collective-permute-start(bf16[2,1,1,2,16,2944]{5,4,3,2,1,0:T(8,128)(2,1)S(1)} %get-tuple-element.239), channel_id=1, source_target_pairs={{0,8},{1,9},{2,10},{3,11},{4,12},{5,13},{6,14},{7,15},{8,0},{9,1},... | collective-permute-start | bytes 1130504 | tf_op jit(solution)/shard_map/ppermute | solution.py:588
  194.6 12.8 %collective-permute-start.18 = (bf16[2,1,1,2,16,2944]{5,4,3,2,1,0:T(8,128)(2,1)S(1)}, bf16[2,1,1,2,16,2944]{5,4,3,2,1,0:T(8,128)(2,1)S(1)}, u32[]{:S(2)}, u32[]{:S(2)}) collective-permute-start(bf16[2,1,1,2,16,2944]{5,4,3,2,1,0:T(8,128)(2,1)S(1)} %get-tuple-element.238), channel_id=1, source_target_pairs={{0,4},{1,5},{2,6},{3,7},{4,0},{5,1},{6,2},{7,3},{8,12},{9,13},{10,... | collective-permute-start | bytes 1130504 | tf_op jit(solution)/shard_map/ppermute | solution.py:588
  196.1 10.8 %collective-permute-start.17 = (bf16[2,1,1,1,16,2304]{5,4,3,2,1,0:T(8,128)(2,1)S(1)}, bf16[2,1,1,1,16,2304]{5,4,3,2,1,0:T(8,128)(2,1)S(1)}, u32[]{:S(2)}, u32[]{:S(2)}) collective-permute-start(bf16[2,1,1,1,16,2304]{5,4,3,2,1,0:T(8,128)(2,1)S(1)} %get-tuple-element.237), channel_id=1, source_target_pairs={{0,8},{1,9},{2,10},{3,11},{4,12},{5,13},{6,14},{7,15},{8,0},{9,1},... | collective-permute-start | bytes 442376 | tf_op jit(solution)/shard_map/ppermute | solution.py:588
  196.6 10.8 %collective-permute-start.16 = (bf16[2,1,1,1,16,2304]{5,4,3,2,1,0:T(8,128)(2,1)S(1)}, bf16[2,1,1,1,16,2304]{5,4,3,2,1,0:T(8,128)(2,1)S(1)}, u32[]{:S(2)}, u32[]{:S(2)}) collective-permute-start(bf16[2,1,1,1,16,2304]{5,4,3,2,1,0:T(8,128)(2,1)S(1)} %get-tuple-element.236), channel_id=1, source_target_pairs={{0,4},{1,5},{2,6},{3,7},{4,0},{5,1},{6,2},{7,3},{8,12},{9,13},{10,... | collective-permute-start | bytes 442376 | tf_op jit(solution)/shard_map/ppermute | solution.py:588
  206.8 6.3 %copy-start.5 = (bf16[256,768]{1,0:T(8,128)(2,1)}, bf16[256,768]{1,0:T(8,128)(2,1)S(1)}, u32[]{:S(2)}) copy-start(bf16[256,768]{1,0:T(8,128)(2,1)S(1)} %collective-permute-done.22.got_first) | copy-start | bytes 1179652
  206.8 10.1 %collective-permute-start.10 = (bf16[16,16,2304]{2,1,0:T(8,128)(2,1)S(1)}, bf16[16,16,2304]{2,1,0:T(8,128)(2,1)S(1)}, u32[]{:S(2)}, u32[]{:S(2)}) collective-permute-start(bf16[16,16,2304]{2,1,0:T(8,128)(2,1)S(1)} %get-tuple-element.228), channel_id=1, source_target_pairs={{0,2},{1,3},{2,0},{3,1},{4,6},{5,7},{6,4},{7,5},{8,10},{9,11},{10,... | collective-permute-start | bytes 3538952 | tf_op jit(solution)/shard_map/ppermute | solution.py:588
  206.9 10.0 %collective-permute-start.15 = (bf16[16,16,1280]{2,1,0:T(8,128)(2,1)S(1)}, bf16[16,16,1280]{2,1,0:T(8,128)(2,1)S(1)}, u32[]{:S(2)}, u32[]{:S(2)}) collective-permute-start(bf16[16,16,1280]{2,1,0:T(8,128)(2,1)S(1)} %get-tuple-element.244), channel_id=1, source_target_pairs={{0,2},{1,3},{2,0},{3,1},{4,6},{5,7},{6,4},{7,5},{8,10},{9,11},{10,... | collective-permute-start | bytes 1966088 | tf_op jit(solution)/shard_map/ppermute | solution.py:588
  207.4 5.7 %copy-start.11 = (bf16[2,1,1,1,16,2304]{5,4,3,2,1,0:T(8,128)(2,1)}, bf16[2,1,1,1,16,2304]{5,4,3,2,1,0:T(8,128)(2,1)S(1)}, u32[]{:S(2)}) copy-start(bf16[2,1,1,1,16,2304]{5,4,3,2,1,0:T(8,128)(2,1)S(1)} %collective-permute-done.16.refs_3_) | copy-start | bytes 442372
  211.8 9.3 %slice-start = ((s8[4718592]{0:T(1024)(128)(4,1)}), s8[4194304]{0:T(1024)(128)(4,1)S(1)}, s32[]{:S(2)}) async-start(s8[4718592]{0:T(1024)(128)(4,1)} %bitcast.99), calls=%async_computation | async-start | bytes 8388608
  213.1 12.1 %collective-permute-start.29 = (bf16[1,1,1,1,16,4608]{5,4,3,2,1,0:T(8,128)(2,1)S(1)}, bf16[1,1,1,1,16,4608]{5,4,3,2,1,0:T(8,128)(2,1)S(1)}, u32[]{:S(2)}, u32[]{:S(2)}) collective-permute-start(bf16[1,1,1,1,16,4608]{5,4,3,2,1,0:T(8,128)(2,1)S(1)} %get-tuple-element.249), channel_id=1, source_target_pairs={{0,16},{1,17},{2,18},{3,19},{4,20},{5,21},{6,22},{7,23},{8,24},{9,... | collective-permute-start | bytes 442376 | tf_op jit(solution)/shard_map/ppermute | solution.py:588
  215.8 10.5 %collective-permute-start.21 = (bf16[2,1,1,1,16,5888]{5,4,3,2,1,0:T(8,128)(2,1)S(1)}, bf16[2,1,1,1,16,5888]{5,4,3,2,1,0:T(8,128)(2,1)S(1)}, u32[]{:S(2)}, u32[]{:S(2)}) collective-permute-start(bf16[2,1,1,1,16,5888]{5,4,3,2,1,0:T(8,128)(2,1)S(1)} %get-tuple-element.252), channel_id=1, source_target_pairs={{0,1},{1,0},{2,3},{3,2},{4,5},{5,4},{6,7},{7,6},{8,9},{9,8},{10,11... | collective-permute-start | bytes 1130504 | tf_op jit(solution)/shard_map/ppermute | solution.py:588
  217.6 20.1 %collective-permute-start.24 = (bf16[2,1,1,2,16,3584]{5,4,3,2,1,0:T(8,128)(2,1)S(1)}, bf16[2,1,1,2,16,3584]{5,4,3,2,1,0:T(8,128)(2,1)S(1)}, u32[]{:S(2)}, u32[]{:S(2)}) collective-permute-start(bf16[2,1,1,2,16,3584]{5,4,3,2,1,0:T(8,128)(2,1)S(1)} %get-tuple-element.254), channel_id=1, source_target_pairs={{0,12},{1,13},{2,14},{3,15},{4,8},{5,9},{6,10},{7,11},{8,4},{9,5},... | collective-permute-start | bytes 1376264 | tf_op jit(solution)/shard_map/ppermute | solution.py:588
  220.2 26.4 %collective-permute-start.23 = (bf16[2,1,1,2,16,3584]{5,4,3,2,1,0:T(8,128)(2,1)S(1)}, bf16[2,1,1,2,16,3584]{5,4,3,2,1,0:T(8,128)(2,1)S(1)}, u32[]{:S(2)}, u32[]{:S(2)}) collective-permute-start(bf16[2,1,1,2,16,3584]{5,4,3,2,1,0:T(8,128)(2,1)S(1)} %get-tuple-element.253), channel_id=1, source_target_pairs={{0,8},{1,9},{2,10},{3,11},{4,12},{5,13},{6,14},{7,15},{8,0},{9,1},... | collective-permute-start | bytes 1376264 | tf_op jit(solution)/shard_map/ppermute | solution.py:588
  220.7 25.9 %collective-permute-start.20 = (bf16[2,1,1,2,16,3584]{5,4,3,2,1,0:T(8,128)(2,1)S(1)}, bf16[2,1,1,2,16,3584]{5,4,3,2,1,0:T(8,128)(2,1)S(1)}, u32[]{:S(2)}, u32[]{:S(2)}) collective-permute-start(bf16[2,1,1,2,16,3584]{5,4,3,2,1,0:T(8,128)(2,1)S(1)} %get-tuple-element.251), channel_id=1, source_target_pairs={{0,4},{1,5},{2,6},{3,7},{4,0},{5,1},{6,2},{7,3},{8,12},{9,13},{10,... | collective-permute-start | bytes 1376264 | tf_op jit(solution)/shard_map/ppermute | solution.py:588
  225.2 30.9 %collective-permute-start.25 = (bf16[384,768]{1,0:T(8,128)(2,1)}, bf16[384,768]{1,0:T(8,128)(2,1)}, u32[]{:S(2)}, u32[]{:S(2)}) collective-permute-start(bf16[384,768]{1,0:T(8,128)(2,1)} %get-tuple-element.266), channel_id=1, source_target_pairs={{0,1},{1,0},{2,3},{3,2},{4,5},{5,4},{6,7},{7,6},{8,9},{9,8},{10,11... | collective-permute-start | bytes 1769480 | tf_op jit(solution)/shard_map/ppermute | solution.py:576
  226.4 24.9 %copy-start.4 = (bf16[256,768]{1,0:T(8,128)(2,1)S(1)}, bf16[256,768]{1,0:T(8,128)(2,1)}, u32[]{:S(2)}) copy-start(bf16[256,768]{1,0:T(8,128)(2,1)} %copy-done.3) | copy-start | bytes 1179652
  226.4 24.9 %copy-start.41 = (bf16[128,768]{1,0:T(8,128)(2,1)S(1)}, bf16[128,768]{1,0:T(8,128)(2,1)}, u32[]{:S(2)}) copy-start(bf16[128,768]{1,0:T(8,128)(2,1)} %get-tuple-element.273.here) | copy-start | bytes 589828
  226.4 26.0 %collective-permute-start.30 = (bf16[1,1,1,1,16,5888]{5,4,3,2,1,0:T(8,128)(2,1)S(1)}, bf16[1,1,1,1,16,5888]{5,4,3,2,1,0:T(8,128)(2,1)S(1)}, u32[]{:S(2)}, u32[]{:S(2)}) collective-permute-start(bf16[1,1,1,1,16,5888]{5,4,3,2,1,0:T(8,128)(2,1)S(1)} %add_parts.12), channel_id=1, source_target_pairs={{0,16},{1,17},{2,18},{3,19},{4,20},{5,21},{6,22},{7,23},{8,24},{9,... | collective-permute-start | bytes 565256 | tf_op jit(solution)/shard_map/ppermute | solution.py:588
  246.9 13.2 %collective-permute-start.26 = (bf16[1,1,1,1,16,3584]{5,4,3,2,1,0:T(8,128)(2,1)S(1)}, bf16[1,1,1,1,16,3584]{5,4,3,2,1,0:T(8,128)(2,1)S(1)}, u32[]{:S(2)}, u32[]{:S(2)}) collective-permute-start(bf16[1,1,1,1,16,3584]{5,4,3,2,1,0:T(8,128)(2,1)S(1)} %get-tuple-element.271), channel_id=1, source_target_pairs={{0,1},{1,0},{2,3},{3,2},{4,5},{5,4},{6,7},{7,6},{8,9},{9,8},{10,11... | collective-permute-start | bytes 344072 | tf_op jit(solution)/shard_map/ppermute | solution.py:588
  247.9 10.8 %collective-permute-start.28 = (bf16[1,1,1,1,16,3584]{5,4,3,2,1,0:T(8,128)(2,1)S(1)}, bf16[1,1,1,1,16,3584]{5,4,3,2,1,0:T(8,128)(2,1)S(1)}, u32[]{:S(2)}, u32[]{:S(2)}) collective-permute-start(bf16[1,1,1,1,16,3584]{5,4,3,2,1,0:T(8,128)(2,1)S(1)} %get-tuple-element.286), channel_id=1, source_target_pairs={{0,17},{1,16},{2,19},{3,18},{4,21},{5,20},{6,23},{7,22},{8,25},{9,... | collective-permute-start | bytes 344072 | tf_op jit(solution)/shard_map/ppermute | solution.py:588
  248.9 11.2 %collective-permute-start.27 = (bf16[1,1,1,1,16,3584]{5,4,3,2,1,0:T(8,128)(2,1)S(1)}, bf16[1,1,1,1,16,3584]{5,4,3,2,1,0:T(8,128)(2,1)S(1)}, u32[]{:S(2)}, u32[]{:S(2)}) collective-permute-start(bf16[1,1,1,1,16,3584]{5,4,3,2,1,0:T(8,128)(2,1)S(1)} %get-tuple-element.284), channel_id=1, source_target_pairs={{0,16},{1,17},{2,18},{3,19},{4,20},{5,21},{6,22},{7,23},{8,24},{9,... | collective-permute-start | bytes 344072 | tf_op jit(solution)/shard_map/ppermute | solution.py:588
  (36 other events, 107.7 us)

commit v4 on v3

--- a/solution.py
+++ b/solution.py
@@ -943,12 +943,14 @@
     )
     ig_got.append(swap_seq(ig_rest))
     if fast:
-        up[0].receive(ig_rest)
+        up[0].outgoing = [later(up[0].outgoing[0], ig_rest)]
+    if fast:
         down[0].receive(ig_rest)
         send(*down)
         all_sum[0].receive(down[0].outgoing[0])
         send(*all_sum)
         spare = all_sum[0].outgoing[0]
+        up[0].receive(spare)
     else:
         spare = ig_rest
     res_long, res_middle, res_short = give_back(

time: 266 us -> 265 us (level)
  waiting for transfers between devices: 22.7 us -> 17.4 us
  starting transfers between devices: 33.8 us -> 37.2 us
    ppermute x23, waiting for transfers between devices: 21.8 us -> 16.5 us  [swap(): lax.ppermute(v, ('dp', 'seq'), [(i, i ^ mask) for i in range(BLOCKS)])]
    ppermute x23, starting transfers between devices: 23.3 us -> 26.6 us  [swap(): lax.ppermute(v, ('dp', 'seq'), [(i, i ^ mask) for i in range(BLOCKS)])]
  transfers between devices with their start and end apart: 31 -> 31, of which waited for: 6 -> 5; matrix products, arithmetic and copies ran while one was open for 2% -> 2% of each run, Pallas kernels for 42% -> 43%
where the time goes in v4:
time: 265 us; the launch traced here: 260 us
  Pallas kernels  181 us (68%)
  starting transfers between devices  37.2 us (14%)
  local copies, waits for them, and re-layouts  18.8 us (7%)
  waiting for transfers between devices  17.4 us (7%)
  between operations  2.78 us (1%)
  other arithmetic  2.71 us (1%)
    pallas_call x2, Pallas kernels, dense_steps(): pl.pallas_call(functools.partial(drop_first(dense_kernel), chunks=4, own=...  67.8 us
    ppermute x23, starting transfers between devices, swap(): lax.ppermute(v, ('dp', 'seq'), [(i, i ^ mask) for i in range(BLOCKS)])  26.6 us
    pallas_call x3, Pallas kernels, attention_forward(): pl.pallas_call(functools.partial(forward_kernel, length=length, row=row,...  26.3 us
    pallas_call x2, Pallas kernels, group_backward(): pl.pallas_call(functools.partial(group_kernel, lengths=lengths, pairs=pai...  24 us
    ppermute x23, waiting for transfers between devices, swap(): lax.ppermute(v, ('dp', 'seq'), [(i, i ^ mask) for i in range(BLOCKS)])  16.5 us
    pallas_call x1, Pallas kernels, first_row_backward(): pl.pallas_call(functools.partial(first_row_kernel, length=length), grid_s...  15.9 us
    unnamed x106, local copies, waits for them, and re-layouts  14.7 us
    pallas_call x1, Pallas kernels, down_grad(): pl.pallas_call(down_grad_kernel, grid_spec=pltpu.PrefetchScalarGridSpec(n...  14.4 us
  transfers between devices with their start and end apart: 31, of which 5 were waited for; matrix products, arithmetic and copies ran while one was open for 2% of the time, Pallas kernels for 43%

profile of v4, /device:TPU:0, one launch (start us, length us, event | category | flops | bytes accessed | tf_op | source)
XLA Modules:
  0.0 260.4 jit_solution(703442175200353795)
XLA Ops:
  0.7 1.9 pad_select_fusion.2
  2.6 2.9 %collective-permute-start = (bf16[128,768]{1,0:T(8,128)(2,1)}, bf16[128,768]{1,0:T(8,128)(2,1)}, u32[]{:S(2)}, u32[]{:S(2)}) collective-permute-start(bf16[128,768]{1,0:T(8,128)(2,1)} %get-tuple-element.305), channel_id=1, source_target_pairs={{0,1},{1,0},{2,3},{3,2},{4,5},{5,4},{6,7},{7,6},{8,9},{9,8},{10,11... | collective-permute-start | bytes 589832 | tf_op jit(solution)/shard_map/ppermute | solution.py:576
  5.5 2.5 dynamic-slice_bitcast_fusion
  11.2 6.3 %attend_2.1 = (bf16[1536,768]{1,0:T(8,128)(2,1)}, bf16[1536,768]{1,0:T(8,128)(2,1)}, bf16[1536,768]{1,0:T(8,128)(2,1)}, bf16[1536,768]{1,0:T(8,128)(2,1)}, bf16[...) custom-call(s32[1]{0:T(128)} %bitcast.s0._.seq, s32[1]{0:T(128)S(6)} %copy.93.s1, ...), custom_call_target="tpu_custom_call" | custom-call | flops 40000000000 | bytes 100000000 | tf_op jit(solution)/shard_map/attend_2/pallas_call | solution.py:153
  17.5 2.5 collective-permute-start.1
  20.0 9.9 %attend_0.1 = (bf16[1536,768]{1,0:T(8,128)(2,1)}, bf16[1536,768]{1,0:T(8,128)(2,1)}, bf16[1536,768]{1,0:T(8,128)(2,1)}, bf16[1536,768]{1,0:T(8,128)(2,1)}, bf16[...) custom-call(s32[1]{0:T(128)} %bitcast.s0._.seq, ...), custom_call_target="tpu_custom_call", output_to_operand_aliasing={{0}: (11, {}), {1}: (12, {}), {2}: (13, {}), {3}: (14, {}),... | custom-call | flops 40000000000 | bytes 100000000 | tf_op jit(solution)/shard_map/attend_0/pallas_call | solution.py:153
  30.7 10.1 %attend_1.1 = (bf16[1536,768]{1,0:T(8,128)(2,1)}, bf16[1536,768]{1,0:T(8,128)(2,1)}, bf16[1536,768]{1,0:T(8,128)(2,1)}, bf16[1536,768]{1,0:T(8,128)(2,1)}, bf16[...) custom-call(s32[1]{0:T(128)} %bitcast.s0._.seq, ...), custom_call_target="tpu_custom_call", output_to_operand_aliasing={{0}: (11, {}), {1}: (12, {}), {2}: (13, {}), {3}: (14, {}),... | custom-call | flops 40000000000 | bytes 100000000 | tf_op jit(solution)/shard_map/attend_1/pallas_call | solution.py:153
  40.8 1.1 collective-permute-start.3
  41.9 24.4 %dense_own.1 = (bf16[4,256,768]{2,1,0:T(8,128)(2,1)}, bf16[1280,3072]{1,0:T(8,128)(2,1)}, bf16[1280,3072]{1,0:T(8,128)(2,1)}, bf16[1280,768]{1,0:T(8,128)(2,1)},...) custom-call(s32[1]{0:T(128)} %bitcast.s0._.seq, ...), custom_call_target="tpu_custom_call" | custom-call | flops 40000000000 | bytes 100000000 | tf_op jit(solution)/shard_map/dense_own/pallas_call | solution.py:291
  67.3 43.4 %dense_rest.1 = (bf16[256,768]{1,0:T(8,128)(2,1)}, bf16[384,768]{1,0:T(8,128)(2,1)}, bf16[128,768]{1,0:T(8,128)(2,1)}, bf16[1280,3072]{1,0:T(8,128)(2,1)}, bf16[...) custom-call(s32[1]{0:T(128)} %bitcast.s0._.seq, ...), custom_call_target="tpu_custom_call", output_to_operand_aliasing={{3}: (17, {}), {4}: (18, {}), {5}: (19, {}), {6}: (20, {}),... | custom-call | flops 40000000000 | bytes 100000000 | tf_op jit(solution)/shard_map/dense_rest/pallas_call | solution.py:291
  110.7 13.2 %up_grad.1 = (bf16[16,16,4608]{2,1,0:T(8,128)(2,1)}, bf16[16,16,4608]{2,1,0:T(8,128)(2,1)}) custom-call(s32[1]{0:T(128)} %bitcast.1.me, bf16[1280,768]{1,0:T(8,128)(2,1)} %get-tuple-element.187.nlow, bf16[1280,3072]{1,0:T(8,128)(2,1)} %get-tuple-element.188.left.right, bf16[1280,3072]{1,0:T(8,128)(2,1)} %get-tuple-element.188.left.right), custom_call_target="tpu_custom_call" | custom-call | flops 40000000000 | bytes 100000000 | tf_op jit(solution)/shard_map/up_grad/pallas_call | solution.py:326
  124.0 1.0 collective-permute-start.8
  125.0 14.4 %down_grad.1 = (bf16[16,16,5888]{2,1,0:T(8,128)(2,1)}, bf16[16,16,5888]{2,1,0:T(8,128)(2,1)}) custom-call(s32[1]{0:T(128)} %bitcast.1.me, bf16[1280,3072]{1,0:T(8,128)(2,1)} %get-tuple-element.191.act, bf16[1280,768]{1,0:T(8,128)(2,1)} %get-tuple-element.192.dbr, bf16[1536,768]{1,0:T(8,128)(2,1)} %get-tuple-element.175.refs_0_.ctx, ...), custom_call_target="tpu_custom_call" | custom-call | flops 40000000000 | bytes 100000000 | tf_op jit(solution)/shard_map/down_grad/pallas_call | solution.py:374
  139.6 1.1 collective-permute-start.9
  140.7 1.7 copy-done.15
  142.4 2.9 %add_parts.7 = (bf16[2,1,2,2,16,2304]{5,4,3,2,1,0:T(8,128)(2,1)S(1)}, bf16[2,1,2,2,16,2304]{5,4,3,2,1,0:T(8,128)(2,1)}, bf16[2,2,1,2,16,2304]{5,4,3,2,1,0:T(8,128)(2,1)S(1)}, bf16[2,2,1,2,16,2304]{5,4,3,2,1,0:T(8,128)(2,1)}) custom-call(bf16[2,2,2,2,16,4608]{5,4,3,2,1,0:T(8,128)(2,1)S(1)} %bitcast.74, ...), custom_call_target="tpu_custom_call" | custom-call | flops 40000000000 | bytes 100000000 | tf_op jit(solution)/shard_map/add_parts/pallas_call | solution.py:662
  146.9 1.5 collective-permute-start.6
  148.4 1.6 collective-permute-start.5
  150.0 15.9 %back_first.1 = (bf16[512,768]{1,0:T(8,128)(2,1)}, bf16[512,768]{1,0:T(8,128)(2,1)}, bf16[512,768]{1,0:T(8,128)(2,1)}, bf16[4,256,768]{2,1,0:T(8,128)(2,1)}, bf16[256,768]{1,0:T(8,128)(2,1)}) custom-call(s32[1]{0:T(128)} %bitcast.s0._.seq, s32[1]{0:T(128)S(6)} %copy.93.s1, s32[1]{0:T(128)S(6)} %copy.94.s2, s32[4]{0:T(128)} %s3.11, ...), custom_call_target="tpu_custom_call" | custom-call | flops 40000000000 | bytes 100000000 | tf_op jit(solution)/shard_map/back_first/pallas_call | solution.py:437
  165.9 1.8 copy-done.14
  167.8 1.1 copy-done.32
  168.8 1.1 copy-done.37
  169.9 2.1 add_parts.8
  174.0 1.1 collective-permute-start.11
  175.2 14.4 %back_group_0.1 = (bf16[1024,512]{1,0:T(8,128)(2,1)S(1)}, bf16[1024,512]{1,0:T(8,128)(2,1)S(1)}, bf16[1024,512]{1,0:T(8,128)(2,1)S(1)}, bf16[16,16,2304]{2,1,0:T...) custom-call(s32[1]{0:T(128)} %bitcast.1.me, s32[1]{0:T(128)} %bitcast.s0._.seq, s32[1]{0:T(128)S(6)} %copy.93.s1, ...), custom_call_target="tpu_custom_call" | custom-call | flops 40000000000 | bytes 100000000 | tf_op jit(solution)/shard_map/back_group_0/pallas_call | solution.py:509
  190.7 1.4 add_parts.9
  192.0 1.6 collective-permute-start.19
  193.7 1.5 collective-permute-start.18
  196.2 1.1 copy-done.26
  197.3 9.7 %back_group_4.1 = (bf16[1024,256]{1,0:T(8,128)(2,1)S(1)}, bf16[1024,256]{1,0:T(8,128)(2,1)S(1)}, bf16[1024,256]{1,0:T(8,128)(2,1)S(1)}, bf16[16,16,1280]{2,1,0:T...) custom-call(s32[1]{0:T(128)} %bitcast.1.me, s32[1]{0:T(128)} %bitcast.s0._.seq, s32[1]{0:T(128)S(6)} %copy.93.s1, ...), custom_call_target="tpu_custom_call" | custom-call | flops 40000000000 | bytes 100000000 | tf_op jit(solution)/shard_map/back_group_4/pallas_call | solution.py:509
  207.6 1.1 copy-done.20
  208.8 1.1 copy-done.23
  209.9 1.1 copy-done.34
  211.0 1.1 copy-done.39
  212.0 1.2 add_parts.10
  213.3 1.2 collective-permute-start.21
  215.2 2.6 collective-permute-start.24
  218.8 4.0 %input_grad.1 = (bf16[4,256,768]{2,1,0:T(8,128)(2,1)}, bf16[128,768]{1,0:T(8,128)(2,1)S(1)}, bf16[384,768]{1,0:T(8,128)(2,1)}) custom-call(s32[1]{0:T(128)} %bitcast.s0._.seq, f32[1536,768]{1,0:T(8,128)S(1)} %bitcast.100, bf16[1024,512]{1,0:T(8,128)(2,1)S(1)} %get-tuple-element.260.rest_0_, ...), custom_call_target="tpu_custom_call", output_to_operand_aliasing={{0}: (11, {})} | custom-call | flops 40000000000 | bytes 100000000 | tf_op jit(solution)/shard_map/input_grad/pallas_call | solution.py:553
  224.1 2.6 collective-permute-start.29
  226.9 5.9 %collective-permute-done.24.refs_4_.refs_9_.refs_14_.refs_19_.refs_24_.refs_29_.refs_34_.refs_39_.refs_44_.refs_12_.refs_20_ = bf16[2,1,1,2,16,3584]{5,4,3,2,1,0:T(8,128)(2,1)S(1)} collective-permute-done((bf16[2,1,1,2,16,3584]{5,4,3,2,1,0:T(8,128)(2,1)S(1)}, bf16[2,1,1,2,16,3584]{5,4,3,2,1,0:T(8,128)(2,1)S(1)}, u32[]{:S(2)}, u32[]{:S(2)}) %collective-permute-start.24) | collective-permute-done | bytes 458784 | tf_op jit(solution)/shard_map/ppermute | solution.py:588
  232.8 3.7 %collective-permute-start.30 = (bf16[1,1,1,1,16,5888]{5,4,3,2,1,0:T(8,128)(2,1)S(1)}, bf16[1,1,1,1,16,5888]{5,4,3,2,1,0:T(8,128)(2,1)S(1)}, u32[]{:S(2)}, u32[]{:S(2)}) collective-permute-start(bf16[1,1,1,1,16,5888]{5,4,3,2,1,0:T(8,128)(2,1)S(1)} %add_parts.12), channel_id=1, source_target_pairs={{0,16},{1,17},{2,18},{3,19},{4,20},{5,21},{6,22},{7,23},{8,24},{9,... | collective-permute-start | bytes 565256 | tf_op jit(solution)/shard_map/ppermute | solution.py:588
  236.5 9.0 %collective-permute-done.23.refs_3_.refs_8_.refs_13_.refs_18_.refs_23_.refs_28_.refs_33_.refs_38_.refs_43_.refs_11_.refs_19_ = bf16[2,1,1,2,16,3584]{5,4,3,2,1,0:T(8,128)(2,1)S(1)} collective-permute-done((bf16[2,1,1,2,16,3584]{5,4,3,2,1,0:T(8,128)(2,1)S(1)}, bf16[2,1,1,2,16,3584]{5,4,3,2,1,0:T(8,128)(2,1)S(1)}, u32[]{:S(2)}, u32[]{:S(2)}) %collective-permute-start.23) | collective-permute-done | bytes 458784 | tf_op jit(solution)/shard_map/ppermute | solution.py:588
  246.8 1.3 collective-permute-start.28
  248.2 2.2 add_halves.2
  250.4 2.2 collective-permute-start.27
  252.7 1.9 last_sums.3
  255.6 2.1 add_halves.3
  257.7 1.1 collective-permute-done.27.refs_6_.refs_14_.refs_22_
  (151 shorter events, 16.8 us)
Async XLA Ops:
  0.7 7.4 %copy-start.46 = (bf16[1,64,768]{2,1,0:T(8,128)(2,1)S(1)}, bf16[1,64,768]{2,1,0:T(8,128)(2,1)}, u32[]{:S(2)}) copy-start(bf16[1,64,768]{2,1,0:T(8,128)(2,1)} %param.45) | copy-start | bytes 294916
  0.7 7.4 %copy-start.45 = (bf16[1,128,768]{2,1,0:T(8,128)(2,1)S(1)}, bf16[1,128,768]{2,1,0:T(8,128)(2,1)}, u32[]{:S(2)}) copy-start(bf16[1,128,768]{2,1,0:T(8,128)(2,1)} %param.46) | copy-start | bytes 589828
  0.7 8.2 %copy-start.43 = (bf16[4,256,768]{2,1,0:T(8,128)(2,1)S(1)}, bf16[4,256,768]{2,1,0:T(8,128)(2,1)}, u32[]{:S(2)}) copy-start(bf16[4,256,768]{2,1,0:T(8,128)(2,1)} %refs_2_.1) | copy-start | bytes 4718596
  2.6 8.6 %collective-permute-start = (bf16[128,768]{1,0:T(8,128)(2,1)}, bf16[128,768]{1,0:T(8,128)(2,1)}, u32[]{:S(2)}, u32[]{:S(2)}) collective-permute-start(bf16[128,768]{1,0:T(8,128)(2,1)} %get-tuple-element.305), channel_id=1, source_target_pairs={{0,1},{1,0},{2,3},{3,2},{4,5},{5,4},{6,7},{7,6},{8,9},{9,8},{10,11... | collective-permute-start | bytes 589832 | tf_op jit(solution)/shard_map/ppermute | solution.py:576
  8.1 12.0 %collective-permute-start.2 = (bf16[256,768]{1,0:T(8,128)(2,1)}, bf16[256,768]{1,0:T(8,128)(2,1)}, u32[]{:S(2)}, u32[]{:S(2)}) collective-permute-start(bf16[256,768]{1,0:T(8,128)(2,1)} %get-tuple-element.299), channel_id=1, source_target_pairs={{0,1},{1,0},{2,3},{3,2},{4,5},{5,4},{6,7},{7,6},{8,9},{9,8},{10,11... | collective-permute-start | bytes 1179656 | tf_op jit(solution)/shard_map/ppermute | solution.py:576
  11.2 6.3 %copy-start.44 = (bf16[256,768]{1,0:T(8,128)(2,1)S(1)}, bf16[256,768]{1,0:T(8,128)(2,1)}, u32[]{:S(2)}) copy-start(bf16[256,768]{1,0:T(8,128)(2,1)} %get-tuple-element.161) | copy-start | bytes 1179652
  17.5 12.4 %collective-permute-start.1 = (bf16[256,768]{1,0:T(8,128)(2,1)S(1)}, bf16[256,768]{1,0:T(8,128)(2,1)S(1)}, u32[]{:S(2)}, u32[]{:S(2)}) collective-permute-start(bf16[256,768]{1,0:T(8,128)(2,1)S(1)} %copy-done.44), channel_id=1, source_target_pairs={{0,1},{1,0},{2,3},{3,2},{4,5},{5,4},{6,7},{7,6},{8,9},{9,8},{10,11... | collective-permute-start | bytes 1179656 | tf_op jit(solution)/shard_map/ppermute | solution.py:576
  40.8 25.5 %collective-permute-start.3 = (bf16[640,768]{1,0:T(8,128)(2,1)S(1)}, bf16[640,768]{1,0:T(8,128)(2,1)S(1)}, u32[]{:S(2)}, u32[]{:S(2)}) collective-permute-start(bf16[640,768]{1,0:T(8,128)(2,1)S(1)} %pad_maximum_fusion), channel_id=1, source_target_pairs={{0,1},{1,0},{2,3},{3,2},{4,5},{5,4},{6,7},{7,6},{8,9},{9,8},{10,11... | collective-permute-start | bytes 2949128 | tf_op jit(solution)/shard_map/ppermute | solution.py:576
  110.7 13.3 %copy-start.49 = (bf16[256,768]{1,0:T(8,128)(2,1)S(1)}, bf16[256,768]{1,0:T(8,128)(2,1)}, u32[]{:S(2)}) copy-start(bf16[256,768]{1,0:T(8,128)(2,1)} %get-tuple-element.218) | copy-start | bytes 1179652
  124.0 16.7 %collective-permute-start.4 = (bf16[16,16,4608]{2,1,0:T(8,128)(2,1)}, bf16[16,16,4608]{2,1,0:T(8,128)(2,1)}, u32[]{:S(2)}, u32[]{:S(2)}) collective-permute-start(bf16[16,16,4608]{2,1,0:T(8,128)(2,1)} %get-tuple-element.189), channel_id=1, source_target_pairs={{0,2},{1,3},{2,0},{3,1},{4,6},{5,7},{6,4},{7,5},{8,10},{9,11},{10,... | collective-permute-start | bytes 7077896 | tf_op jit(solution)/shard_map/ppermute | solution.py:588
  124.0 15.6 %collective-permute-start.8 = (bf16[256,768]{1,0:T(8,128)(2,1)S(1)}, bf16[256,768]{1,0:T(8,128)(2,1)S(1)}, u32[]{:S(2)}, u32[]{:S(2)}) collective-permute-start(bf16[256,768]{1,0:T(8,128)(2,1)S(1)} %copy-done.49), channel_id=1, source_target_pairs={{0,1},{1,0},{2,3},{3,2},{4,5},{5,4},{6,7},{7,6},{8,9},{9,8},{10,11... | collective-permute-start | bytes 1179656 | tf_op jit(solution)/shard_map/ppermute | solution.py:576
  139.3 26.6 %collective-permute-start.7 = (bf16[16,16,5888]{2,1,0:T(8,128)(2,1)}, bf16[16,16,5888]{2,1,0:T(8,128)(2,1)S(1)}, u32[]{:S(2)}, u32[]{:S(2)}) collective-permute-start(bf16[16,16,5888]{2,1,0:T(8,128)(2,1)} %get-tuple-element.195), channel_id=1, source_target_pairs={{0,2},{1,3},{2,0},{3,1},{4,6},{5,7},{6,4},{7,5},{8,10},{9,11},{10,... | collective-permute-start | bytes 9043976 | tf_op jit(solution)/shard_map/ppermute | solution.py:588
  139.6 26.3 %collective-permute-start.9 = (bf16[384,768]{1,0:T(8,128)(2,1)}, bf16[384,768]{1,0:T(8,128)(2,1)}, u32[]{:S(2)}, u32[]{:S(2)}) collective-permute-start(bf16[384,768]{1,0:T(8,128)(2,1)} %get-tuple-element.221), channel_id=1, source_target_pairs={{0,1},{1,0},{2,3},{3,2},{4,5},{5,4},{6,7},{7,6},{8,9},{9,8},{10,11... | collective-permute-start | bytes 1769480 | tf_op jit(solution)/shard_map/ppermute | solution.py:576
  146.9 19.0 %collective-permute-start.6 = (bf16[2,2,1,2,16,2304]{5,4,3,2,1,0:T(8,128)(2,1)}, bf16[2,2,1,2,16,2304]{5,4,3,2,1,0:T(8,128)(2,1)S(1)}, u32[]{:S(2)}, u32[]{:S(2)}) collective-permute-start(bf16[2,2,1,2,16,2304]{5,4,3,2,1,0:T(8,128)(2,1)} %get-tuple-element.199), channel_id=1, source_target_pairs={{0,4},{1,5},{2,6},{3,7},{4,0},{5,1},{6,2},{7,3},{8,12},{9,13},{10,... | collective-permute-start | bytes 1769480 | tf_op jit(solution)/shard_map/ppermute | solution.py:588
  148.4 17.5 %collective-permute-start.5 = (bf16[2,1,2,2,16,2304]{5,4,3,2,1,0:T(8,128)(2,1)}, bf16[2,1,2,2,16,2304]{5,4,3,2,1,0:T(8,128)(2,1)}, u32[]{:S(2)}, u32[]{:S(2)}) collective-permute-start(bf16[2,1,2,2,16,2304]{5,4,3,2,1,0:T(8,128)(2,1)} %get-tuple-element.198), channel_id=1, source_target_pairs={{0,8},{1,9},{2,10},{3,11},{4,12},{5,13},{6,14},{7,15},{8,0},{9,1},... | collective-permute-start | bytes 1769480 | tf_op jit(solution)/shard_map/ppermute | solution.py:588
  172.1 18.6 %copy-start.19 = (bf16[2,1,2,2,16,2944]{5,4,3,2,1,0:T(8,128)(2,1)}, bf16[2,1,2,2,16,2944]{5,4,3,2,1,0:T(8,128)(2,1)S(1)}, u32[]{:S(2)}) copy-start(bf16[2,1,2,2,16,2944]{5,4,3,2,1,0:T(8,128)(2,1)S(1)} %get-tuple-element.233.refs_6_.refs_8_.refs_0_.refs_10_) | copy-start | bytes 2260996
  172.1 18.5 %copy-start.22 = (bf16[2,2,1,2,16,2944]{5,4,3,2,1,0:T(8,128)(2,1)}, bf16[2,2,1,2,16,2944]{5,4,3,2,1,0:T(8,128)(2,1)S(1)}, u32[]{:S(2)}) copy-start(bf16[2,2,1,2,16,2944]{5,4,3,2,1,0:T(8,128)(2,1)S(1)} %get-tuple-element.235.refs_8_.refs_11_.refs_4_.refs_15_) | copy-start | bytes 2260996
  172.1 18.5 %collective-permute-start.14 = (bf16[2,2,1,2,16,2944]{5,4,3,2,1,0:T(8,128)(2,1)S(1)}, bf16[2,2,1,2,16,2944]{5,4,3,2,1,0:T(8,128)(2,1)S(1)}, u32[]{:S(2)}, u32[]{:S(2)}) collective-permute-start(bf16[2,2,1,2,16,2944]{5,4,3,2,1,0:T(8,128)(2,1)S(1)} %get-tuple-element.216), channel_id=1, source_target_pairs={{0,4},{1,5},{2,6},{3,7},{4,0},{5,1},{6,2},{7,3},{8,12},{9,13},{10,... | collective-permute-start | bytes 2261000 | tf_op jit(solution)/shard_map/ppermute | solution.py:588
  172.6 18.0 %collective-permute-start.13 = (bf16[2,1,2,2,16,2944]{5,4,3,2,1,0:T(8,128)(2,1)S(1)}, bf16[2,1,2,2,16,2944]{5,4,3,2,1,0:T(8,128)(2,1)S(1)}, u32[]{:S(2)}, u32[]{:S(2)}) collective-permute-start(bf16[2,1,2,2,16,2944]{5,4,3,2,1,0:T(8,128)(2,1)S(1)} %get-tuple-element.215), channel_id=1, source_target_pairs={{0,8},{1,9},{2,10},{3,11},{4,12},{5,13},{6,14},{7,15},{8,0},{9,1},... | collective-permute-start | bytes 2261000 | tf_op jit(solution)/shard_map/ppermute | solution.py:588
  173.1 17.5 %collective-permute-start.12 = (bf16[2,2,1,1,16,2304]{5,4,3,2,1,0:T(8,128)(2,1)S(1)}, bf16[2,2,1,1,16,2304]{5,4,3,2,1,0:T(8,128)(2,1)S(1)}, u32[]{:S(2)}, u32[]{:S(2)}) collective-permute-start(bf16[2,2,1,1,16,2304]{5,4,3,2,1,0:T(8,128)(2,1)S(1)} %get-tuple-element.214), channel_id=1, source_target_pairs={{0,1},{1,0},{2,3},{3,2},{4,5},{5,4},{6,7},{7,6},{8,9},{9,8},{10,11... | collective-permute-start | bytes 884744 | tf_op jit(solution)/shard_map/ppermute | solution.py:588
  174.0 16.5 %collective-permute-start.11 = (bf16[2,1,2,1,16,2304]{5,4,3,2,1,0:T(8,128)(2,1)S(1)}, bf16[2,1,2,1,16,2304]{5,4,3,2,1,0:T(8,128)(2,1)S(1)}, u32[]{:S(2)}, u32[]{:S(2)}) collective-permute-start(bf16[2,1,2,1,16,2304]{5,4,3,2,1,0:T(8,128)(2,1)S(1)} %get-tuple-element.213), channel_id=1, source_target_pairs={{0,1},{1,0},{2,3},{3,2},{4,5},{5,4},{6,7},{7,6},{8,9},{9,8},{10,11... | collective-permute-start | bytes 884744 | tf_op jit(solution)/shard_map/ppermute | solution.py:588
  175.1 14.4 %copy-start.48 = (bf16[256,768]{1,0:T(8,128)(2,1)S(1)}, bf16[256,768]{1,0:T(8,128)(2,1)}, u32[]{:S(2)}) copy-start(bf16[256,768]{1,0:T(8,128)(2,1)} %get-tuple-element.257) | copy-start | bytes 1179652
  175.1 15.5 %copy-start.33 = (bf16[2,1,2,2,16,2304]{5,4,3,2,1,0:T(8,128)(2,1)S(1)}, bf16[2,1,2,2,16,2304]{5,4,3,2,1,0:T(8,128)(2,1)}, u32[]{:S(2)}) copy-start(bf16[2,1,2,2,16,2304]{5,4,3,2,1,0:T(8,128)(2,1)} %copy-done.31) | copy-start | bytes 1769476
  175.2 15.5 %copy-start.38 = (bf16[2,2,1,2,16,2304]{5,4,3,2,1,0:T(8,128)(2,1)S(1)}, bf16[2,2,1,2,16,2304]{5,4,3,2,1,0:T(8,128)(2,1)}, u32[]{:S(2)}) copy-start(bf16[2,2,1,2,16,2304]{5,4,3,2,1,0:T(8,128)(2,1)} %copy-done.36) | copy-start | bytes 1769476
  189.6 17.4 %collective-permute-start.22 = (bf16[256,768]{1,0:T(8,128)(2,1)S(1)}, bf16[256,768]{1,0:T(8,128)(2,1)S(1)}, u32[]{:S(2)}, u32[]{:S(2)}) collective-permute-start(bf16[256,768]{1,0:T(8,128)(2,1)S(1)} %copy-done.48), channel_id=1, source_target_pairs={{0,1},{1,0},{2,3},{3,2},{4,5},{5,4},{6,7},{7,6},{8,9},{9,8},{10,11... | collective-permute-start | bytes 1179656 | tf_op jit(solution)/shard_map/ppermute | solution.py:576
  190.5 17.1 %copy-start.7 = (bf16[2,2,1,1,16,2304]{5,4,3,2,1,0:T(8,128)(2,1)}, bf16[2,2,1,1,16,2304]{5,4,3,2,1,0:T(8,128)(2,1)S(1)}, u32[]{:S(2)}) copy-start(bf16[2,2,1,1,16,2304]{5,4,3,2,1,0:T(8,128)(2,1)S(1)} %collective-permute-done.12.refs_5_.refs_6_.refs_7_) | copy-start | bytes 884740
  190.5 17.1 %copy-start.9 = (bf16[2,1,2,1,16,2304]{5,4,3,2,1,0:T(8,128)(2,1)}, bf16[2,1,2,1,16,2304]{5,4,3,2,1,0:T(8,128)(2,1)S(1)}, u32[]{:S(2)}) copy-start(bf16[2,1,2,1,16,2304]{5,4,3,2,1,0:T(8,128)(2,1)S(1)} %collective-permute-done.11.refs_2_) | copy-start | bytes 884740
  192.0 15.5 %collective-permute-start.19 = (bf16[2,1,1,2,16,2944]{5,4,3,2,1,0:T(8,128)(2,1)S(1)}, bf16[2,1,1,2,16,2944]{5,4,3,2,1,0:T(8,128)(2,1)S(1)}, u32[]{:S(2)}, u32[]{:S(2)}) collective-permute-start(bf16[2,1,1,2,16,2944]{5,4,3,2,1,0:T(8,128)(2,1)S(1)} %get-tuple-element.240), channel_id=1, source_target_pairs={{0,8},{1,9},{2,10},{3,11},{4,12},{5,13},{6,14},{7,15},{8,0},{9,1},... | collective-permute-start | bytes 1130504 | tf_op jit(solution)/shard_map/ppermute | solution.py:588
  193.7 13.9 %collective-permute-start.18 = (bf16[2,1,1,2,16,2944]{5,4,3,2,1,0:T(8,128)(2,1)S(1)}, bf16[2,1,1,2,16,2944]{5,4,3,2,1,0:T(8,128)(2,1)S(1)}, u32[]{:S(2)}, u32[]{:S(2)}) collective-permute-start(bf16[2,1,1,2,16,2944]{5,4,3,2,1,0:T(8,128)(2,1)S(1)} %get-tuple-element.239), channel_id=1, source_target_pairs={{0,4},{1,5},{2,6},{3,7},{4,0},{5,1},{6,2},{7,3},{8,12},{9,13},{10,... | collective-permute-start | bytes 1130504 | tf_op jit(solution)/shard_map/ppermute | solution.py:588
  195.2 11.9 %collective-permute-start.17 = (bf16[2,1,1,1,16,2304]{5,4,3,2,1,0:T(8,128)(2,1)S(1)}, bf16[2,1,1,1,16,2304]{5,4,3,2,1,0:T(8,128)(2,1)S(1)}, u32[]{:S(2)}, u32[]{:S(2)}) collective-permute-start(bf16[2,1,1,1,16,2304]{5,4,3,2,1,0:T(8,128)(2,1)S(1)} %get-tuple-element.238), channel_id=1, source_target_pairs={{0,8},{1,9},{2,10},{3,11},{4,12},{5,13},{6,14},{7,15},{8,0},{9,1},... | collective-permute-start | bytes 442376 | tf_op jit(solution)/shard_map/ppermute | solution.py:588
  195.6 11.9 %collective-permute-start.16 = (bf16[2,1,1,1,16,2304]{5,4,3,2,1,0:T(8,128)(2,1)S(1)}, bf16[2,1,1,1,16,2304]{5,4,3,2,1,0:T(8,128)(2,1)S(1)}, u32[]{:S(2)}, u32[]{:S(2)}) collective-permute-start(bf16[2,1,1,1,16,2304]{5,4,3,2,1,0:T(8,128)(2,1)S(1)} %get-tuple-element.237), channel_id=1, source_target_pairs={{0,4},{1,5},{2,6},{3,7},{4,0},{5,1},{6,2},{7,3},{8,12},{9,13},{10,... | collective-permute-start | bytes 442376 | tf_op jit(solution)/shard_map/ppermute | solution.py:588
  207.0 7.5 %collective-permute-start.10 = (bf16[16,16,2304]{2,1,0:T(8,128)(2,1)S(1)}, bf16[16,16,2304]{2,1,0:T(8,128)(2,1)S(1)}, u32[]{:S(2)}, u32[]{:S(2)}) collective-permute-start(bf16[16,16,2304]{2,1,0:T(8,128)(2,1)S(1)} %get-tuple-element.229), channel_id=1, source_target_pairs={{0,2},{1,3},{2,0},{3,1},{4,6},{5,7},{6,4},{7,5},{8,10},{9,11},{10,... | collective-permute-start | bytes 3538952 | tf_op jit(solution)/shard_map/ppermute | solution.py:588
  207.1 7.4 %collective-permute-start.15 = (bf16[16,16,1280]{2,1,0:T(8,128)(2,1)S(1)}, bf16[16,16,1280]{2,1,0:T(8,128)(2,1)S(1)}, u32[]{:S(2)}, u32[]{:S(2)}) collective-permute-start(bf16[16,16,1280]{2,1,0:T(8,128)(2,1)S(1)} %get-tuple-element.245), channel_id=1, source_target_pairs={{0,2},{1,3},{2,0},{3,1},{4,6},{5,7},{6,4},{7,5},{8,10},{9,11},{10,... | collective-permute-start | bytes 1966088 | tf_op jit(solution)/shard_map/ppermute | solution.py:588
  212.0 6.7 %slice-start = ((s8[4718592]{0:T(1024)(128)(4,1)}), s8[4194304]{0:T(1024)(128)(4,1)S(1)}, s32[]{:S(2)}) async-start(s8[4718592]{0:T(1024)(128)(4,1)} %bitcast.99), calls=%async_computation | async-start | bytes 8388608
  213.3 10.8 %collective-permute-start.21 = (bf16[2,1,1,1,16,5888]{5,4,3,2,1,0:T(8,128)(2,1)S(1)}, bf16[2,1,1,1,16,5888]{5,4,3,2,1,0:T(8,128)(2,1)S(1)}, u32[]{:S(2)}, u32[]{:S(2)}) collective-permute-start(bf16[2,1,1,1,16,5888]{5,4,3,2,1,0:T(8,128)(2,1)S(1)} %get-tuple-element.253), channel_id=1, source_target_pairs={{0,1},{1,0},{2,3},{3,2},{4,5},{5,4},{6,7},{7,6},{8,9},{9,8},{10,11... | collective-permute-start | bytes 1130504 | tf_op jit(solution)/shard_map/ppermute | solution.py:588
  215.2 17.6 %collective-permute-start.24 = (bf16[2,1,1,2,16,3584]{5,4,3,2,1,0:T(8,128)(2,1)S(1)}, bf16[2,1,1,2,16,3584]{5,4,3,2,1,0:T(8,128)(2,1)S(1)}, u32[]{:S(2)}, u32[]{:S(2)}) collective-permute-start(bf16[2,1,1,2,16,3584]{5,4,3,2,1,0:T(8,128)(2,1)S(1)} %get-tuple-element.255), channel_id=1, source_target_pairs={{0,12},{1,13},{2,14},{3,15},{4,8},{5,9},{6,10},{7,11},{8,4},{9,5},... | collective-permute-start | bytes 1376264 | tf_op jit(solution)/shard_map/ppermute | solution.py:588
  217.8 27.7 %collective-permute-start.23 = (bf16[2,1,1,2,16,3584]{5,4,3,2,1,0:T(8,128)(2,1)S(1)}, bf16[2,1,1,2,16,3584]{5,4,3,2,1,0:T(8,128)(2,1)S(1)}, u32[]{:S(2)}, u32[]{:S(2)}) collective-permute-start(bf16[2,1,1,2,16,3584]{5,4,3,2,1,0:T(8,128)(2,1)S(1)} %get-tuple-element.254), channel_id=1, source_target_pairs={{0,8},{1,9},{2,10},{3,11},{4,12},{5,13},{6,14},{7,15},{8,0},{9,1},... | collective-permute-start | bytes 1376264 | tf_op jit(solution)/shard_map/ppermute | solution.py:588
  218.2 27.3 %collective-permute-start.20 = (bf16[2,1,1,2,16,3584]{5,4,3,2,1,0:T(8,128)(2,1)S(1)}, bf16[2,1,1,2,16,3584]{5,4,3,2,1,0:T(8,128)(2,1)S(1)}, u32[]{:S(2)}, u32[]{:S(2)}) collective-permute-start(bf16[2,1,1,2,16,3584]{5,4,3,2,1,0:T(8,128)(2,1)S(1)} %get-tuple-element.252), channel_id=1, source_target_pairs={{0,4},{1,5},{2,6},{3,7},{4,0},{5,1},{6,2},{7,3},{8,12},{9,13},{10,... | collective-permute-start | bytes 1376264 | tf_op jit(solution)/shard_map/ppermute | solution.py:588
  218.8 7.9 %copy-start.21 = (bf16[2,1,2,2,16,2944]{5,4,3,2,1,0:T(8,128)(2,1)S(1)}, bf16[2,1,2,2,16,2944]{5,4,3,2,1,0:T(8,128)(2,1)}, u32[]{:S(2)}) copy-start(bf16[2,1,2,2,16,2944]{5,4,3,2,1,0:T(8,128)(2,1)} %copy-done.19) | copy-start | bytes 2260996
  218.8 7.9 %copy-start.24 = (bf16[2,2,1,2,16,2944]{5,4,3,2,1,0:T(8,128)(2,1)S(1)}, bf16[2,2,1,2,16,2944]{5,4,3,2,1,0:T(8,128)(2,1)}, u32[]{:S(2)}) copy-start(bf16[2,2,1,2,16,2944]{5,4,3,2,1,0:T(8,128)(2,1)} %copy-done.22) | copy-start | bytes 2260996
  222.8 32.8 %collective-permute-start.25 = (bf16[384,768]{1,0:T(8,128)(2,1)}, bf16[384,768]{1,0:T(8,128)(2,1)}, u32[]{:S(2)}, u32[]{:S(2)}) collective-permute-start(bf16[384,768]{1,0:T(8,128)(2,1)} %get-tuple-element.267), channel_id=1, source_target_pairs={{0,1},{1,0},{2,3},{3,2},{4,5},{5,4},{6,7},{7,6},{8,9},{9,8},{10,11... | collective-permute-start | bytes 1769480 | tf_op jit(solution)/shard_map/ppermute | solution.py:576
  224.1 26.3 %collective-permute-start.29 = (bf16[1,1,1,1,16,4608]{5,4,3,2,1,0:T(8,128)(2,1)S(1)}, bf16[1,1,1,1,16,4608]{5,4,3,2,1,0:T(8,128)(2,1)S(1)}, u32[]{:S(2)}, u32[]{:S(2)}) collective-permute-start(bf16[1,1,1,1,16,4608]{5,4,3,2,1,0:T(8,128)(2,1)S(1)} %get-tuple-element.293), channel_id=1, source_target_pairs={{0,16},{1,17},{2,18},{3,19},{4,20},{5,21},{6,22},{7,23},{8,24},{9,... | collective-permute-start | bytes 442376 | tf_op jit(solution)/shard_map/ppermute | solution.py:588
  226.8 21.3 %copy-start.4 = (bf16[256,768]{1,0:T(8,128)(2,1)S(1)}, bf16[256,768]{1,0:T(8,128)(2,1)}, u32[]{:S(2)}) copy-start(bf16[256,768]{1,0:T(8,128)(2,1)} %copy-done.3) | copy-start | bytes 1179652
  226.8 21.3 %copy-start.41 = (bf16[128,768]{1,0:T(8,128)(2,1)S(1)}, bf16[128,768]{1,0:T(8,128)(2,1)}, u32[]{:S(2)}) copy-start(bf16[128,768]{1,0:T(8,128)(2,1)} %get-tuple-element.274.here) | copy-start | bytes 589828
  232.8 19.9 %collective-permute-start.30 = (bf16[1,1,1,1,16,5888]{5,4,3,2,1,0:T(8,128)(2,1)S(1)}, bf16[1,1,1,1,16,5888]{5,4,3,2,1,0:T(8,128)(2,1)S(1)}, u32[]{:S(2)}, u32[]{:S(2)}) collective-permute-start(bf16[1,1,1,1,16,5888]{5,4,3,2,1,0:T(8,128)(2,1)S(1)} %add_parts.12), channel_id=1, source_target_pairs={{0,16},{1,17},{2,18},{3,19},{4,20},{5,21},{6,22},{7,23},{8,24},{9,... | collective-permute-start | bytes 565256 | tf_op jit(solution)/shard_map/ppermute | solution.py:588
  245.8 13.0 %collective-permute-start.26 = (bf16[1,1,1,1,16,3584]{5,4,3,2,1,0:T(8,128)(2,1)S(1)}, bf16[1,1,1,1,16,3584]{5,4,3,2,1,0:T(8,128)(2,1)S(1)}, u32[]{:S(2)}, u32[]{:S(2)}) collective-permute-start(bf16[1,1,1,1,16,3584]{5,4,3,2,1,0:T(8,128)(2,1)S(1)} %get-tuple-element.272), channel_id=1, source_target_pairs={{0,1},{1,0},{2,3},{3,2},{4,5},{5,4},{6,7},{7,6},{8,9},{9,8},{10,11... | collective-permute-start | bytes 344072 | tf_op jit(solution)/shard_map/ppermute | solution.py:588
  246.8 10.9 %collective-permute-start.28 = (bf16[1,1,1,1,16,3584]{5,4,3,2,1,0:T(8,128)(2,1)S(1)}, bf16[1,1,1,1,16,3584]{5,4,3,2,1,0:T(8,128)(2,1)S(1)}, u32[]{:S(2)}, u32[]{:S(2)}) collective-permute-start(bf16[1,1,1,1,16,3584]{5,4,3,2,1,0:T(8,128)(2,1)S(1)} %get-tuple-element.287), channel_id=1, source_target_pairs={{0,17},{1,16},{2,19},{3,18},{4,21},{5,20},{6,23},{7,22},{8,25},{9,... | collective-permute-start | bytes 344072 | tf_op jit(solution)/shard_map/ppermute | solution.py:588
  250.4 8.4 %collective-permute-start.27 = (bf16[1,1,1,1,16,3584]{5,4,3,2,1,0:T(8,128)(2,1)S(1)}, bf16[1,1,1,1,16,3584]{5,4,3,2,1,0:T(8,128)(2,1)S(1)}, u32[]{:S(2)}, u32[]{:S(2)}) collective-permute-start(bf16[1,1,1,1,16,3584]{5,4,3,2,1,0:T(8,128)(2,1)S(1)} %get-tuple-element.285), channel_id=1, source_target_pairs={{0,16},{1,17},{2,18},{3,19},{4,20},{5,21},{6,22},{7,23},{8,24},{9,... | collective-permute-start | bytes 344072 | tf_op jit(solution)/shard_map/ppermute | solution.py:588
  (36 other events, 126.2 us)
